TPU v7x, 32 devices: a whole 2x2x4 slice. The times are simulated.
32 devices in a mesh: parts: 2 (over x), cell: 16 (over z, y, core).
Axes of the slice: x: 2, y: 2, z: 4, core: 2. Of those that a mesh axis runs over, the one named last changes fastest.
Arguments:
- vectors: bfloat16 [49152, 768], P(('parts', 'cell')), parts along dimension 0, may hold values from -12 to 12
- row_slot: int32 [2, 49152], P(None, ('parts', 'cell')), parts along dimension 1, may hold values from 0 to 31, as said below
- fine_codes: int32 [2, 49152], P(None, ('parts', 'cell')), parts along dimension 1, may hold values from 0 to 2047
- cell_list: int32 [2, 1024], P(None, ('parts', 'cell')), parts along dimension 1, may hold values from 0 to 511, as said below
- coarse_in: float32 [8192, 768], P('cell'), may hold values from -6 to 6
- fine_in: float32 [2048, 768], replicated, may hold values from -6 to 6
Outputs:
- coarse_out: float32 [16384, 768], P(('parts', 'cell')), parts along dimension 0
- fine_out: float32 [4096, 768], P(('parts', 'cell')), parts along dimension 0
There are 2 independent parts, one for each index of `parts`. A program takes and returns all parts, laid end to end along the dimension named above; an argument that names none is the same for every part. Nothing has to cross between parts.
Inputs may be any that keep to these rules, and one draw needn't show every extreme that they name: In sweep 0, row_slot is nondecreasing over each device's 1536 vectors. `cell_list`: each run of 2 consecutive entries of a device's list is nondecreasing.
All inputs are finite; a program needn't handle non-finite values.
Results may differ from a plain program's by a relative error of at most 0.0028.
Values sent between devices are 32-bit elements; how exact they have to be, the bound alone decides.
No kernel may reach another device: no remote copies, remote signals or barrier semaphores. Data moves between devices by JAX's collectives and lax.ppermute only.
A program may use at most 128 MiB of HBM per device.

v0:
```python
import jax
import jax.numpy as jnp
from jax import lax
from jax.experimental import pallas as pl
from jax.experimental.pallas import tpu as pltpu
from jax.sharding import PartitionSpec as P


def code_tally(code_rows, codewords):
    return jax.ops.segment_sum(
        jnp.ones(code_rows.shape, jnp.float32), code_rows, num_segments=codewords
    )


def fine_update(code_term, totals_share, old_share, share_rows):
    part_sums = lax.psum_scatter(
        code_term(jnp.int32(0), lax.axis_size("cell") * share_rows),
        "cell",
        scatter_dimension=0,
        tiled=True,
    )
    return jnp.where(
        totals_share[:, None] > 0, part_sums / jnp.maximum(totals_share, 1.0)[:, None], old_share
    )


def routed_plan(vectors, row_slot, fine_codes, cell_list, coarse_in, fine_in):
    groups = lax.axis_size("cell")
    rows_here, feature = vectors.shape
    listed = cell_list.shape[1]
    slot_count = listed // groups
    owner_cells = coarse_in.shape[0]
    codewords = fine_in.shape[0]
    share_rows = codewords // groups
    share_start = lax.axis_index("cell") * share_rows
    fine_book = fine_in
    fine_share = lax.dynamic_slice_in_dim(fine_in, share_start, share_rows, 0)
    coarse = coarse_in
    list_iota = lax.iota(jnp.int32, listed)
    for sweep in range(2):
        code_totals = lax.psum(code_tally(fine_codes[sweep], codewords), "cell")
        slot_rows = row_slot[sweep]
        code_rows = fine_codes[sweep]
        picked = jnp.take(fine_book, code_rows, axis=0)
        residual = (vectors.astype(jnp.float32) - picked).astype(jnp.bfloat16)
        slot_hot = (slot_rows[None, :] == list_iota[:, None]).astype(jnp.bfloat16)
        slot_sums = jnp.dot(slot_hot, residual, preferred_element_type=jnp.float32)
        slot_counts = jnp.sum(slot_hot, axis=1, dtype=jnp.float32)
        slot_cells = cell_list[sweep].astype(jnp.float32)
        got_sums, got_counts, got_cells = (
            lax.all_to_all(
                slot_sums.reshape(groups, slot_count, feature),
                "cell",
                split_axis=0,
                concat_axis=0,
                tiled=True,
            ),
            lax.all_to_all(
                slot_counts.reshape(groups, slot_count),
                "cell",
                split_axis=0,
                concat_axis=0,
                tiled=True,
            ),
            lax.all_to_all(
                slot_cells.reshape(groups, slot_count),
                "cell",
                split_axis=0,
                concat_axis=0,
                tiled=True,
            ),
        )
        flat_cells = got_cells.reshape(groups * slot_count).astype(jnp.int32)
        cell_sums = jax.ops.segment_sum(
            got_sums.reshape(groups * slot_count, feature), flat_cells, num_segments=owner_cells
        )
        cell_counts = jax.ops.segment_sum(
            got_counts.reshape(groups * slot_count), flat_cells, num_segments=owner_cells
        )
        coarse = jnp.where(
            cell_counts[:, None] > 0, cell_sums / jnp.maximum(cell_counts, 1.0)[:, None], coarse
        )
        returned_rows = jnp.take(coarse, flat_cells, axis=0).reshape(groups, slot_count, feature)
        arrived = lax.all_to_all(returned_rows, "cell", split_axis=0, concat_axis=0, tiled=True)
        entry_centers = arrived.reshape(listed, feature)
        row_centers = jnp.take(entry_centers, slot_rows, axis=0)
        fine_residual = (vectors.astype(jnp.float32) - row_centers).astype(jnp.bfloat16)

        def code_term(start, count, code_rows=code_rows, fine_residual=fine_residual):
            wanted = start + lax.iota(jnp.int32, count)
            code_hot = (code_rows[None, :] == wanted[:, None]).astype(jnp.bfloat16)
            return jnp.dot(code_hot, fine_residual, preferred_element_type=jnp.float32)

        totals_share = lax.dynamic_slice_in_dim(code_totals, share_start, share_rows, 0)
        if sweep == 0:
            full_sums = lax.psum(code_term(0, codewords), "cell")
            fine_book = jnp.where(
                code_totals[:, None] > 0,
                full_sums / jnp.maximum(code_totals, 1.0)[:, None],
                fine_book,
            )
            fine_share = lax.dynamic_slice_in_dim(fine_book, share_start, share_rows, 0)
        else:
            fine_share = fine_update(code_term, totals_share, fine_share, share_rows)
    return (coarse, fine_share)


F32 = jnp.float32
BF16 = jnp.bfloat16
LOW = 256
LANES = 128
PARAMS = pltpu.CompilerParams(vmem_limit_bytes=58 * 2**20)
VMEM = pl.BlockSpec(memory_space=pltpu.VMEM)
SMEM = pl.BlockSpec(memory_space=pltpu.SMEM)
ANY = pl.BlockSpec(memory_space=pl.ANY)


def iota(shape, axis):
    return lax.broadcasted_iota(jnp.int32, shape, axis)


def matmul(left, right):
    return jnp.dot(left, right, preferred_element_type=F32)


def matmul_nt(left, right):
    return lax.dot_general(left, right, (((1,), (1,)), ((), ())), preferred_element_type=F32)


def split(values):
    high = values.astype(BF16)
    return high, (values - high.astype(F32)).astype(BF16)


def hot_rows(codes, rows=LOW):
    inside = jnp.where((codes >= 0) & (codes < rows), codes, -1)
    inside = inside.astype(F32).astype(BF16)
    row = iota((rows, codes.shape[1]), 0).astype(F32).astype(BF16)
    return jnp.where(row == inside, jnp.ones((), BF16), jnp.zeros((), BF16))


def pair_block(codes, slots, listed, high):
    left = hot_rows((codes >> 8) * listed + slots, high * listed)
    return matmul_nt(left, hot_rows(codes & (LOW - 1)))


def pack_kernel(fine_codes, row_slot, cell_list, packed):
    half = fine_codes.shape[1] // 2
    listed = cell_list.shape[1]
    packed[:, half:] = jnp.zeros((8, LANES), jnp.int32)
    for number, ref in enumerate((fine_codes, row_slot)):
        for sweep in range(2):
            for part in range(2):
                row = 4 * number + 2 * sweep + part
                packed[row : row + 1, :half] = ref[
                    sweep : sweep + 1, part * half : (part + 1) * half
                ]
    packed[0:2, half : half + listed] = cell_list[...]


def own_cells_kernel(
    groups, listed, me_ref, vectors, fine_codes, row_slot, fine_in, first_ref, second_ref, to_ref
):
    high = fine_in.shape[0] // LOW
    first = matmul(hot_rows(row_slot[0:1, :], listed), vectors[...])
    second_ref[...] = matmul(hot_rows(row_slot[1:2, :], listed), vectors[...])
    pairs = pair_block(fine_codes[0:1, :], row_slot[0:1, :], listed, high)
    for digit in range(high):
        pairs_high, pairs_low = split(pairs[digit * listed : (digit + 1) * listed])
        both = jnp.concatenate([pairs_high, pairs_low], axis=0)
        book = fine_in[digit * LOW : (digit + 1) * LOW, :]
        book_high, book_low = split(book)
        taken = matmul(both, book_high) + matmul(both, book_low)
        first = first - taken[:listed] - taken[listed:]
    first_ref[...] = first
    slots = listed // groups
    top = groups.bit_length() - 1
    for owner in range(groups):
        block = owner ^ me_ref[0]
        at = sum((1 - (block >> bit & 1)) << (top - 1 - bit) for bit in range(top))
        to_ref[at, 0] = first[owner * slots : (owner + 1) * slots]


def own_codes_kernel(base, vectors, fine_codes, _, sums_ref):
    codes = fine_codes[0:1, :] - base
    for start in range(0, sums_ref.shape[0], 2 * LOW):
        hot = jnp.concatenate(
            [hot_rows(codes - start), hot_rows(codes - start - LOW)], axis=0
        )
        sums_ref[start : start + 2 * LOW, :] = matmul(hot, vectors[...])


def position(block, groups):
    return (block & 1) * (groups // 2) + (block >> 1 & 1) * (groups // 4) + (block >> 2)


def sums_kernel(
    groups,
    slot_count,
    owner_cells,
    cuts,
    orders,
    me_ref,
    codes_ref,
    vectors,
    fine_codes,
    low_sums_ref,
    high_sums_ref,
    first_ref,
    second_ref,
    share_ref,
    *refs,
):
    out_refs, refs = refs[: 3 * len(cuts)], refs[3 * len(cuts) :]
    code_info_ref, entry_info_ref, refs = refs[0], refs[1], refs[2:]
    table0, table1, cell0, cell1, wide, terms, permuted, rows_hot = refs[:8]
    fine, bracket, centers_ref, pairs_ref, left = refs[8:13]
    in_sem, out_sem, stages = refs[13], refs[14], refs[15:]
    me = me_ref[0]
    codewords, feature = fine.shape
    listed = groups * slot_count
    entries = groups * listed
    high = codewords // LOW
    half = codes_ref.shape[2] - LANES
    share_rows = share_ref.shape[0]

    loads = [
        pltpu.make_async_copy(
            ref, fine.at[pl.ds(at * (codewords // 2), codewords // 2)], in_sem.at[at]
        )
        for at, ref in enumerate((low_sums_ref, high_sums_ref))
    ]
    for load in loads:
        load.start()

    rows_hot[...] = iota(rows_hot.shape, 0).astype(F32).astype(BF16)
    one, zero = jnp.ones((), BF16), jnp.zeros((), BF16)

    def hot(codes):
        return jnp.where(rows_hot[...] == codes.astype(F32).astype(BF16), one, zero)

    def device_tables(device, carry):
        at = position(device ^ me, groups)
        for sweep, table in enumerate((table0, table1)):
            block = jnp.zeros((high * listed, LOW), F32)
            for part in range(2):
                row = 2 * sweep + part
                codes = codes_ref[at, row : row + 1, :half]
                slots = codes_ref[at, row + 4 : row + 5, :half]
                block = block + matmul_nt(
                    hot((codes >> 8) * listed + slots)[: high * listed], hot(codes & (LOW - 1))
                )
            rows = pl.ds(pl.multiple_of(device * listed, listed), listed)
            for digit in range(high):
                table[rows, digit * LOW : (digit + 1) * LOW] = block[
                    digit * listed : (digit + 1) * listed
                ]
        return carry

    lax.fori_loop(0, groups, device_tables, 0)
    for device in range(groups):
        at = position(device ^ me, groups)
        for sweep, cell in enumerate((cell0, cell1)):
            row = codes_ref[at, sweep : sweep + 1, half : half + listed]
            cell[device * slot_count : (device + 1) * slot_count, :] = jnp.broadcast_to(
                row, (slot_count, listed)
            )

    row_at = iota((entries, listed), 0)
    owner_of = row_at // listed
    slot_of = owner_of * slot_count + row_at % slot_count
    is_slot = slot_of == iota((entries, listed), 1)
    device_of = (row_at // slot_count) % groups

    def entry_cells(cell):
        tiled = jnp.concatenate([cell[...]] * groups, axis=0)
        picked = jnp.sum(jnp.where(is_slot, tiled, 0), axis=1, keepdims=True)
        return picked.astype(F32)

    owner_col = owner_of[:, :1].astype(F32)
    cells = [entry_cells(cell0), entry_cells(cell1)]
    names = [cell + owner_col * float(owner_cells) for cell in cells]

    entry_row = iota((entries, entries), 0)
    natural = (
        ((entry_row // slot_count) % groups) * listed
        + (entry_row // listed) * slot_count
        + entry_row % slot_count
    )
    order = (natural == iota((entries, entries), 1)).astype(BF16)
    code_counts = [jnp.sum(table[...], axis=0, keepdims=True) for table in (table0, table1)]
    entry_counts = []
    for table in (table0, table1):
        count_high, count_low = split(
            jnp.broadcast_to(jnp.sum(table[...], axis=1, keepdims=True), (entries, LANES))
        )
        entry_counts.append(matmul(order, count_high) + matmul(order, count_low))
    most = jnp.maximum(jnp.max(table0[...]), jnp.max(table1[...]))
    large = most > LOW
    for digit in range(high):
        columns = slice(digit * LOW, (digit + 1) * LOW)
        permuted[0, :, columns] = matmul(order, table1[:, columns].astype(BF16)).astype(BF16)

    @pl.when(large)
    def _():
        for digit in range(high):
            columns = slice(digit * LOW, (digit + 1) * LOW)
            rest = split(table1[:, columns])[1]
            permuted[1, :, columns] = matmul(order, rest).astype(BF16)

    own_row = codes_ref[0, 0:1, half : half + listed].astype(F32)
    own_row = own_row + (iota((1, listed), 1) // slot_count).astype(F32) * float(owner_cells)
    match = (names[0] == own_row).astype(BF16)
    match = lax.dot_general(match, order, (((0,), (0,)), ((), ())), preferred_element_type=F32)
    match = match.astype(BF16)
    held = jnp.zeros((listed, 1), F32)
    for digit in range(high):
        columns = slice(digit * LOW, (digit + 1) * LOW)
        table_high, table_low = split(table0[:, columns])
        used = matmul(match, table_high) + matmul(match, table_low)
        held = held + jnp.sum(used, axis=1, keepdims=True)
        used_high, used_low = split(used)
        wide[0:listed, columns] = used_high.astype(F32)
        wide[listed : 2 * listed, columns] = used_low.astype(F32)
    wide[2 * listed : 2 * listed + 8, :] = jnp.broadcast_to(code_counts[0], (8, codewords))
    wide[2 * listed + 8 : 2 * listed + 16, :] = jnp.broadcast_to(code_counts[1], (8, codewords))
    wide[2 * listed + 16 :, :] = jnp.zeros((LANES - 2 * listed - 16, codewords), F32)
    center_high, center_low = split(first_ref[...] / jnp.maximum(held, 1.0))
    blank = jnp.zeros((LANES - 2 * listed, feature), BF16)
    center_high = jnp.concatenate([center_high, center_high, blank], axis=0)
    center_low = jnp.concatenate([center_low, center_low, blank], axis=0)
    for load in loads:
        load.wait()
    for digit in range(high):
        rows = slice(digit * LOW, (digit + 1) * LOW)
        columns = wide[:, rows].T
        code_info_ref[rows, :] = columns
        taken = jnp.where(iota((LOW, LANES), 1) < 2 * listed, columns, 0.0).astype(BF16)
        first_fine = fine[rows, :] - (matmul(taken, center_high) + matmul(taken, center_low))
        scaled = first_fine / jnp.maximum(columns[:, 2 * listed : 2 * listed + 1], 1.0)
        terms[0, rows, :], terms[1, rows, :] = split(scaled)
        fine[rows, :] = jnp.where(
            columns[:, 2 * listed + 8 : 2 * listed + 9] > 0, 0.0, first_fine
        )
    mine = pl.ds(pl.multiple_of(me * share_rows, share_rows), share_rows)
    empty = code_info_ref[mine, 2 * listed : 2 * listed + 1] == 0
    for part, share in enumerate(split(share_ref[...])):
        terms[part, mine, :] = jnp.where(
            empty, share.astype(F32), terms[part, mine, :].astype(F32)
        ).astype(BF16)

    own_entry = (is_slot & (device_of == me)).astype(BF16)
    second_high, second_low = split(second_ref[...])
    bracket[...] = (
        matmul(own_entry, second_high)
        + matmul(own_entry, second_low)
        - matmul(permuted[0], terms[0])
        - matmul(permuted[0], terms[1])
    )

    @pl.when(large)
    def _():
        bracket[...] -= matmul(permuted[1], terms[0])

    same = (
        jnp.broadcast_to(names[1], (entries, entries))
        == jnp.broadcast_to(names[1], (entries, LANES)).T[0:1, :]
    ).astype(BF16)
    total_high, total_low = split(entry_counts[1])
    totals = matmul(same, total_high) + matmul(same, total_low)
    bracket_high, bracket_low = split(bracket[...])
    centers = matmul(same, bracket_high) + matmul(same, bracket_low)
    centers = centers / jnp.maximum(totals[:, :1], 1.0)
    centers_ref[0], centers_ref[1] = split(centers)
    lane = iota((entries, LANES), 1)
    info = jnp.where(lane == 0, entry_counts[0], entry_counts[1])
    info = jnp.where(lane == 2, cells[0], info)
    entry_info_ref[...] = jnp.where(lane == 3, cells[1], info)

    eye = (iota((LOW, LOW), 0) == iota((LOW, LOW), 1)).astype(BF16)
    for digit in range(high):
        rows = slice(digit * LOW, (digit + 1) * LOW)
        pairs_ref[rows, :] = -matmul_nt(eye, permuted[0, :, rows]).astype(BF16)
    rows_here = vectors.shape[0]
    codes = fine_codes[1:2, :]
    copies = []
    for odd in (1, 0):
        blocks = [at for at in range(groups) if at % 2 == odd]
        for at, block in enumerate(blocks):
            owner = me ^ block
            rows = pl.ds(pl.multiple_of(owner * share_rows, share_rows), share_rows)
            to = slice(at * share_rows, (at + 1) * share_rows)
            left[to, :rows_here] = hot_rows(codes - owner * share_rows, share_rows)
            left[to, rows_here:] = pairs_ref[rows, :]
        start = 0
        for chunk, cut in enumerate(cuts):
            columns = slice(start, start + cut)
            start += cut
            sums = (
                matmul(left[:, :rows_here], vectors[:, columns])
                + matmul(left[:, rows_here:], centers_ref[0, :, columns])
                + matmul(left[:, rows_here:], centers_ref[1, :, columns])
            )
            for part, order_of in enumerate(orders[chunk]):
                if order_of[0] % 2 != odd:
                    continue
                number = 3 * chunk + part
                stage = stages[number]
                for to, block in enumerate(order_of):
                    owner = me ^ block
                    rows = pl.ds(pl.multiple_of(owner * share_rows, share_rows), share_rows)
                    cell_rows = pl.ds(pl.multiple_of(owner * listed, listed), listed)
                    at = blocks.index(block) * share_rows
                    stage[to, :share_rows, :] = sums[at : at + share_rows] + fine[rows, columns]
                    stage[to, share_rows:, :] = bracket[cell_rows, columns]

                @pl.when(large)
                def _():
                    for to, block in enumerate(order_of):
                        owner = me ^ block
                        rows = pl.ds(pl.multiple_of(owner * share_rows, share_rows), share_rows)
                        rest = lax.dot_general(
                            permuted[1, :, rows],
                            centers_ref[0, :, columns],
                            (((0,), (0,)), ((), ())),
                            preferred_element_type=F32,
                        )
                        stage[to, :share_rows, :] -= rest

                copy = pltpu.make_async_copy(stage, out_refs[number], out_sem.at[number])
                copy.start()
                copies.append(copy)
    for copy in copies:
        copy.wait()


def final_kernel(
    groups, slot_count, share_rows, cuts, me_ref, coarse_in, fine_share, first_sums, *refs
):
    last_refs, (code_info, entry_info, coarse_out, fine_out, own_first) = refs[:-5], refs[-5:]
    listed = entry_info.shape[0]
    owner_cells = coarse_in.shape[0]
    by_lane = entry_info[...].T
    for device in range(groups):
        rows = slice(device * slot_count, (device + 1) * slot_count)
        own_first[rows, :] = first_sums[device ^ me_ref[0]]
    hits, counts = [], []
    for sweep in range(2):
        cell = by_lane[2 + sweep : 3 + sweep, :].astype(jnp.int32)
        hit = iota((owner_cells, listed), 0) == cell
        counts.append(
            jnp.sum(jnp.where(hit, by_lane[sweep : sweep + 1, :], 0.0), axis=1, keepdims=True)
        )
        hits.append(hit.astype(BF16))
    first_count = code_info[:, 2 * listed : 2 * listed + 1]
    last_count = code_info[:, 2 * listed + 8 : 2 * listed + 9]
    count = jnp.where(last_count > 0, last_count, first_count)
    start = 0
    for cut, last_sums in zip(cuts, last_refs):
        columns = slice(start, start + cut)
        start += cut
        coarse = coarse_in[:, columns]
        for sweep, sums in enumerate((own_first[:, columns], last_sums[share_rows:, :])):
            sums_high, sums_low = split(sums)
            found = matmul(hits[sweep], sums_high) + matmul(hits[sweep], sums_low)
            weight = 1.0 / jnp.maximum(counts[sweep], 1.0)
            coarse = jnp.where(counts[sweep] > 0, found * weight, coarse)
        coarse_out[:, columns] = coarse
        fine_out[:, columns] = jnp.where(
            count > 0,
            last_sums[:share_rows, :] * (1.0 / jnp.maximum(count, 1.0)),
            fine_share[:, columns],
        )


def exchange(values, step):
    groups = lax.axis_size("cell")
    return lax.ppermute(values, "cell", [(at, at ^ step) for at in range(groups)])


def block_order(bits):
    order = [0]
    for bit in list(bits)[::-1]:
        order = [block + (1 << bit) for block in order] + order
    return order


def block_orders(bits):
    order = block_order(bits)
    half = len(order) // 2
    return [block + 1 for block in order], order[:half], order[half:]


def after(values, *others):
    return lax.optimization_barrier((values, *others))[0]


def halved(got, other, kept):
    half = other.shape[0]
    return other + got[:half], kept + got[half:]


def swap(blocks, bit):
    half = blocks.shape[0] // 2
    got = exchange(blocks[:half], 1 << bit)
    return jnp.concatenate([blocks[half:], got], axis=1)


def local(kernel, shapes, in_specs, out_specs, scratch, flops, name, aliases=None):
    return pl.pallas_call(
        kernel,
        out_shape=tuple(jax.ShapeDtypeStruct(shape, dtype) for shape, dtype in shapes),
        grid_spec=pltpu.PrefetchScalarGridSpec(
            num_scalar_prefetch=1,
            grid=(1,),
            in_specs=in_specs,
            out_specs=out_specs,
            scratch_shapes=scratch,
        ),
        input_output_aliases=aliases or {},
        compiler_params=PARAMS,
        cost_estimate=pl.CostEstimate(
            flops=int(flops), bytes_accessed=10**6, transcendentals=0
        ),
        name=name,
    )


def block(shape, *place):
    return pl.BlockSpec(
        shape, lambda step, me: tuple(me[0] if at is None else at for at in place)
    )


def dense_plan(vectors, row_slot, fine_codes, cell_list, coarse_in, fine_in):
    groups = lax.axis_size("cell")
    rows_here, feature = vectors.shape
    listed = cell_list.shape[1]
    slot_count = listed // groups
    owner_cells = coarse_in.shape[0]
    codewords = fine_in.shape[0]
    share_rows = codewords // groups
    entries = groups * listed
    half = rows_here // 2
    me = lax.axis_index("cell").reshape(1).astype(jnp.int32)

    packed = local(
        lambda me_ref, *refs: pack_kernel(*refs),
        [((8, half + LANES), jnp.int32)],
        [VMEM] * 3,
        [VMEM],
        [],
        1e9,
        "pack",
    )(me, fine_codes, row_slot, cell_list)[0]
    first, second, first_to = local(
        lambda *refs: own_cells_kernel(groups, listed, *refs),
        [((listed, feature), F32)] * 2 + [((groups, 1, slot_count, feature), F32)],
        [VMEM] * 4,
        [VMEM] * 3,
        [],
        5e9,
        "own_cells",
    )(me, vectors, fine_codes, row_slot, fine_in)
    far = groups // 4
    gathered = jnp.stack([packed] + [exchange(packed, 4 * step) for step in range(1, far)])
    sums = []
    for step, base in ((2, 0), (1, codewords // 2)):
        sums += local(
            lambda me_ref, *refs, base=base: own_codes_kernel(base, *refs),
            [((codewords // 2, feature), F32)],
            [VMEM, VMEM, ANY],
            [VMEM],
            [],
            6e9,
            "own_codes",
        )(me, vectors, fine_codes, gathered)
        gathered = jnp.concatenate([gathered, exchange(gathered, step)])

    top = groups.bit_length() - 1
    near_first = list(range(1, top))
    far_first = near_first[1:] + near_first[:1]
    cuts = [feature // 3] * 3
    bits = [near_first, far_first, near_first]
    orders = [block_orders(each) for each in bits]
    shapes = [
        (len(order), share_rows + listed, cut)
        for cut, three in zip(cuts, orders)
        for order in three
    ]
    *terms, code_info, entry_info = local(
        lambda *refs: sums_kernel(groups, slot_count, owner_cells, cuts, orders, *refs),
        [(shape, F32) for shape in shapes]
        + [((codewords, LANES), F32), ((entries, LANES), F32)],
        [VMEM] * 3 + [ANY] * 2 + [VMEM] * 2 + [block((share_rows, feature), None, 0)],
        [ANY] * len(shapes) + [VMEM] * 2,
        [
            pltpu.VMEM((entries, codewords), F32),
            pltpu.VMEM((entries, codewords), F32),
            pltpu.VMEM((listed, listed), jnp.int32),
            pltpu.VMEM((listed, listed), jnp.int32),
            pltpu.VMEM((LANES, codewords), F32),
            pltpu.VMEM((2, codewords, feature), BF16),
            pltpu.VMEM((2, entries, codewords), BF16),
            pltpu.VMEM((LOW, half), BF16),
            pltpu.VMEM((codewords, feature), F32),
            pltpu.VMEM((entries, feature), F32),
            pltpu.VMEM((2, entries, feature), BF16),
            pltpu.VMEM((codewords, entries), BF16),
            pltpu.VMEM((codewords // 2, rows_here + entries), BF16),
            pltpu.SemaphoreType.DMA((2,)),
            pltpu.SemaphoreType.DMA((len(shapes),)),
        ]
        + [pltpu.VMEM(shape, F32) for shape in shapes],
        40e9,
        "sums",
    )(me, gathered, vectors, fine_codes, *sums, first, second, fine_in)

    finished = []
    for at, steps in enumerate(bits):
        away, other, kept = terms[3 * at : 3 * at + 3]
        other, kept = halved(exchange(away, 1), other, kept)
        if at == len(bits) - 1:
            for bit in range(top):
                first_to = swap(after(first_to, other), bit)
        for bit in steps[:-1]:
            got = exchange(other, 1 << bit)
            half = got.shape[0] // 2
            other, kept = halved(got, kept[:half], kept[half:])
        finished.append((kept + exchange(other, 1 << steps[-1]))[0])
    return local(
        lambda *refs: final_kernel(groups, slot_count, share_rows, cuts, *refs),
        [(coarse_in.shape, F32), ((share_rows, feature), F32)],
        [VMEM, block((share_rows, feature), None, 0)]
        + [VMEM] * (1 + len(cuts))
        + [block((share_rows, LANES), None, 0), block((listed, LANES), None, 0)],
        [VMEM] * 2,
        [pltpu.VMEM((listed, feature), F32)],
        1e9,
        "outputs",
    )(me, coarse_in, fine_in, first_to[0], *finished, code_info, entry_info)


def fits_dense(mesh_groups, listed, codewords, rows_here, feature):
    entries = mesh_groups * listed
    power = mesh_groups & (mesh_groups - 1) == 0 and mesh_groups >= 4
    digits = codewords % (2 * LOW) == 0 and (codewords // LOW) * listed <= LOW
    shapes = rows_here % (2 * LANES) == 0 and feature % (6 * LANES) == 0
    return power and digits and shapes and entries * codewords <= 2**20


def per_device(vectors, row_slot, fine_codes, cell_list, coarse_in, fine_in):
    groups = lax.axis_size("cell")
    dense = fits_dense(groups, cell_list.shape[1], *fine_in.shape[:1], *vectors.shape)
    plan = dense_plan if dense else routed_plan
    return plan(vectors, row_slot, fine_codes, cell_list, coarse_in, fine_in)


def solution(mesh):
    return jax.shard_map(
        per_device,
        mesh=mesh,
        in_specs=(
            P(("parts", "cell"), None),
            P(None, ("parts", "cell")),
            P(None, ("parts", "cell")),
            P(None, ("parts", "cell")),
            P("cell", None),
            P(),
        ),
        out_specs=(P(("parts", "cell"), None), P(("parts", "cell"), None)),
        check_vma=False,
    )
```

profile of v0, /device:TPU:0, one launch (start us, length us, event | category | flops | bytes accessed | tf_op | source)
XLA Modules:
  0.0 141.4 jit_solution(3918611989015133046)
XLA Ops:
  0.6 1.3 pack.1
  2.0 5.0 %collective-permute-start.2 = (s32[8,896]{1,0:T(8,128)}, s32[8,896]{1,0:T(8,128)S(1)}, u32[]{:S(2)}, u32[]{:S(2)}) collective-permute-start(s32[8,896]{1,0:T(8,128)} %pack.1), channel_id=1, source_target_pairs={{0,12},{1,13},{2,14},{3,15},{4,8},{5,9},{6,10},{7,11},{8,4},{9,5},... | collective-permute-start | bytes 86024 | tf_op jit(solution)/shard_map/ppermute | solution.py:478
  7.6 6.6 %own_cells.1 = (f32[32,768]{1,0:T(8,128)}, f32[32,768]{1,0:T(8,128)}, f32[16,1,2,768]{3,2,1,0:T(2,128)}) custom-call(s32[1]{0:T(128)} %bitcast.refs_0_.me_ref, bf16[1536,768]{1,0:T(8,128)(2,1)} %refs_2_.6, s32[2,1536]{1,0:T(2,128)} %refs_3_.3, s32[2,1536]{1,0:T(2,128)} %refs_1_.6, f32[2048,768]{1,0:T(8,128)} %refs_2_.7), custom_call_target="tpu_custom_call" | custom-call | flops 5000000000 | bytes 1000000 | tf_op jit(solution)/shard_map/own_cells/pallas_call | solution.py:556
  14.3 1.8 %collective-permute-start.3 = (s32[4,8,896]{2,1,0:T(8,128)S(1)}, s32[4,8,896]{2,1,0:T(8,128)S(1)}, u32[]{:S(2)}, u32[]{:S(2)}) collective-permute-start(s32[4,8,896]{2,1,0:T(8,128)S(1)} %pad_add_fusion.refs_2_), channel_id=1, source_target_pairs={{0,2},{1,3},{2,0},{3,1},{4,6},{5,7},{6,4},{7,5},{8,10},{9,11},{10,... | collective-permute-start | bytes 344072 | tf_op jit(solution)/shard_map/ppermute | solution.py:478
  16.1 5.9 %own_codes.2.refs_4_ = f32[1024,768]{1,0:T(8,128)} custom-call(s32[1]{0:T(128)} %bitcast.refs_0_.me_ref, bf16[1536,768]{1,0:T(8,128)(2,1)} %refs_2_.6, s32[2,1536]{1,0:T(2,128)} %refs_3_.3, s32[4,8,896]{2,1,0:T(8,128)} %copy-done.4), custom_call_target="tpu_custom_call" | custom-call | flops 6000000000 | bytes 1000000 | tf_op jit(solution)/shard_map/own_codes/pallas_call | solution.py:569
  22.7 5.9 %own_codes.3.refs_5_ = f32[1024,768]{1,0:T(8,128)} custom-call(s32[1]{0:T(128)} %bitcast.refs_0_.me_ref, bf16[1536,768]{1,0:T(8,128)(2,1)} %refs_2_.6, s32[2,1536]{1,0:T(2,128)} %refs_3_.3, s32[8,8,896]{2,1,0:T(8,128)} %copy-done.7), custom_call_target="tpu_custom_call" | custom-call | flops 6000000000 | bytes 1000000 | tf_op jit(solution)/shard_map/own_codes/pallas_call | solution.py:569
  28.7 0.8 copy-done.8
  29.5 35.7 %sums.1 = (f32[8,160,256]{2,1,0:T(8,128)}, f32[4,160,256]{2,1,0:T(8,128)}, f32[4,160,256]{2,1,0:T(8,128)}, f32[8,160,256]{2,1,0:T(8,128)}, f32[4,160,256]{2,1,0:...) custom-call(s32[1]{0:T(128)} %bitcast.refs_0_.me_ref, ...), custom_call_target="tpu_custom_call" | custom-call | flops 40000000000 | bytes 1000000 | tf_op jit(solution)/shard_map/sums/pallas_call | solution.py:591
  65.8 2.7 %collective-permute-done.5 = f32[8,160,256]{2,1,0:T(8,128)S(1)} collective-permute-done((f32[8,160,256]{2,1,0:T(8,128)}, f32[8,160,256]{2,1,0:T(8,128)S(1)}, u32[]{:S(2)}, u32[]{:S(2)}) %collective-permute-start.5) | collective-permute-done | bytes 1310752 | tf_op jit(solution)/shard_map/ppermute | solution.py:478
  68.6 1.6 %slice_add_fusion = (f32[4,160,256]{2,1,0:T(8,128)S(1)}, f32[4,160,256]{2,1,0:T(8,128)S(1)}) fusion(f32[4,160,256]{2,1,0:T(8,128)} %get-tuple-element.35, f32[8,160,256]{2,1,0:T(8,128)S(1)} %collective-permute-done.5, f32[4,160,256]{2,1,0:T(8,128)} %get-tuple-element.23), kind=kLoop, calls=%fused_computation | loop fusion | flops 327680 | bytes 3932160 | tf_op jit(solution)/shard_map/add | solution.py:500
  70.8 0.7 collective-permute-done.6
  72.2 1.5 %collective-permute-start.18 = (f32[4,160,256]{2,1,0:T(8,128)S(1)}, f32[4,160,256]{2,1,0:T(8,128)S(1)}, u32[]{:S(2)}, u32[]{:S(2)}) collective-permute-start(f32[4,160,256]{2,1,0:T(8,128)S(1)} %get-tuple-element.41), channel_id=1, source_target_pairs={{0,2},{1,3},{2,0},{3,1},{4,6},{5,7},{6,4},{7,5},{8,10},{9,11},{10,... | collective-permute-start | bytes 1966088 | tf_op jit(solution)/shard_map/ppermute | solution.py:478
  73.7 2.6 %collective-permute-done.7 = f32[4,2,2,768]{3,2,1,0:T(2,128)S(1)} collective-permute-done((f32[4,2,2,768]{3,2,1,0:T(2,128)S(1)}, f32[4,2,2,768]{3,2,1,0:T(2,128)S(1)}, u32[]{:S(2)}, u32[]{:S(2)}) %collective-permute-start.7) | collective-permute-done | bytes 49184 | tf_op jit(solution)/shard_map/ppermute | solution.py:478
  76.3 1.3 collective-permute-start.8
  78.2 2.3 %collective-permute-done.8 = f32[2,4,2,768]{3,2,1,0:T(2,128)S(1)} collective-permute-done((f32[2,4,2,768]{3,2,1,0:T(2,128)S(1)}, f32[2,4,2,768]{3,2,1,0:T(2,128)S(1)}, u32[]{:S(2)}, u32[]{:S(2)}) %collective-permute-start.8) | collective-permute-done | bytes 49184 | tf_op jit(solution)/shard_map/ppermute | solution.py:478
  80.5 2.2 %collective-permute-start.9 = (f32[1,8,2,768]{3,2,1,0:T(2,128)S(1)}, f32[1,8,2,768]{3,2,1,0:T(2,128)S(1)}, u32[]{:S(2)}, u32[]{:S(2)}) collective-permute-start(f32[1,8,2,768]{3,2,1,0:T(2,128)S(1)} %get-tuple-element.53), channel_id=1, source_target_pairs={{0,8},{1,9},{2,10},{3,11},{4,12},{5,13},{6,14},{7,15},{8,0},{9,1},... | collective-permute-start | bytes 147464 | tf_op jit(solution)/shard_map/ppermute | solution.py:478
  82.9 2.1 %collective-permute-start.15 = (f32[4,160,256]{2,1,0:T(8,128)S(1)}, f32[4,160,256]{2,1,0:T(8,128)S(1)}, u32[]{:S(2)}, u32[]{:S(2)}) collective-permute-start(f32[4,160,256]{2,1,0:T(8,128)S(1)} %get-tuple-element.45), channel_id=1, source_target_pairs={{0,4},{1,5},{2,6},{3,7},{4,0},{5,1},{6,2},{7,3},{8,12},{9,13},{10,... | collective-permute-start | bytes 1966088 | tf_op jit(solution)/shard_map/ppermute | solution.py:478
  85.0 0.7 collective-permute-done.9
  86.3 3.9 %collective-permute-done.18 = f32[4,160,256]{2,1,0:T(8,128)S(1)} collective-permute-done((f32[4,160,256]{2,1,0:T(8,128)S(1)}, f32[4,160,256]{2,1,0:T(8,128)S(1)}, u32[]{:S(2)}, u32[]{:S(2)}) %collective-permute-start.18) | collective-permute-done | bytes 655392 | tf_op jit(solution)/shard_map/ppermute | solution.py:478
  90.4 1.3 collective-permute-start.19
  91.7 11.9 %collective-permute-done.11 = f32[4,160,256]{2,1,0:T(8,128)S(1)} collective-permute-done((f32[4,160,256]{2,1,0:T(8,128)S(1)}, f32[4,160,256]{2,1,0:T(8,128)S(1)}, u32[]{:S(2)}, u32[]{:S(2)}) %collective-permute-start.11) | collective-permute-done | bytes 655392 | tf_op jit(solution)/shard_map/ppermute | solution.py:478
  103.6 1.3 collective-permute-start.12
  105.0 3.0 %collective-permute-start.16 = (f32[2,160,256]{2,1,0:T(8,128)S(1)}, f32[2,160,256]{2,1,0:T(8,128)S(1)}, u32[]{:S(2)}, u32[]{:S(2)}) collective-permute-start(f32[2,160,256]{2,1,0:T(8,128)S(1)} %get-tuple-element.43), channel_id=1, source_target_pairs={{0,8},{1,9},{2,10},{3,11},{4,12},{5,13},{6,14},{7,15},{8,0},{9,1},... | collective-permute-start | bytes 983048 | tf_op jit(solution)/shard_map/ppermute | solution.py:478
  108.1 11.1 %collective-permute-done.12 = f32[2,160,256]{2,1,0:T(8,128)S(1)} collective-permute-done((f32[2,160,256]{2,1,0:T(8,128)S(1)}, f32[2,160,256]{2,1,0:T(8,128)S(1)}, u32[]{:S(2)}, u32[]{:S(2)}) %collective-permute-start.12) | collective-permute-done | bytes 327712 | tf_op jit(solution)/shard_map/ppermute | solution.py:478
  119.8 10.9 %collective-permute-done.16 = f32[2,160,256]{2,1,0:T(8,128)S(1)} collective-permute-done((f32[2,160,256]{2,1,0:T(8,128)S(1)}, f32[2,160,256]{2,1,0:T(8,128)S(1)}, u32[]{:S(2)}, u32[]{:S(2)}) %collective-permute-start.16) | collective-permute-done | bytes 327712 | tf_op jit(solution)/shard_map/ppermute | solution.py:478
  130.7 0.9 collective-permute-start.17
  131.6 2.6 %collective-permute-done.20 = f32[1,160,256]{2,1,0:T(8,128)S(1)} collective-permute-done((f32[1,160,256]{2,1,0:T(8,128)S(1)}, f32[1,160,256]{2,1,0:T(8,128)S(1)}, u32[]{:S(2)}, u32[]{:S(2)}) %collective-permute-start.20) | collective-permute-done | bytes 163872 | tf_op jit(solution)/shard_map/ppermute | solution.py:478
  134.2 0.7 fusion.1.refs_6_
  134.9 1.2 collective-permute-done.13
  136.0 0.7 fusion.5.refs_4_
  136.8 0.7 fusion.3.refs_5_
  137.4 4.0 %outputs.1 = (f32[512,768]{1,0:T(8,128)}, f32[128,768]{1,0:T(8,128)}) custom-call(s32[1]{0:T(128)} %bitcast.refs_0_.me_ref, f32[512,768]{1,0:T(8,128)} %refs_1_.9, f32[2048,768]{1,0:T(8,128)} %refs_2_.7, f32[16,2,768]{2,1,0:T(2,128)} %maximum_bitcast_fusion.refs_3_, f32[160,256]{1,0:T(8,128)} %fusion.5.refs_4_, f32[160,256]{1,0:T(8,128)} %fusion.3.refs_5_, ...), custom_call_target="tpu_custom_call" | custom-call | flops 1000000000 | bytes 1000000 | tf_op jit(solution)/shard_map/outputs/pallas_call | solution.py:631
  (63 shorter events, 5.7 us)
Async XLA Ops:
  2.0 12.2 %copy-start.5 = (s32[8,896]{1,0:T(8,128)S(1)}, s32[8,896]{1,0:T(8,128)}, u32[]{:S(2)}) copy-start(s32[8,896]{1,0:T(8,128)} %pack.1) | copy-start | bytes 86020
  2.0 12.2 %collective-permute-start.2 = (s32[8,896]{1,0:T(8,128)}, s32[8,896]{1,0:T(8,128)S(1)}, u32[]{:S(2)}, u32[]{:S(2)}) collective-permute-start(s32[8,896]{1,0:T(8,128)} %pack.1), channel_id=1, source_target_pairs={{0,12},{1,13},{2,14},{3,15},{4,8},{5,9},{6,10},{7,11},{8,4},{9,5},... | collective-permute-start | bytes 86024 | tf_op jit(solution)/shard_map/ppermute | solution.py:478
  7.0 7.2 %collective-permute-start.1 = (s32[8,896]{1,0:T(8,128)}, s32[8,896]{1,0:T(8,128)S(1)}, u32[]{:S(2)}, u32[]{:S(2)}) collective-permute-start(s32[8,896]{1,0:T(8,128)} %pack.1), channel_id=1, source_target_pairs={{0,8},{1,9},{2,10},{3,11},{4,12},{5,13},{6,14},{7,15},{8,0},{9,1},... | collective-permute-start | bytes 86024 | tf_op jit(solution)/shard_map/ppermute | solution.py:478
  7.0 7.2 %collective-permute-start = (s32[8,896]{1,0:T(8,128)}, s32[8,896]{1,0:T(8,128)S(1)}, u32[]{:S(2)}, u32[]{:S(2)}) collective-permute-start(s32[8,896]{1,0:T(8,128)} %pack.1), channel_id=1, source_target_pairs={{0,4},{1,5},{2,6},{3,7},{4,0},{5,1},{6,2},{7,3},{8,12},{9,13},{10,... | collective-permute-start | bytes 86024 | tf_op jit(solution)/shard_map/ppermute | solution.py:478
  14.2 1.8 %copy-start.4 = (s32[4,8,896]{2,1,0:T(8,128)}, s32[4,8,896]{2,1,0:T(8,128)S(1)}, u32[]{:S(2)}) copy-start(s32[4,8,896]{2,1,0:T(8,128)S(1)} %pad_add_fusion.refs_2_) | copy-start | bytes 344068
  14.3 7.7 %collective-permute-start.3 = (s32[4,8,896]{2,1,0:T(8,128)S(1)}, s32[4,8,896]{2,1,0:T(8,128)S(1)}, u32[]{:S(2)}, u32[]{:S(2)}) collective-permute-start(s32[4,8,896]{2,1,0:T(8,128)S(1)} %pad_add_fusion.refs_2_), channel_id=1, source_target_pairs={{0,2},{1,3},{2,0},{3,1},{4,6},{5,7},{6,4},{7,5},{8,10},{9,11},{10,... | collective-permute-start | bytes 344072 | tf_op jit(solution)/shard_map/ppermute | solution.py:478
  22.0 0.7 copy-start.7
  22.1 6.6 %collective-permute-start.4 = (s32[8,8,896]{2,1,0:T(8,128)S(1)}, s32[8,8,896]{2,1,0:T(8,128)S(1)}, u32[]{:S(2)}, u32[]{:S(2)}) collective-permute-start(s32[8,8,896]{2,1,0:T(8,128)S(1)} %get-tuple-element.50.refs_2_), channel_id=1, source_target_pairs={{0,1},{1,0},{2,3},{3,2},{4,5},{5,4},{6,7},{7,6},{8,9},{9,8},{10,11... | collective-permute-start | bytes 688136 | tf_op jit(solution)/shard_map/ppermute | solution.py:478
  28.7 0.8 copy-start.8
  65.2 3.3 %collective-permute-start.5 = (f32[8,160,256]{2,1,0:T(8,128)}, f32[8,160,256]{2,1,0:T(8,128)S(1)}, u32[]{:S(2)}, u32[]{:S(2)}) collective-permute-start(f32[8,160,256]{2,1,0:T(8,128)} %get-tuple-element.24), channel_id=1, source_target_pairs={{0,1},{1,0},{2,3},{3,2},{4,5},{5,4},{6,7},{7,6},{8,9},{9,8},{10,11... | collective-permute-start | bytes 3932168 | tf_op jit(solution)/shard_map/ppermute | solution.py:478
  65.3 12.3 %collective-permute-start.10 = (f32[8,160,256]{2,1,0:T(8,128)}, f32[8,160,256]{2,1,0:T(8,128)S(1)}, u32[]{:S(2)}, u32[]{:S(2)}) collective-permute-start(f32[8,160,256]{2,1,0:T(8,128)} %get-tuple-element.30), channel_id=1, source_target_pairs={{0,1},{1,0},{2,3},{3,2},{4,5},{5,4},{6,7},{7,6},{8,9},{9,8},{10,11... | collective-permute-start | bytes 3932168 | tf_op jit(solution)/shard_map/ppermute | solution.py:478
  68.5 1.6 %copy-start.6 = (f32[16,1,2,768]{3,2,1,0:T(2,128)S(1)}, f32[16,1,2,768]{3,2,1,0:T(2,128)}, u32[]{:S(2)}) copy-start(f32[16,1,2,768]{3,2,1,0:T(2,128)} %get-tuple-element.25) | copy-start | bytes 294916
  68.6 1.9 %copy-start.9 = (f32[8,160,256]{2,1,0:T(8,128)S(1)}, f32[8,160,256]{2,1,0:T(8,128)}, u32[]{:S(2)}) copy-start(f32[8,160,256]{2,1,0:T(8,128)} %get-tuple-element.33) | copy-start | bytes 3932164
  68.6 9.0 %copy-start.3 = (f32[4,160,256]{2,1,0:T(8,128)S(1)}, f32[4,160,256]{2,1,0:T(8,128)}, u32[]{:S(2)}) copy-start(f32[4,160,256]{2,1,0:T(8,128)} %get-tuple-element.29) | copy-start | bytes 1966084
  70.2 7.4 %copy-start.2 = (f32[4,160,256]{2,1,0:T(8,128)S(1)}, f32[4,160,256]{2,1,0:T(8,128)}, u32[]{:S(2)}) copy-start(f32[4,160,256]{2,1,0:T(8,128)} %get-tuple-element.31) | copy-start | bytes 1966084
  70.2 1.3 collective-permute-start.6
  70.4 12.3 %collective-permute-start.14 = (f32[8,160,256]{2,1,0:T(8,128)S(1)}, f32[8,160,256]{2,1,0:T(8,128)S(1)}, u32[]{:S(2)}, u32[]{:S(2)}) collective-permute-start(f32[8,160,256]{2,1,0:T(8,128)S(1)} %copy-done.9), channel_id=1, source_target_pairs={{0,1},{1,0},{2,3},{3,2},{4,5},{5,4},{6,7},{7,6},{8,9},{9,8},{10,11... | collective-permute-start | bytes 3932168 | tf_op jit(solution)/shard_map/ppermute | solution.py:478
  71.6 4.7 %collective-permute-start.7 = (f32[4,2,2,768]{3,2,1,0:T(2,128)S(1)}, f32[4,2,2,768]{3,2,1,0:T(2,128)S(1)}, u32[]{:S(2)}, u32[]{:S(2)}) collective-permute-start(f32[4,2,2,768]{3,2,1,0:T(2,128)S(1)} %get-tuple-element.57), channel_id=1, source_target_pairs={{0,2},{1,3},{2,0},{3,1},{4,6},{5,7},{6,4},{7,5},{8,10},{9,11},{10,... | collective-permute-start | bytes 147464 | tf_op jit(solution)/shard_map/ppermute | solution.py:478
  72.2 18.1 %collective-permute-start.18 = (f32[4,160,256]{2,1,0:T(8,128)S(1)}, f32[4,160,256]{2,1,0:T(8,128)S(1)}, u32[]{:S(2)}, u32[]{:S(2)}) collective-permute-start(f32[4,160,256]{2,1,0:T(8,128)S(1)} %get-tuple-element.41), channel_id=1, source_target_pairs={{0,2},{1,3},{2,0},{3,1},{4,6},{5,7},{6,4},{7,5},{8,10},{9,11},{10,... | collective-permute-start | bytes 1966088 | tf_op jit(solution)/shard_map/ppermute | solution.py:478
  76.3 4.2 %collective-permute-start.8 = (f32[2,4,2,768]{3,2,1,0:T(2,128)S(1)}, f32[2,4,2,768]{3,2,1,0:T(2,128)S(1)}, u32[]{:S(2)}, u32[]{:S(2)}) collective-permute-start(f32[2,4,2,768]{3,2,1,0:T(2,128)S(1)} %get-tuple-element.55), channel_id=1, source_target_pairs={{0,4},{1,5},{2,6},{3,7},{4,0},{5,1},{6,2},{7,3},{8,12},{9,13},{10,... | collective-permute-start | bytes 147464 | tf_op jit(solution)/shard_map/ppermute | solution.py:478
  77.6 5.1 %copy-start = (f32[4,160,256]{2,1,0:T(8,128)S(1)}, f32[4,160,256]{2,1,0:T(8,128)}, u32[]{:S(2)}) copy-start(f32[4,160,256]{2,1,0:T(8,128)} %get-tuple-element.34) | copy-start | bytes 1966084
  77.6 5.1 %copy-start.1 = (f32[4,160,256]{2,1,0:T(8,128)S(1)}, f32[4,160,256]{2,1,0:T(8,128)}, u32[]{:S(2)}) copy-start(f32[4,160,256]{2,1,0:T(8,128)} %get-tuple-element.32) | copy-start | bytes 1966084
  77.8 25.7 %collective-permute-start.11 = (f32[4,160,256]{2,1,0:T(8,128)S(1)}, f32[4,160,256]{2,1,0:T(8,128)S(1)}, u32[]{:S(2)}, u32[]{:S(2)}) collective-permute-start(f32[4,160,256]{2,1,0:T(8,128)S(1)} %get-tuple-element.49), channel_id=1, source_target_pairs={{0,2},{1,3},{2,0},{3,1},{4,6},{5,7},{6,4},{7,5},{8,10},{9,11},{10,... | collective-permute-start | bytes 1966088 | tf_op jit(solution)/shard_map/ppermute | solution.py:478
  80.5 5.2 %collective-permute-start.9 = (f32[1,8,2,768]{3,2,1,0:T(2,128)S(1)}, f32[1,8,2,768]{3,2,1,0:T(2,128)S(1)}, u32[]{:S(2)}, u32[]{:S(2)}) collective-permute-start(f32[1,8,2,768]{3,2,1,0:T(2,128)S(1)} %get-tuple-element.53), channel_id=1, source_target_pairs={{0,8},{1,9},{2,10},{3,11},{4,12},{5,13},{6,14},{7,15},{8,0},{9,1},... | collective-permute-start | bytes 147464 | tf_op jit(solution)/shard_map/ppermute | solution.py:478
  82.9 22.0 %collective-permute-start.15 = (f32[4,160,256]{2,1,0:T(8,128)S(1)}, f32[4,160,256]{2,1,0:T(8,128)S(1)}, u32[]{:S(2)}, u32[]{:S(2)}) collective-permute-start(f32[4,160,256]{2,1,0:T(8,128)S(1)} %get-tuple-element.45), channel_id=1, source_target_pairs={{0,4},{1,5},{2,6},{3,7},{4,0},{5,1},{6,2},{7,3},{8,12},{9,13},{10,... | collective-permute-start | bytes 1966088 | tf_op jit(solution)/shard_map/ppermute | solution.py:478
  90.4 17.7 %collective-permute-start.19 = (f32[2,160,256]{2,1,0:T(8,128)S(1)}, f32[2,160,256]{2,1,0:T(8,128)S(1)}, u32[]{:S(2)}, u32[]{:S(2)}) collective-permute-start(f32[2,160,256]{2,1,0:T(8,128)S(1)} %get-tuple-element.39), channel_id=1, source_target_pairs={{0,4},{1,5},{2,6},{3,7},{4,0},{5,1},{6,2},{7,3},{8,12},{9,13},{10,... | collective-permute-start | bytes 983048 | tf_op jit(solution)/shard_map/ppermute | solution.py:478
  103.6 15.6 %collective-permute-start.12 = (f32[2,160,256]{2,1,0:T(8,128)S(1)}, f32[2,160,256]{2,1,0:T(8,128)S(1)}, u32[]{:S(2)}, u32[]{:S(2)}) collective-permute-start(f32[2,160,256]{2,1,0:T(8,128)S(1)} %get-tuple-element.47), channel_id=1, source_target_pairs={{0,4},{1,5},{2,6},{3,7},{4,0},{5,1},{6,2},{7,3},{8,12},{9,13},{10,... | collective-permute-start | bytes 983048 | tf_op jit(solution)/shard_map/ppermute | solution.py:478
  105.0 25.7 %collective-permute-start.16 = (f32[2,160,256]{2,1,0:T(8,128)S(1)}, f32[2,160,256]{2,1,0:T(8,128)S(1)}, u32[]{:S(2)}, u32[]{:S(2)}) collective-permute-start(f32[2,160,256]{2,1,0:T(8,128)S(1)} %get-tuple-element.43), channel_id=1, source_target_pairs={{0,8},{1,9},{2,10},{3,11},{4,12},{5,13},{6,14},{7,15},{8,0},{9,1},... | collective-permute-start | bytes 983048 | tf_op jit(solution)/shard_map/ppermute | solution.py:478
  108.0 26.2 %collective-permute-start.20 = (f32[1,160,256]{2,1,0:T(8,128)S(1)}, f32[1,160,256]{2,1,0:T(8,128)S(1)}, u32[]{:S(2)}, u32[]{:S(2)}) collective-permute-start(f32[1,160,256]{2,1,0:T(8,128)S(1)} %slice_add_fusion.12), channel_id=1, source_target_pairs={{0,8},{1,9},{2,10},{3,11},{4,12},{5,13},{6,14},{7,15},{8,0},{9,1},... | collective-permute-start | bytes 491528 | tf_op jit(solution)/shard_map/ppermute | solution.py:478
  119.3 16.8 %collective-permute-start.13 = (f32[1,160,256]{2,1,0:T(8,128)S(1)}, f32[1,160,256]{2,1,0:T(8,128)S(1)}, u32[]{:S(2)}, u32[]{:S(2)}) collective-permute-start(f32[1,160,256]{2,1,0:T(8,128)S(1)} %slice_add_fusion.16), channel_id=1, source_target_pairs={{0,8},{1,9},{2,10},{3,11},{4,12},{5,13},{6,14},{7,15},{8,0},{9,1},... | collective-permute-start | bytes 491528 | tf_op jit(solution)/shard_map/ppermute | solution.py:478
  130.7 6.0 %collective-permute-start.17 = (f32[1,160,256]{2,1,0:T(8,128)S(1)}, f32[1,160,256]{2,1,0:T(8,128)S(1)}, u32[]{:S(2)}, u32[]{:S(2)}) collective-permute-start(f32[1,160,256]{2,1,0:T(8,128)S(1)} %slice_add_fusion.14), channel_id=1, source_target_pairs={{0,2},{1,3},{2,0},{3,1},{4,6},{5,7},{6,4},{7,5},{8,10},{9,11},{10,... | collective-permute-start | bytes 491528 | tf_op jit(solution)/shard_map/ppermute | solution.py:478
where the time goes:
time: 142 us; the launch traced here: 141 us
  Pallas kernels  59.5 us (42%)
  waiting for transfers between devices  50.5 us (36%)
  starting transfers between devices  23.8 us (17%)
  other arithmetic  5.16 us (4%)
  local copies, waits for them, and re-layouts  1.52 us (1%)
    ppermute x21, waiting for transfers between devices, exchange(): lax.ppermute(values, 'cell', [(at, at ^ step) for at in range(groups)])  50.5 us
    pallas_call x1, Pallas kernels, dense_plan(): local(lambda *refs: sums_kernel(groups, slot_count, owner_cells, cuts, or...  35.7 us
    ppermute x21, starting transfers between devices, exchange(): lax.ppermute(values, 'cell', [(at, at ^ step) for at in range(groups)])  23.8 us
    pallas_call x2, Pallas kernels, dense_plan(): local(lambda me_ref, *refs, base=base: own_codes_kernel(base, *refs), [((...  11.9 us
    pallas_call x1, Pallas kernels, dense_plan(): local(lambda *refs: own_cells_kernel(groups, listed, *refs), [((listed, f...  6.59 us
    pallas_call x1, Pallas kernels, dense_plan(): local(lambda *refs: final_kernel(groups, slot_count, share_rows, cuts, *r...  3.96 us
  transfers between devices with their start and end apart: 21, of which 11 were waited for; matrix products, arithmetic and copies ran while one was open for 3% of the time, Pallas kernels for 13%

commit v1 on v0

--- a/solution.py
+++ b/solution.py
@@ -177,7 +177,8 @@
     top = groups.bit_length() - 1
     for owner in range(groups):
         block = owner ^ me_ref[0]
-        at = sum((1 - (block >> bit & 1)) << (top - 1 - bit) for bit in range(top))
+        at = sum((1 - (block >> bit & 1)) << (top - 1 - bit) for bit in range(2))
+        at = at + groups // 4 - 1 - (block >> 2)
         to_ref[at, 0] = first[owner * slots : (owner + 1) * slots]
 
 
@@ -576,6 +577,8 @@
             "own_codes",
         )(me, vectors, fine_codes, gathered)
         gathered = jnp.concatenate([gathered, exchange(gathered, step)])
+        if step == 2:
+            first_to = swap(first_to, 0)
 
     top = groups.bit_length() - 1
     near_first = list(range(1, top))
@@ -616,13 +619,16 @@
         "sums",
     )(me, gathered, vectors, fine_codes, *sums, first, second, fine_in)
 
+    first_to = swap(after(first_to, terms[0]), 1)
     finished = []
     for at, steps in enumerate(bits):
         away, other, kept = terms[3 * at : 3 * at + 3]
         other, kept = halved(exchange(away, 1), other, kept)
         if at == len(bits) - 1:
-            for bit in range(top):
-                first_to = swap(after(first_to, other), bit)
+            first_to = after(first_to, other)[::-1]
+            first_to = jnp.concatenate(
+                [first_to[0]] + [exchange(first_to[z], 4 * z) for z in range(1, far)]
+            )
         for bit in steps[:-1]:
             got = exchange(other, 1 << bit)
             half = got.shape[0] // 2
@@ -638,7 +644,7 @@
         [pltpu.VMEM((listed, feature), F32)],
         1e9,
         "outputs",
-    )(me, coarse_in, fine_in, first_to[0], *finished, code_info, entry_info)
+    )(me, coarse_in, fine_in, first_to, *finished, code_info, entry_info)
 
 
 def fits_dense(mesh_groups, listed, codewords, rows_here, feature):

time: 142 us -> 135 us (0.951)
  waiting for transfers between devices: 50.5 us -> 45.2 us
  starting transfers between devices: 23.8 us -> 21 us
    ppermute x21 -> x22, waiting for transfers between devices: 50.5 us -> 45.2 us  [exchange(): lax.ppermute(values, 'cell', [(at, at ^ step) for at in range(groups)])]
    ppermute x21 -> x22, starting transfers between devices: 23.8 us -> 21 us  [exchange(): lax.ppermute(values, 'cell', [(at, at ^ step) for at in range(groups)])]
  transfers between devices with their start and end apart: 21 -> 22, of which waited for: 11 -> 8; matrix products, arithmetic and copies ran while one was open for 3% -> 3% of each run, Pallas kernels for 13% -> 14%
where the time goes in v1:
time: 135 us; the launch traced here: 134 us
  Pallas kernels  59.6 us (44%)
  waiting for transfers between devices  45.2 us (33%)
  starting transfers between devices  21 us (16%)
  other arithmetic  5.11 us (4%)
  local copies, waits for them, and re-layouts  2.49 us (2%)
    ppermute x22, waiting for transfers between devices, exchange(): lax.ppermute(values, 'cell', [(at, at ^ step) for at in range(groups)])  45.2 us
    pallas_call x1, Pallas kernels, dense_plan(): local(lambda *refs: sums_kernel(groups, slot_count, owner_cells, cuts, or...  35.8 us
    ppermute x22, starting transfers between devices, exchange(): lax.ppermute(values, 'cell', [(at, at ^ step) for at in range(groups)])  21 us
    pallas_call x2, Pallas kernels, dense_plan(): local(lambda me_ref, *refs, base=base: own_codes_kernel(base, *refs), [((...  11.9 us
    pallas_call x1, Pallas kernels, dense_plan(): local(lambda *refs: own_cells_kernel(groups, listed, *refs), [((listed, f...  6.59 us
    pallas_call x1, Pallas kernels, dense_plan(): local(lambda *refs: final_kernel(groups, slot_count, share_rows, cuts, *r...  3.97 us
  transfers between devices with their start and end apart: 22, of which 8 were waited for; matrix products, arithmetic and copies ran while one was open for 3% of the time, Pallas kernels for 14%

profile of v1, /device:TPU:0, one launch (start us, length us, event | category | flops | bytes accessed | tf_op | source)
XLA Modules:
  0.0 134.2 jit_solution(11764460013533460879)
XLA Ops:
  0.6 1.3 %pack.1 = s32[8,896]{1,0:T(8,128)} custom-call(s32[1]{0:T(128)} %bitcast.refs_0_.me_ref, s32[2,1536]{1,0:T(2,128)} %refs_3_.3, s32[2,1536]{1,0:T(2,128)} %refs_1_.6, s32[2,32]{1,0:T(2,128)} %refs_2_.5), custom_call_target="tpu_custom_call" | custom-call | flops 1000000000 | bytes 1000000 | tf_op jit(solution)/shard_map/pack/pallas_call | solution.py:548
  2.0 5.0 %collective-permute-start.3 = (s32[8,896]{1,0:T(8,128)}, s32[8,896]{1,0:T(8,128)S(1)}, u32[]{:S(2)}, u32[]{:S(2)}) collective-permute-start(s32[8,896]{1,0:T(8,128)} %pack.1), channel_id=1, source_target_pairs={{0,12},{1,13},{2,14},{3,15},{4,8},{5,9},{6,10},{7,11},{8,4},{9,5},... | collective-permute-start | bytes 86024 | tf_op jit(solution)/shard_map/ppermute | solution.py:479
  7.6 6.6 %own_cells.1 = (f32[32,768]{1,0:T(8,128)}, f32[32,768]{1,0:T(8,128)}, f32[16,1,2,768]{3,2,1,0:T(2,128)}) custom-call(s32[1]{0:T(128)} %bitcast.refs_0_.me_ref, bf16[1536,768]{1,0:T(8,128)(2,1)} %refs_2_.6, s32[2,1536]{1,0:T(2,128)} %refs_3_.3, s32[2,1536]{1,0:T(2,128)} %refs_1_.6, f32[2048,768]{1,0:T(8,128)} %refs_2_.7), custom_call_target="tpu_custom_call" | custom-call | flops 5000000000 | bytes 1000000 | tf_op jit(solution)/shard_map/own_cells/pallas_call | solution.py:557
  14.3 1.8 %collective-permute-start.4 = (s32[4,8,896]{2,1,0:T(8,128)S(1)}, s32[4,8,896]{2,1,0:T(8,128)S(1)}, u32[]{:S(2)}, u32[]{:S(2)}) collective-permute-start(s32[4,8,896]{2,1,0:T(8,128)S(1)} %pad_add_fusion.refs_2_), channel_id=1, source_target_pairs={{0,2},{1,3},{2,0},{3,1},{4,6},{5,7},{6,4},{7,5},{8,10},{9,11},{10,... | collective-permute-start | bytes 344072 | tf_op jit(solution)/shard_map/ppermute | solution.py:479
  16.1 5.9 %own_codes.2.refs_4_ = f32[1024,768]{1,0:T(8,128)} custom-call(s32[1]{0:T(128)} %bitcast.refs_0_.me_ref, bf16[1536,768]{1,0:T(8,128)(2,1)} %refs_2_.6, s32[2,1536]{1,0:T(2,128)} %refs_3_.3, s32[4,8,896]{2,1,0:T(8,128)} %copy-done.4), custom_call_target="tpu_custom_call" | custom-call | flops 6000000000 | bytes 1000000 | tf_op jit(solution)/shard_map/own_codes/pallas_call | solution.py:570
  22.1 0.6 copy-done.7
  22.7 6.0 %own_codes.3.refs_5_ = f32[1024,768]{1,0:T(8,128)} custom-call(s32[1]{0:T(128)} %bitcast.refs_0_.me_ref, bf16[1536,768]{1,0:T(8,128)(2,1)} %refs_2_.6, s32[2,1536]{1,0:T(2,128)} %refs_3_.3, s32[8,8,896]{2,1,0:T(8,128)} %copy-done.7), custom_call_target="tpu_custom_call" | custom-call | flops 6000000000 | bytes 1000000 | tf_op jit(solution)/shard_map/own_codes/pallas_call | solution.py:570
  28.7 0.8 copy-done.8
  29.5 35.8 %sums.1 = (f32[8,160,256]{2,1,0:T(8,128)}, f32[4,160,256]{2,1,0:T(8,128)}, f32[4,160,256]{2,1,0:T(8,128)}, f32[8,160,256]{2,1,0:T(8,128)}, f32[4,160,256]{2,1,0:...) custom-call(s32[1]{0:T(128)} %bitcast.refs_0_.me_ref, ...), custom_call_target="tpu_custom_call" | custom-call | flops 40000000000 | bytes 1000000 | tf_op jit(solution)/shard_map/sums/pallas_call | solution.py:594
  66.5 2.1 %collective-permute-done = f32[8,1,2,768]{3,2,1,0:T(2,128)S(1)} collective-permute-done((f32[8,1,2,768]{3,2,1,0:T(2,128)S(1)}, f32[8,1,2,768]{3,2,1,0:T(2,128)S(1)}, u32[]{:S(2)}, u32[]{:S(2)}) %collective-permute-start) | collective-permute-done | bytes 49184 | tf_op jit(solution)/shard_map/ppermute | solution.py:479
  68.6 0.6 collective-permute-start.6
  69.2 3.5 %collective-permute-done.6 = f32[4,2,2,768]{3,2,1,0:T(2,128)S(1)} collective-permute-done((f32[4,2,2,768]{3,2,1,0:T(2,128)S(1)}, f32[4,2,2,768]{3,2,1,0:T(2,128)S(1)}, u32[]{:S(2)}, u32[]{:S(2)}) %collective-permute-start.6) | collective-permute-done | bytes 49184 | tf_op jit(solution)/shard_map/ppermute | solution.py:479
  72.8 1.6 %slice_add_fusion = (f32[4,160,256]{2,1,0:T(8,128)S(1)}, f32[4,160,256]{2,1,0:T(8,128)S(1)}) fusion(f32[4,160,256]{2,1,0:T(8,128)} %get-tuple-element.31, f32[8,160,256]{2,1,0:T(8,128)S(1)} %collective-permute-done.7, f32[4,160,256]{2,1,0:T(8,128)} %get-tuple-element.23), kind=kLoop, calls=%fused_computation | loop fusion | flops 327680 | bytes 3932160 | tf_op jit(solution)/shard_map/add | solution.py:501
  74.4 0.6 collective-permute-start.19
  75.0 3.7 %collective-permute-start.10 = (f32[4,2,768]{2,1,0:T(2,128)S(1)}, f32[4,2,768]{2,1,0:T(2,128)S(1)}, u32[]{:S(2)}, u32[]{:S(2)}) collective-permute-start(f32[4,2,768]{2,1,0:T(2,128)S(1)} %get-tuple-element.49), channel_id=1, source_target_pairs={{0,12},{1,13},{2,14},{3,15},{4,8},{5,9},{6,10},{7,11},{8,4},{9,5},... | collective-permute-start | bytes 73736 | tf_op jit(solution)/shard_map/ppermute | solution.py:479
  79.0 0.8 copy-done
  80.2 1.5 %collective-permute-start.12 = (f32[4,160,256]{2,1,0:T(8,128)S(1)}, f32[4,160,256]{2,1,0:T(8,128)S(1)}, u32[]{:S(2)}, u32[]{:S(2)}) collective-permute-start(f32[4,160,256]{2,1,0:T(8,128)S(1)} %get-tuple-element.45), channel_id=1, source_target_pairs={{0,2},{1,3},{2,0},{3,1},{4,6},{5,7},{6,4},{7,5},{8,10},{9,11},{10,... | collective-permute-start | bytes 1966088 | tf_op jit(solution)/shard_map/ppermute | solution.py:479
  81.7 1.0 collective-permute-start.8
  82.7 10.2 %collective-permute-done.9 = f32[4,2,768]{2,1,0:T(2,128)S(1)} collective-permute-done((f32[4,2,768]{2,1,0:T(2,128)S(1)}, f32[4,2,768]{2,1,0:T(2,128)S(1)}, u32[]{:S(2)}, u32[]{:S(2)}) %collective-permute-start.9) | collective-permute-done | bytes 24608 | tf_op jit(solution)/shard_map/ppermute | solution.py:479
  92.9 2.5 %collective-permute-done.8 = f32[4,2,768]{2,1,0:T(2,128)S(1)} collective-permute-done((f32[4,2,768]{2,1,0:T(2,128)S(1)}, f32[4,2,768]{2,1,0:T(2,128)S(1)}, u32[]{:S(2)}, u32[]{:S(2)}) %collective-permute-start.8) | collective-permute-done | bytes 24608 | tf_op jit(solution)/shard_map/ppermute | solution.py:479
  95.4 0.7 pad_maximum_fusion.2.refs_3_
  96.6 0.9 collective-permute-start.17
  97.5 6.6 %collective-permute-done.12 = f32[4,160,256]{2,1,0:T(8,128)S(1)} collective-permute-done((f32[4,160,256]{2,1,0:T(8,128)S(1)}, f32[4,160,256]{2,1,0:T(8,128)S(1)}, u32[]{:S(2)}, u32[]{:S(2)}) %collective-permute-start.12) | collective-permute-done | bytes 655392 | tf_op jit(solution)/shard_map/ppermute | solution.py:479
  104.2 1.3 collective-permute-start.13
  105.5 6.3 %collective-permute-done.20 = f32[2,160,256]{2,1,0:T(8,128)S(1)} collective-permute-done((f32[2,160,256]{2,1,0:T(8,128)S(1)}, f32[2,160,256]{2,1,0:T(8,128)S(1)}, u32[]{:S(2)}, u32[]{:S(2)}) %collective-permute-start.20) | collective-permute-done | bytes 327712 | tf_op jit(solution)/shard_map/ppermute | solution.py:479
  112.1 2.0 %collective-permute-start.18 = (f32[1,160,256]{2,1,0:T(8,128)S(1)}, f32[1,160,256]{2,1,0:T(8,128)S(1)}, u32[]{:S(2)}, u32[]{:S(2)}) collective-permute-start(f32[1,160,256]{2,1,0:T(8,128)S(1)} %slice_add_fusion.14), channel_id=1, source_target_pairs={{0,2},{1,3},{2,0},{3,1},{4,6},{5,7},{6,4},{7,5},{8,10},{9,11},{10,... | collective-permute-start | bytes 491528 | tf_op jit(solution)/shard_map/ppermute | solution.py:479
  114.1 7.0 %collective-permute-done.13 = f32[2,160,256]{2,1,0:T(8,128)S(1)} collective-permute-done((f32[2,160,256]{2,1,0:T(8,128)S(1)}, f32[2,160,256]{2,1,0:T(8,128)S(1)}, u32[]{:S(2)}, u32[]{:S(2)}) %collective-permute-start.13) | collective-permute-done | bytes 327712 | tf_op jit(solution)/shard_map/ppermute | solution.py:479
  121.2 0.7 fusion.1.refs_6_
  122.0 0.7 fusion.3.refs_5_
  122.7 6.9 %collective-permute-done.14 = f32[1,160,256]{2,1,0:T(8,128)S(1)} collective-permute-done((f32[1,160,256]{2,1,0:T(8,128)S(1)}, f32[1,160,256]{2,1,0:T(8,128)S(1)}, u32[]{:S(2)}, u32[]{:S(2)}) %collective-permute-start.14) | collective-permute-done | bytes 163872 | tf_op jit(solution)/shard_map/ppermute | solution.py:479
  129.6 0.7 fusion.5.refs_4_
  130.3 4.0 %outputs.1 = (f32[512,768]{1,0:T(8,128)}, f32[128,768]{1,0:T(8,128)}) custom-call(s32[1]{0:T(128)} %bitcast.refs_0_.me_ref, f32[512,768]{1,0:T(8,128)} %refs_1_.9, f32[2048,768]{1,0:T(8,128)} %refs_2_.7, f32[16,2,768]{2,1,0:T(2,128)} %pad_maximum_fusion.2.refs_3_, f32[160,256]{1,0:T(8,128)} %fusion.5.refs_4_, f32[160,256]{1,0:T(8,128)} %fusion.3.refs_5_, ...), custom_call_target="tpu_custom_call" | custom-call | flops 1000000000 | bytes 1000000 | tf_op jit(solution)/shard_map/outputs/pallas_call | solution.py:637
  (61 shorter events, 3.6 us)
Async XLA Ops:
  2.0 12.2 %copy-start.5 = (s32[8,896]{1,0:T(8,128)S(1)}, s32[8,896]{1,0:T(8,128)}, u32[]{:S(2)}) copy-start(s32[8,896]{1,0:T(8,128)} %pack.1) | copy-start | bytes 86020
  2.0 12.2 %collective-permute-start.3 = (s32[8,896]{1,0:T(8,128)}, s32[8,896]{1,0:T(8,128)S(1)}, u32[]{:S(2)}, u32[]{:S(2)}) collective-permute-start(s32[8,896]{1,0:T(8,128)} %pack.1), channel_id=1, source_target_pairs={{0,12},{1,13},{2,14},{3,15},{4,8},{5,9},{6,10},{7,11},{8,4},{9,5},... | collective-permute-start | bytes 86024 | tf_op jit(solution)/shard_map/ppermute | solution.py:479
  7.0 7.2 %collective-permute-start.2 = (s32[8,896]{1,0:T(8,128)}, s32[8,896]{1,0:T(8,128)S(1)}, u32[]{:S(2)}, u32[]{:S(2)}) collective-permute-start(s32[8,896]{1,0:T(8,128)} %pack.1), channel_id=1, source_target_pairs={{0,8},{1,9},{2,10},{3,11},{4,12},{5,13},{6,14},{7,15},{8,0},{9,1},... | collective-permute-start | bytes 86024 | tf_op jit(solution)/shard_map/ppermute | solution.py:479
  7.0 7.2 %collective-permute-start.1 = (s32[8,896]{1,0:T(8,128)}, s32[8,896]{1,0:T(8,128)S(1)}, u32[]{:S(2)}, u32[]{:S(2)}) collective-permute-start(s32[8,896]{1,0:T(8,128)} %pack.1), channel_id=1, source_target_pairs={{0,4},{1,5},{2,6},{3,7},{4,0},{5,1},{6,2},{7,3},{8,12},{9,13},{10,... | collective-permute-start | bytes 86024 | tf_op jit(solution)/shard_map/ppermute | solution.py:479
  14.2 1.8 %copy-start.4 = (s32[4,8,896]{2,1,0:T(8,128)}, s32[4,8,896]{2,1,0:T(8,128)S(1)}, u32[]{:S(2)}) copy-start(s32[4,8,896]{2,1,0:T(8,128)S(1)} %pad_add_fusion.refs_2_) | copy-start | bytes 344068
  14.3 7.8 %collective-permute-start.4 = (s32[4,8,896]{2,1,0:T(8,128)S(1)}, s32[4,8,896]{2,1,0:T(8,128)S(1)}, u32[]{:S(2)}, u32[]{:S(2)}) collective-permute-start(s32[4,8,896]{2,1,0:T(8,128)S(1)} %pad_add_fusion.refs_2_), channel_id=1, source_target_pairs={{0,2},{1,3},{2,0},{3,1},{4,6},{5,7},{6,4},{7,5},{8,10},{9,11},{10,... | collective-permute-start | bytes 344072 | tf_op jit(solution)/shard_map/ppermute | solution.py:479
  22.0 0.7 copy-start.7
  22.1 6.6 %collective-permute-start.5 = (s32[8,8,896]{2,1,0:T(8,128)S(1)}, s32[8,8,896]{2,1,0:T(8,128)S(1)}, u32[]{:S(2)}, u32[]{:S(2)}) collective-permute-start(s32[8,8,896]{2,1,0:T(8,128)S(1)} %get-tuple-element.46.refs_2_), channel_id=1, source_target_pairs={{0,1},{1,0},{2,3},{3,2},{4,5},{5,4},{6,7},{7,6},{8,9},{9,8},{10,11... | collective-permute-start | bytes 688136 | tf_op jit(solution)/shard_map/ppermute | solution.py:479
  28.7 0.8 copy-start.8
  29.5 36.4 %copy-start.6 = (f32[16,1,2,768]{3,2,1,0:T(2,128)S(1)}, f32[16,1,2,768]{3,2,1,0:T(2,128)}, u32[]{:S(2)}) copy-start(f32[16,1,2,768]{3,2,1,0:T(2,128)} %get-tuple-element.18) | copy-start | bytes 294916
  65.3 7.5 %collective-permute-start.7 = (f32[8,160,256]{2,1,0:T(8,128)}, f32[8,160,256]{2,1,0:T(8,128)S(1)}, u32[]{:S(2)}, u32[]{:S(2)}) collective-permute-start(f32[8,160,256]{2,1,0:T(8,128)} %get-tuple-element.24), channel_id=1, source_target_pairs={{0,1},{1,0},{2,3},{3,2},{4,5},{5,4},{6,7},{7,6},{8,9},{9,8},{10,11... | collective-permute-start | bytes 3932168 | tf_op jit(solution)/shard_map/ppermute | solution.py:479
  65.4 13.3 %collective-permute-start.15 = (f32[8,160,256]{2,1,0:T(8,128)}, f32[8,160,256]{2,1,0:T(8,128)S(1)}, u32[]{:S(2)}, u32[]{:S(2)}) collective-permute-start(f32[8,160,256]{2,1,0:T(8,128)} %get-tuple-element.29), channel_id=1, source_target_pairs={{0,1},{1,0},{2,3},{3,2},{4,5},{5,4},{6,7},{7,6},{8,9},{9,8},{10,11... | collective-permute-start | bytes 3932168 | tf_op jit(solution)/shard_map/ppermute | solution.py:479
  65.9 2.6 %collective-permute-start = (f32[8,1,2,768]{3,2,1,0:T(2,128)S(1)}, f32[8,1,2,768]{3,2,1,0:T(2,128)S(1)}, u32[]{:S(2)}, u32[]{:S(2)}) collective-permute-start(f32[8,1,2,768]{3,2,1,0:T(2,128)S(1)} %get-tuple-element.55), channel_id=1, source_target_pairs={{0,1},{1,0},{2,3},{3,2},{4,5},{5,4},{6,7},{7,6},{8,9},{9,8},{10,11... | collective-permute-start | bytes 147464 | tf_op jit(solution)/shard_map/ppermute | solution.py:479
  66.0 13.0 %collective-permute-start.11 = (f32[8,160,256]{2,1,0:T(8,128)}, f32[8,160,256]{2,1,0:T(8,128)S(1)}, u32[]{:S(2)}, u32[]{:S(2)}) collective-permute-start(f32[8,160,256]{2,1,0:T(8,128)} %get-tuple-element.21), channel_id=1, source_target_pairs={{0,1},{1,0},{2,3},{3,2},{4,5},{5,4},{6,7},{7,6},{8,9},{9,8},{10,11... | collective-permute-start | bytes 3932168 | tf_op jit(solution)/shard_map/ppermute | solution.py:479
  68.6 4.2 %collective-permute-start.6 = (f32[4,2,2,768]{3,2,1,0:T(2,128)S(1)}, f32[4,2,2,768]{3,2,1,0:T(2,128)S(1)}, u32[]{:S(2)}, u32[]{:S(2)}) collective-permute-start(f32[4,2,2,768]{3,2,1,0:T(2,128)S(1)} %get-tuple-element.53), channel_id=1, source_target_pairs={{0,2},{1,3},{2,0},{3,1},{4,6},{5,7},{6,4},{7,5},{8,10},{9,11},{10,... | collective-permute-start | bytes 147464 | tf_op jit(solution)/shard_map/ppermute | solution.py:479
  72.8 5.9 %copy-start.2 = (f32[4,160,256]{2,1,0:T(8,128)S(1)}, f32[4,160,256]{2,1,0:T(8,128)}, u32[]{:S(2)}) copy-start(f32[4,160,256]{2,1,0:T(8,128)} %get-tuple-element.30) | copy-start | bytes 1966084
  72.8 5.9 %copy-start.3 = (f32[4,160,256]{2,1,0:T(8,128)S(1)}, f32[4,160,256]{2,1,0:T(8,128)}, u32[]{:S(2)}) copy-start(f32[4,160,256]{2,1,0:T(8,128)} %get-tuple-element.28) | copy-start | bytes 1966084
  74.4 21.6 %collective-permute-start.19 = (f32[4,160,256]{2,1,0:T(8,128)S(1)}, f32[4,160,256]{2,1,0:T(8,128)S(1)}, u32[]{:S(2)}, u32[]{:S(2)}) collective-permute-start(f32[4,160,256]{2,1,0:T(8,128)S(1)} %get-tuple-element.37), channel_id=1, source_target_pairs={{0,2},{1,3},{2,0},{3,1},{4,6},{5,7},{6,4},{7,5},{8,10},{9,11},{10,... | collective-permute-start | bytes 1966088 | tf_op jit(solution)/shard_map/ppermute | solution.py:479
  75.0 6.7 %collective-permute-start.10 = (f32[4,2,768]{2,1,0:T(2,128)S(1)}, f32[4,2,768]{2,1,0:T(2,128)S(1)}, u32[]{:S(2)}, u32[]{:S(2)}) collective-permute-start(f32[4,2,768]{2,1,0:T(2,128)S(1)} %get-tuple-element.49), channel_id=1, source_target_pairs={{0,12},{1,13},{2,14},{3,15},{4,8},{5,9},{6,10},{7,11},{8,4},{9,5},... | collective-permute-start | bytes 73736 | tf_op jit(solution)/shard_map/ppermute | solution.py:479
  78.7 1.1 copy-start
  78.7 1.3 copy-start.1
  78.9 17.6 %collective-permute-start.16 = (f32[4,160,256]{2,1,0:T(8,128)S(1)}, f32[4,160,256]{2,1,0:T(8,128)S(1)}, u32[]{:S(2)}, u32[]{:S(2)}) collective-permute-start(f32[4,160,256]{2,1,0:T(8,128)S(1)} %get-tuple-element.41), channel_id=1, source_target_pairs={{0,4},{1,5},{2,6},{3,7},{4,0},{5,1},{6,2},{7,3},{8,12},{9,13},{10,... | collective-permute-start | bytes 1966088 | tf_op jit(solution)/shard_map/ppermute | solution.py:479
  80.2 24.0 %collective-permute-start.12 = (f32[4,160,256]{2,1,0:T(8,128)S(1)}, f32[4,160,256]{2,1,0:T(8,128)S(1)}, u32[]{:S(2)}, u32[]{:S(2)}) collective-permute-start(f32[4,160,256]{2,1,0:T(8,128)S(1)} %get-tuple-element.45), channel_id=1, source_target_pairs={{0,2},{1,3},{2,0},{3,1},{4,6},{5,7},{6,4},{7,5},{8,10},{9,11},{10,... | collective-permute-start | bytes 1966088 | tf_op jit(solution)/shard_map/ppermute | solution.py:479
  81.7 11.2 %collective-permute-start.9 = (f32[4,2,768]{2,1,0:T(2,128)S(1)}, f32[4,2,768]{2,1,0:T(2,128)S(1)}, u32[]{:S(2)}, u32[]{:S(2)}) collective-permute-start(f32[4,2,768]{2,1,0:T(2,128)S(1)} %get-tuple-element.50), channel_id=1, source_target_pairs={{0,8},{1,9},{2,10},{3,11},{4,12},{5,13},{6,14},{7,15},{8,0},{9,1},... | collective-permute-start | bytes 73736 | tf_op jit(solution)/shard_map/ppermute | solution.py:479
  81.7 13.6 %collective-permute-start.8 = (f32[4,2,768]{2,1,0:T(2,128)S(1)}, f32[4,2,768]{2,1,0:T(2,128)S(1)}, u32[]{:S(2)}, u32[]{:S(2)}) collective-permute-start(f32[4,2,768]{2,1,0:T(2,128)S(1)} %get-tuple-element.51), channel_id=1, source_target_pairs={{0,4},{1,5},{2,6},{3,7},{4,0},{5,1},{6,2},{7,3},{8,12},{9,13},{10,... | collective-permute-start | bytes 73736 | tf_op jit(solution)/shard_map/ppermute | solution.py:479
  96.1 15.7 %collective-permute-start.20 = (f32[2,160,256]{2,1,0:T(8,128)S(1)}, f32[2,160,256]{2,1,0:T(8,128)S(1)}, u32[]{:S(2)}, u32[]{:S(2)}) collective-permute-start(f32[2,160,256]{2,1,0:T(8,128)S(1)} %get-tuple-element.35), channel_id=1, source_target_pairs={{0,4},{1,5},{2,6},{3,7},{4,0},{5,1},{6,2},{7,3},{8,12},{9,13},{10,... | collective-permute-start | bytes 983048 | tf_op jit(solution)/shard_map/ppermute | solution.py:479
  96.6 15.5 %collective-permute-start.17 = (f32[2,160,256]{2,1,0:T(8,128)S(1)}, f32[2,160,256]{2,1,0:T(8,128)S(1)}, u32[]{:S(2)}, u32[]{:S(2)}) collective-permute-start(f32[2,160,256]{2,1,0:T(8,128)S(1)} %get-tuple-element.39), channel_id=1, source_target_pairs={{0,8},{1,9},{2,10},{3,11},{4,12},{5,13},{6,14},{7,15},{8,0},{9,1},... | collective-permute-start | bytes 983048 | tf_op jit(solution)/shard_map/ppermute | solution.py:479
  104.2 16.9 %collective-permute-start.13 = (f32[2,160,256]{2,1,0:T(8,128)S(1)}, f32[2,160,256]{2,1,0:T(8,128)S(1)}, u32[]{:S(2)}, u32[]{:S(2)}) collective-permute-start(f32[2,160,256]{2,1,0:T(8,128)S(1)} %get-tuple-element.43), channel_id=1, source_target_pairs={{0,4},{1,5},{2,6},{3,7},{4,0},{5,1},{6,2},{7,3},{8,12},{9,13},{10,... | collective-permute-start | bytes 983048 | tf_op jit(solution)/shard_map/ppermute | solution.py:479
  111.9 9.4 %collective-permute-start.21 = (f32[1,160,256]{2,1,0:T(8,128)S(1)}, f32[1,160,256]{2,1,0:T(8,128)S(1)}, u32[]{:S(2)}, u32[]{:S(2)}) collective-permute-start(f32[1,160,256]{2,1,0:T(8,128)S(1)} %slice_add_fusion.12), channel_id=1, source_target_pairs={{0,8},{1,9},{2,10},{3,11},{4,12},{5,13},{6,14},{7,15},{8,0},{9,1},... | collective-permute-start | bytes 491528 | tf_op jit(solution)/shard_map/ppermute | solution.py:479
  112.1 9.8 %collective-permute-start.18 = (f32[1,160,256]{2,1,0:T(8,128)S(1)}, f32[1,160,256]{2,1,0:T(8,128)S(1)}, u32[]{:S(2)}, u32[]{:S(2)}) collective-permute-start(f32[1,160,256]{2,1,0:T(8,128)S(1)} %slice_add_fusion.14), channel_id=1, source_target_pairs={{0,2},{1,3},{2,0},{3,1},{4,6},{5,7},{6,4},{7,5},{8,10},{9,11},{10,... | collective-permute-start | bytes 491528 | tf_op jit(solution)/shard_map/ppermute | solution.py:479
  121.2 8.4 %collective-permute-start.14 = (f32[1,160,256]{2,1,0:T(8,128)S(1)}, f32[1,160,256]{2,1,0:T(8,128)S(1)}, u32[]{:S(2)}, u32[]{:S(2)}) collective-permute-start(f32[1,160,256]{2,1,0:T(8,128)S(1)} %slice_add_fusion.16), channel_id=1, source_target_pairs={{0,8},{1,9},{2,10},{3,11},{4,12},{5,13},{6,14},{7,15},{8,0},{9,1},... | collective-permute-start | bytes 491528 | tf_op jit(solution)/shard_map/ppermute | solution.py:479

commit v2 on v1

--- a/solution.py
+++ b/solution.py
@@ -210,6 +210,7 @@
     first_ref,
     second_ref,
     share_ref,
+    _,
     *refs,
 ):
     out_refs, refs = refs[: 3 * len(cuts)], refs[3 * len(cuts) :]
@@ -238,7 +239,8 @@
     one, zero = jnp.ones((), BF16), jnp.zeros((), BF16)
 
     def hot(codes):
-        return jnp.where(rows_hot[...] == codes.astype(F32).astype(BF16), one, zero)
+        rows = rows_hot[:, : codes.shape[1]]
+        return jnp.where(rows == codes.astype(F32).astype(BF16), one, zero)
 
     def device_tables(device, carry):
         at = position(device ^ me, groups)
@@ -290,13 +292,14 @@
     )
     order = (natural == iota((entries, entries), 1)).astype(BF16)
     code_counts = [jnp.sum(table[...], axis=0, keepdims=True) for table in (table0, table1)]
-    entry_counts = []
-    for table in (table0, table1):
-        count_high, count_low = split(
-            jnp.broadcast_to(jnp.sum(table[...], axis=1, keepdims=True), (entries, LANES))
-        )
+    entry_counts, most = [], 0.0
+    for sweep, table in enumerate((table0, table1)):
+        entry_count = jnp.sum(table[...], axis=1, keepdims=True)
+        most = jnp.maximum(
+            most, jnp.minimum(jnp.max(entry_count), jnp.max(code_counts[sweep]))
+        )
+        count_high, count_low = split(jnp.broadcast_to(entry_count, (entries, LANES)))
         entry_counts.append(matmul(order, count_high) + matmul(order, count_low))
-    most = jnp.maximum(jnp.max(table0[...]), jnp.max(table1[...]))
     large = most > LOW
     for digit in range(high):
         columns = slice(digit * LOW, (digit + 1) * LOW)
@@ -314,15 +317,20 @@
     match = (names[0] == own_row).astype(BF16)
     match = lax.dot_general(match, order, (((0,), (0,)), ((), ())), preferred_element_type=F32)
     match = match.astype(BF16)
-    held = jnp.zeros((listed, 1), F32)
     for digit in range(high):
         columns = slice(digit * LOW, (digit + 1) * LOW)
-        table_high, table_low = split(table0[:, columns])
-        used = matmul(match, table_high) + matmul(match, table_low)
-        held = held + jnp.sum(used, axis=1, keepdims=True)
-        used_high, used_low = split(used)
-        wide[0:listed, columns] = used_high.astype(F32)
-        wide[listed : 2 * listed, columns] = used_low.astype(F32)
+        wide[0:listed, columns] = matmul(match, table0[:, columns].astype(BF16))
+
+    @pl.when(large)
+    def _():
+        for digit in range(high):
+            columns = slice(digit * LOW, (digit + 1) * LOW)
+            wide[0:listed, columns] += matmul(match, split(table0[:, columns])[1])
+
+    held = jnp.sum(wide[0:listed, :], axis=1, keepdims=True)
+    used_high, used_low = split(wide[0:listed, :])
+    wide[0:listed, :] = used_high.astype(F32)
+    wide[listed : 2 * listed, :] = used_low.astype(F32)
     wide[2 * listed : 2 * listed + 8, :] = jnp.broadcast_to(code_counts[0], (8, codewords))
     wide[2 * listed + 8 : 2 * listed + 16, :] = jnp.broadcast_to(code_counts[1], (8, codewords))
     wide[2 * listed + 16 :, :] = jnp.zeros((LANES - 2 * listed - 16, codewords), F32)
@@ -338,7 +346,7 @@
         code_info_ref[rows, :] = columns
         taken = jnp.where(iota((LOW, LANES), 1) < 2 * listed, columns, 0.0).astype(BF16)
         first_fine = fine[rows, :] - (matmul(taken, center_high) + matmul(taken, center_low))
-        scaled = first_fine / jnp.maximum(columns[:, 2 * listed : 2 * listed + 1], 1.0)
+        scaled = first_fine * (1.0 / jnp.maximum(columns[:, 2 * listed : 2 * listed + 1], 1.0))
         terms[0, rows, :], terms[1, rows, :] = split(scaled)
         fine[rows, :] = jnp.where(
             columns[:, 2 * listed + 8 : 2 * listed + 9] > 0, 0.0, first_fine
@@ -371,7 +379,7 @@
     totals = matmul(same, total_high) + matmul(same, total_low)
     bracket_high, bracket_low = split(bracket[...])
     centers = matmul(same, bracket_high) + matmul(same, bracket_low)
-    centers = centers / jnp.maximum(totals[:, :1], 1.0)
+    centers = centers * (1.0 / jnp.maximum(totals[:, :1], 1.0))
     centers_ref[0], centers_ref[1] = split(centers)
     lane = iota((entries, LANES), 1)
     info = jnp.where(lane == 0, entry_counts[0], entry_counts[1])
@@ -391,7 +399,9 @@
             owner = me ^ block
             rows = pl.ds(pl.multiple_of(owner * share_rows, share_rows), share_rows)
             to = slice(at * share_rows, (at + 1) * share_rows)
-            left[to, :rows_here] = hot_rows(codes - owner * share_rows, share_rows)
+            own = codes - owner * share_rows
+            own = jnp.where((own >= 0) & (own < share_rows), own, -1)
+            left[to, :rows_here] = hot(own)[:share_rows]
             left[to, rows_here:] = pairs_ref[rows, :]
         start = 0
         for chunk, cut in enumerate(cuts):
@@ -457,7 +467,8 @@
     last_count = code_info[:, 2 * listed + 8 : 2 * listed + 9]
     count = jnp.where(last_count > 0, last_count, first_count)
     start = 0
-    for cut, last_sums in zip(cuts, last_refs):
+    for cut, kept, got in zip(cuts, last_refs[::2], last_refs[1::2]):
+        last_sums = kept[0] + got[0]
         columns = slice(start, start + cut)
         start += cut
         coarse = coarse_in[:, columns]
@@ -576,9 +587,8 @@
             6e9,
             "own_codes",
         )(me, vectors, fine_codes, gathered)
+        first_to = swap(after(first_to, gathered), 2 - step)
         gathered = jnp.concatenate([gathered, exchange(gathered, step)])
-        if step == 2:
-            first_to = swap(first_to, 0)
 
     top = groups.bit_length() - 1
     near_first = list(range(1, top))
@@ -595,7 +605,7 @@
         lambda *refs: sums_kernel(groups, slot_count, owner_cells, cuts, orders, *refs),
         [(shape, F32) for shape in shapes]
         + [((codewords, LANES), F32), ((entries, LANES), F32)],
-        [VMEM] * 3 + [ANY] * 2 + [VMEM] * 2 + [block((share_rows, feature), None, 0)],
+        [VMEM] * 3 + [ANY] * 2 + [VMEM] * 2 + [block((share_rows, feature), None, 0), ANY],
         [ANY] * len(shapes) + [VMEM] * 2,
         [
             pltpu.VMEM((entries, codewords), F32),
@@ -605,7 +615,7 @@
             pltpu.VMEM((LANES, codewords), F32),
             pltpu.VMEM((2, codewords, feature), BF16),
             pltpu.VMEM((2, entries, codewords), BF16),
-            pltpu.VMEM((LOW, half), BF16),
+            pltpu.VMEM((LOW, rows_here), BF16),
             pltpu.VMEM((codewords, feature), F32),
             pltpu.VMEM((entries, feature), F32),
             pltpu.VMEM((2, entries, feature), BF16),
@@ -617,9 +627,8 @@
         + [pltpu.VMEM(shape, F32) for shape in shapes],
         40e9,
         "sums",
-    )(me, gathered, vectors, fine_codes, *sums, first, second, fine_in)
-
-    first_to = swap(after(first_to, terms[0]), 1)
+    )(me, gathered, vectors, fine_codes, *sums, first, second, fine_in, first_to)
+
     finished = []
     for at, steps in enumerate(bits):
         away, other, kept = terms[3 * at : 3 * at + 3]
@@ -633,12 +642,12 @@
             got = exchange(other, 1 << bit)
             half = got.shape[0] // 2
             other, kept = halved(got, kept[:half], kept[half:])
-        finished.append((kept + exchange(other, 1 << steps[-1]))[0])
+        finished += [kept, exchange(other, 1 << steps[-1])]
     return local(
         lambda *refs: final_kernel(groups, slot_count, share_rows, cuts, *refs),
         [(coarse_in.shape, F32), ((share_rows, feature), F32)],
         [VMEM, block((share_rows, feature), None, 0)]
-        + [VMEM] * (1 + len(cuts))
+        + [VMEM] * (1 + 2 * len(cuts))
         + [block((share_rows, LANES), None, 0), block((listed, LANES), None, 0)],
         [VMEM] * 2,
         [pltpu.VMEM((listed, feature), F32)],

time: 135 us -> 143 us (1.059)
  starting transfers between devices: 21 us -> 26 us
  waiting for transfers between devices: 45.2 us -> 49 us
    ppermute x22, starting transfers between devices: 21 us -> 26 us  [exchange(): lax.ppermute(values, 'cell', [(at, at ^ step) for at in range(groups)])]
    ppermute x22, waiting for transfers between devices: 45.2 us -> 49 us  [exchange(): lax.ppermute(values, 'cell', [(at, at ^ step) for at in range(groups)])]
    squeeze x3 -> x0, other arithmetic: 2.12 us -> none  [dense_plan(): finished.append((kept + exchange(other, 1 << steps[-1]))[0])]
    add x9, other arithmetic: 2.22 us -> 4.28 us  [halved(): return (other + got[:half], kept + got[half:])]
  transfers between devices with their start and end apart: 22 -> 22, of which waited for: 8 -> 8; matrix products, arithmetic and copies ran while one was open for 3% -> 4% of each run, Pallas kernels for 14% -> 13%
where the time goes in v2:
time: 143 us
  Pallas kernels  59.3 us (41%)
  waiting for transfers between devices  49 us (34%)
  starting transfers between devices  26 us (18%)
  other arithmetic  5.7 us (4%)
  local copies, waits for them, and re-layouts  2.15 us (2%)
    ppermute x22, waiting for transfers between devices, exchange(): lax.ppermute(values, 'cell', [(at, at ^ step) for at in range(groups)])  49 us
    pallas_call x1, Pallas kernels, dense_plan(): local(lambda *refs: sums_kernel(groups, slot_count, owner_cells, cuts, or...  35.4 us
    ppermute x22, starting transfers between devices, exchange(): lax.ppermute(values, 'cell', [(at, at ^ step) for at in range(groups)])  26 us
    pallas_call x2, Pallas kernels, dense_plan(): local(lambda me_ref, *refs, base=base: own_codes_kernel(base, *refs), [((...  11.8 us
    pallas_call x1, Pallas kernels, dense_plan(): local(lambda *refs: own_cells_kernel(groups, listed, *refs), [((listed, f...  6.58 us
    add x9, other arithmetic, halved(): return (other + got[:half], kept + got[half:])  4.28 us
    pallas_call x1, Pallas kernels, dense_plan(): local(lambda *refs: final_kernel(groups, slot_count, share_rows, cuts, *r...  4.16 us
  transfers between devices with their start and end apart: 22, of which 8 were waited for; matrix products, arithmetic and copies ran while one was open for 4% of the time, Pallas kernels for 13%

profile of v2, /device:TPU:0, one launch (start us, length us, event | category | flops | bytes accessed | tf_op | source)
XLA Modules:
  0.0 143.1 jit_solution(14626443868071238865)
XLA Ops:
  0.6 1.3 pack.1
  2.0 5.0 %collective-permute-start.2 = (s32[8,896]{1,0:T(8,128)}, s32[8,896]{1,0:T(8,128)S(1)}, u32[]{:S(2)}, u32[]{:S(2)}) collective-permute-start(s32[8,896]{1,0:T(8,128)} %pack.1), channel_id=1, source_target_pairs={{0,12},{1,13},{2,14},{3,15},{4,8},{5,9},{6,10},{7,11},{8,4},{9,5},... | collective-permute-start | bytes 86024 | tf_op jit(solution)/shard_map/ppermute | solution.py:490
  7.6 6.6 %own_cells.1 = (f32[32,768]{1,0:T(8,128)}, f32[32,768]{1,0:T(8,128)}, f32[16,1,2,768]{3,2,1,0:T(2,128)}) custom-call(s32[1]{0:T(128)} %bitcast.refs_0_.me_ref, bf16[1536,768]{1,0:T(8,128)(2,1)} %refs_2_.6, s32[2,1536]{1,0:T(2,128)} %refs_3_.3, s32[2,1536]{1,0:T(2,128)} %refs_1_.6, f32[2048,768]{1,0:T(8,128)} %refs_2_.7), custom_call_target="tpu_custom_call" | custom-call | flops 5000000000 | bytes 1000000 | tf_op jit(solution)/shard_map/own_cells/pallas_call | solution.py:568
  14.3 1.8 %collective-permute-start.4 = (s32[4,8,896]{2,1,0:T(8,128)S(1)}, s32[4,8,896]{2,1,0:T(8,128)S(1)}, u32[]{:S(2)}, u32[]{:S(2)}) collective-permute-start(s32[4,8,896]{2,1,0:T(8,128)S(1)} %pad_add_fusion.refs_2_), channel_id=1, source_target_pairs={{0,2},{1,3},{2,0},{3,1},{4,6},{5,7},{6,4},{7,5},{8,10},{9,11},{10,... | collective-permute-start | bytes 344072 | tf_op jit(solution)/shard_map/ppermute | solution.py:490
  16.1 5.9 %own_codes.2.refs_4_ = f32[1024,768]{1,0:T(8,128)} custom-call(s32[1]{0:T(128)} %bitcast.refs_0_.me_ref, bf16[1536,768]{1,0:T(8,128)(2,1)} %refs_2_.6, s32[2,1536]{1,0:T(2,128)} %refs_3_.3, s32[4,8,896]{2,1,0:T(8,128)} %copy-done.8), custom_call_target="tpu_custom_call" | custom-call | flops 6000000000 | bytes 1000000 | tf_op jit(solution)/shard_map/own_codes/pallas_call | solution.py:581
  22.1 1.2 collective-permute-done.3
  24.2 5.9 %own_codes.3.refs_5_ = f32[1024,768]{1,0:T(8,128)} custom-call(s32[1]{0:T(128)} %bitcast.refs_0_.me_ref, bf16[1536,768]{1,0:T(8,128)(2,1)} %refs_2_.6, s32[2,1536]{1,0:T(2,128)} %refs_3_.3, s32[8,8,896]{2,1,0:T(8,128)} %copy-done.11), custom_call_target="tpu_custom_call" | custom-call | flops 6000000000 | bytes 1000000 | tf_op jit(solution)/shard_map/own_codes/pallas_call | solution.py:581
  30.2 0.7 pad_maximum_fusion.1.refs_9_
  30.9 0.8 copy-done.12
  31.7 35.4 %sums.1 = (f32[8,160,256]{2,1,0:T(8,128)}, f32[4,160,256]{2,1,0:T(8,128)}, f32[4,160,256]{2,1,0:T(8,128)}, f32[8,160,256]{2,1,0:T(8,128)}, f32[4,160,256]{2,1,0:...) custom-call(s32[1]{0:T(128)} %bitcast.refs_0_.me_ref, ...), custom_call_target="tpu_custom_call" | custom-call | flops 40000000000 | bytes 1000000 | tf_op jit(solution)/shard_map/sums/pallas_call | solution.py:604
  67.7 2.7 %collective-permute-done.7 = f32[8,160,256]{2,1,0:T(8,128)S(1)} collective-permute-done((f32[8,160,256]{2,1,0:T(8,128)}, f32[8,160,256]{2,1,0:T(8,128)S(1)}, u32[]{:S(2)}, u32[]{:S(2)}) %collective-permute-start.7) | collective-permute-done | bytes 1310752 | tf_op jit(solution)/shard_map/ppermute | solution.py:490
  70.4 1.6 %slice_add_fusion = (f32[4,160,256]{2,1,0:T(8,128)S(1)}, f32[4,160,256]{2,1,0:T(8,128)S(1)}) fusion(f32[4,160,256]{2,1,0:T(8,128)} %get-tuple-element.33, f32[8,160,256]{2,1,0:T(8,128)S(1)} %collective-permute-done.7, f32[4,160,256]{2,1,0:T(8,128)} %get-tuple-element.24), kind=kLoop, calls=%fused_computation | loop fusion | flops 327680 | bytes 3932160 | tf_op jit(solution)/shard_map/add | solution.py:512
  72.0 1.5 %collective-permute-start.19 = (f32[4,160,256]{2,1,0:T(8,128)S(1)}, f32[4,160,256]{2,1,0:T(8,128)S(1)}, u32[]{:S(2)}, u32[]{:S(2)}) collective-permute-start(f32[4,160,256]{2,1,0:T(8,128)S(1)} %get-tuple-element.39), channel_id=1, source_target_pairs={{0,2},{1,3},{2,0},{3,1},{4,6},{5,7},{6,4},{7,5},{8,10},{9,11},{10,... | collective-permute-start | bytes 1966088 | tf_op jit(solution)/shard_map/ppermute | solution.py:490
  73.7 0.6 collective-permute-start.12
  75.0 1.3 collective-permute-start.16
  76.3 3.1 %collective-permute-start.10 = (f32[4,2,768]{2,1,0:T(2,128)S(1)}, f32[4,2,768]{2,1,0:T(2,128)S(1)}, u32[]{:S(2)}, u32[]{:S(2)}) collective-permute-start(f32[4,2,768]{2,1,0:T(2,128)S(1)} %get-tuple-element.57), channel_id=1, source_target_pairs={{0,12},{1,13},{2,14},{3,15},{4,8},{5,9},{6,10},{7,11},{8,4},{9,5},... | collective-permute-start | bytes 73736 | tf_op jit(solution)/shard_map/ppermute | solution.py:490
  79.4 10.2 %collective-permute-done.19 = f32[4,160,256]{2,1,0:T(8,128)S(1)} collective-permute-done((f32[4,160,256]{2,1,0:T(8,128)S(1)}, f32[4,160,256]{2,1,0:T(8,128)S(1)}, u32[]{:S(2)}, u32[]{:S(2)}) %collective-permute-start.19) | collective-permute-done | bytes 655392 | tf_op jit(solution)/shard_map/ppermute | solution.py:490
  89.7 1.3 collective-permute-start.20
  91.0 11.8 %collective-permute-done.12 = f32[4,160,256]{2,1,0:T(8,128)S(1)} collective-permute-done((f32[4,160,256]{2,1,0:T(8,128)S(1)}, f32[4,160,256]{2,1,0:T(8,128)S(1)}, u32[]{:S(2)}, u32[]{:S(2)}) %collective-permute-start.12) | collective-permute-done | bytes 655392 | tf_op jit(solution)/shard_map/ppermute | solution.py:490
  102.9 1.3 collective-permute-start.13
  104.3 3.0 %collective-permute-start.17 = (f32[2,160,256]{2,1,0:T(8,128)S(1)}, f32[2,160,256]{2,1,0:T(8,128)S(1)}, u32[]{:S(2)}, u32[]{:S(2)}) collective-permute-start(f32[2,160,256]{2,1,0:T(8,128)S(1)} %get-tuple-element.41), channel_id=1, source_target_pairs={{0,8},{1,9},{2,10},{3,11},{4,12},{5,13},{6,14},{7,15},{8,0},{9,1},... | collective-permute-start | bytes 983048 | tf_op jit(solution)/shard_map/ppermute | solution.py:490
  107.3 0.7 slice_add_fusion.12
  108.1 10.5 %collective-permute-done.13 = f32[2,160,256]{2,1,0:T(8,128)S(1)} collective-permute-done((f32[2,160,256]{2,1,0:T(8,128)S(1)}, f32[2,160,256]{2,1,0:T(8,128)S(1)}, u32[]{:S(2)}, u32[]{:S(2)}) %collective-permute-start.13) | collective-permute-done | bytes 327712 | tf_op jit(solution)/shard_map/ppermute | solution.py:490
  118.6 0.7 slice_add_fusion.16
  119.7 10.5 %collective-permute-done.17 = f32[2,160,256]{2,1,0:T(8,128)S(1)} collective-permute-done((f32[2,160,256]{2,1,0:T(8,128)S(1)}, f32[2,160,256]{2,1,0:T(8,128)S(1)}, u32[]{:S(2)}, u32[]{:S(2)}) %collective-permute-start.17) | collective-permute-done | bytes 327712 | tf_op jit(solution)/shard_map/ppermute | solution.py:490
  130.3 0.7 slice_add_fusion.14
  131.0 1.5 %collective-permute-start.18 = (f32[1,160,256]{2,1,0:T(8,128)S(1)}, f32[1,160,256]{2,1,0:T(8,128)S(1)}, u32[]{:S(2)}, u32[]{:S(2)}) collective-permute-start(f32[1,160,256]{2,1,0:T(8,128)S(1)} %get-tuple-element.50), channel_id=1, source_target_pairs={{0,2},{1,3},{2,0},{3,1},{4,6},{5,7},{6,4},{7,5},{8,10},{9,11},{10,... | collective-permute-start | bytes 491528 | tf_op jit(solution)/shard_map/ppermute | solution.py:490
  132.4 2.9 %collective-permute-start.8 = (f32[4,2,768]{2,1,0:T(2,128)S(1)}, f32[4,2,768]{2,1,0:T(2,128)S(1)}, u32[]{:S(2)}, u32[]{:S(2)}) collective-permute-start(f32[4,2,768]{2,1,0:T(2,128)S(1)} %get-tuple-element.59), channel_id=1, source_target_pairs={{0,4},{1,5},{2,6},{3,7},{4,0},{5,1},{6,2},{7,3},{8,12},{9,13},{10,... | collective-permute-start | bytes 73736 | tf_op jit(solution)/shard_map/ppermute | solution.py:490
  135.4 1.8 %collective-permute-done.9 = f32[4,2,768]{2,1,0:T(2,128)S(1)} collective-permute-done((f32[4,2,768]{2,1,0:T(2,128)S(1)}, f32[4,2,768]{2,1,0:T(2,128)S(1)}, u32[]{:S(2)}, u32[]{:S(2)}) %collective-permute-start.9) | collective-permute-done | bytes 24608 | tf_op jit(solution)/shard_map/ppermute | solution.py:490
  137.4 0.7 pad_maximum_fusion.2.refs_3_
  138.1 0.6 copy-done.5
  138.9 4.2 %outputs.1 = (f32[512,768]{1,0:T(8,128)}, f32[128,768]{1,0:T(8,128)}) custom-call(s32[1]{0:T(128)} %bitcast.refs_0_.me_ref, f32[512,768]{1,0:T(8,128)} %refs_1_.9, f32[2048,768]{1,0:T(8,128)} %refs_2_.7, f32[16,2,768]{2,1,0:T(2,128)} %pad_maximum_fusion.2.refs_3_, f32[1,160,256]{2,1,0:T(8,128)} %get-tuple-element.53.refs_4_, f32[1,160,256]{2,1,0:T(8,128)} %copy-done.6, ...), custom_call_target="tpu_custom_call" | custom-call | flops 1000000000 | bytes 1000000 | tf_op jit(solution)/shard_map/outputs/pallas_call | solution.py:646
  (66 shorter events, 4.3 us)
Async XLA Ops:
  2.0 12.2 %copy-start.9 = (s32[8,896]{1,0:T(8,128)S(1)}, s32[8,896]{1,0:T(8,128)}, u32[]{:S(2)}) copy-start(s32[8,896]{1,0:T(8,128)} %pack.1) | copy-start | bytes 86020
  2.0 12.2 %collective-permute-start.2 = (s32[8,896]{1,0:T(8,128)}, s32[8,896]{1,0:T(8,128)S(1)}, u32[]{:S(2)}, u32[]{:S(2)}) collective-permute-start(s32[8,896]{1,0:T(8,128)} %pack.1), channel_id=1, source_target_pairs={{0,12},{1,13},{2,14},{3,15},{4,8},{5,9},{6,10},{7,11},{8,4},{9,5},... | collective-permute-start | bytes 86024 | tf_op jit(solution)/shard_map/ppermute | solution.py:490
  7.0 7.2 %collective-permute-start.1 = (s32[8,896]{1,0:T(8,128)}, s32[8,896]{1,0:T(8,128)S(1)}, u32[]{:S(2)}, u32[]{:S(2)}) collective-permute-start(s32[8,896]{1,0:T(8,128)} %pack.1), channel_id=1, source_target_pairs={{0,8},{1,9},{2,10},{3,11},{4,12},{5,13},{6,14},{7,15},{8,0},{9,1},... | collective-permute-start | bytes 86024 | tf_op jit(solution)/shard_map/ppermute | solution.py:490
  7.0 7.2 %collective-permute-start = (s32[8,896]{1,0:T(8,128)}, s32[8,896]{1,0:T(8,128)S(1)}, u32[]{:S(2)}, u32[]{:S(2)}) collective-permute-start(s32[8,896]{1,0:T(8,128)} %pack.1), channel_id=1, source_target_pairs={{0,4},{1,5},{2,6},{3,7},{4,0},{5,1},{6,2},{7,3},{8,12},{9,13},{10,... | collective-permute-start | bytes 86024 | tf_op jit(solution)/shard_map/ppermute | solution.py:490
  14.2 1.8 %copy-start.8 = (s32[4,8,896]{2,1,0:T(8,128)}, s32[4,8,896]{2,1,0:T(8,128)S(1)}, u32[]{:S(2)}) copy-start(s32[4,8,896]{2,1,0:T(8,128)S(1)} %pad_add_fusion.refs_2_) | copy-start | bytes 344068
  14.2 7.7 %copy-start.10 = (f32[16,1,2,768]{3,2,1,0:T(2,128)S(1)}, f32[16,1,2,768]{3,2,1,0:T(2,128)}, u32[]{:S(2)}) copy-start(f32[16,1,2,768]{3,2,1,0:T(2,128)} %get-tuple-element.20) | copy-start | bytes 294916
  14.3 9.1 %collective-permute-start.4 = (s32[4,8,896]{2,1,0:T(8,128)S(1)}, s32[4,8,896]{2,1,0:T(8,128)S(1)}, u32[]{:S(2)}, u32[]{:S(2)}) collective-permute-start(s32[4,8,896]{2,1,0:T(8,128)S(1)} %pad_add_fusion.refs_2_), channel_id=1, source_target_pairs={{0,2},{1,3},{2,0},{3,1},{4,6},{5,7},{6,4},{7,5},{8,10},{9,11},{10,... | collective-permute-start | bytes 344072 | tf_op jit(solution)/shard_map/ppermute | solution.py:490
  22.0 1.3 collective-permute-start.3
  23.4 0.9 copy-start.11
  23.4 7.5 %collective-permute-start.6 = (s32[8,8,896]{2,1,0:T(8,128)S(1)}, s32[8,8,896]{2,1,0:T(8,128)S(1)}, u32[]{:S(2)}, u32[]{:S(2)}) collective-permute-start(s32[8,8,896]{2,1,0:T(8,128)S(1)} %get-tuple-element.55.refs_2_), channel_id=1, source_target_pairs={{0,1},{1,0},{2,3},{3,2},{4,5},{5,4},{6,7},{7,6},{8,9},{9,8},{10,11... | collective-permute-start | bytes 688136 | tf_op jit(solution)/shard_map/ppermute | solution.py:490
  23.6 6.6 %collective-permute-start.5 = (f32[4,2,2,768]{3,2,1,0:T(2,128)S(1)}, f32[4,2,2,768]{3,2,1,0:T(2,128)S(1)}, u32[]{:S(2)}, u32[]{:S(2)}) collective-permute-start(f32[4,2,2,768]{3,2,1,0:T(2,128)S(1)} %get-tuple-element.61), channel_id=1, source_target_pairs={{0,2},{1,3},{2,0},{3,1},{4,6},{5,7},{6,4},{7,5},{8,10},{9,11},{10,... | collective-permute-start | bytes 147464 | tf_op jit(solution)/shard_map/ppermute | solution.py:490
  30.9 0.8 copy-start.12
  67.1 3.3 %collective-permute-start.7 = (f32[8,160,256]{2,1,0:T(8,128)}, f32[8,160,256]{2,1,0:T(8,128)S(1)}, u32[]{:S(2)}, u32[]{:S(2)}) collective-permute-start(f32[8,160,256]{2,1,0:T(8,128)} %get-tuple-element.25), channel_id=1, source_target_pairs={{0,1},{1,0},{2,3},{3,2},{4,5},{5,4},{6,7},{7,6},{8,9},{9,8},{10,11... | collective-permute-start | bytes 3932168 | tf_op jit(solution)/shard_map/ppermute | solution.py:490
  67.2 6.3 %collective-permute-start.11 = (f32[8,160,256]{2,1,0:T(8,128)}, f32[8,160,256]{2,1,0:T(8,128)S(1)}, u32[]{:S(2)}, u32[]{:S(2)}) collective-permute-start(f32[8,160,256]{2,1,0:T(8,128)} %get-tuple-element.28), channel_id=1, source_target_pairs={{0,1},{1,0},{2,3},{3,2},{4,5},{5,4},{6,7},{7,6},{8,9},{9,8},{10,11... | collective-permute-start | bytes 3932168 | tf_op jit(solution)/shard_map/ppermute | solution.py:490
  67.7 6.7 %collective-permute-start.15 = (f32[8,160,256]{2,1,0:T(8,128)}, f32[8,160,256]{2,1,0:T(8,128)S(1)}, u32[]{:S(2)}, u32[]{:S(2)}) collective-permute-start(f32[8,160,256]{2,1,0:T(8,128)} %get-tuple-element.31), channel_id=1, source_target_pairs={{0,1},{1,0},{2,3},{3,2},{4,5},{5,4},{6,7},{7,6},{8,9},{9,8},{10,11... | collective-permute-start | bytes 3932168 | tf_op jit(solution)/shard_map/ppermute | solution.py:490
  70.4 3.1 %copy-start.2 = (f32[4,160,256]{2,1,0:T(8,128)S(1)}, f32[4,160,256]{2,1,0:T(8,128)}, u32[]{:S(2)}) copy-start(f32[4,160,256]{2,1,0:T(8,128)} %get-tuple-element.29) | copy-start | bytes 1966084
  70.4 3.1 %copy-start.3 = (f32[4,160,256]{2,1,0:T(8,128)S(1)}, f32[4,160,256]{2,1,0:T(8,128)}, u32[]{:S(2)}) copy-start(f32[4,160,256]{2,1,0:T(8,128)} %get-tuple-element.27) | copy-start | bytes 1966084
  72.0 17.6 %collective-permute-start.19 = (f32[4,160,256]{2,1,0:T(8,128)S(1)}, f32[4,160,256]{2,1,0:T(8,128)S(1)}, u32[]{:S(2)}, u32[]{:S(2)}) collective-permute-start(f32[4,160,256]{2,1,0:T(8,128)S(1)} %get-tuple-element.39), channel_id=1, source_target_pairs={{0,2},{1,3},{2,0},{3,1},{4,6},{5,7},{6,4},{7,5},{8,10},{9,11},{10,... | collective-permute-start | bytes 1966088 | tf_op jit(solution)/shard_map/ppermute | solution.py:490
  73.5 1.1 copy-start
  73.5 1.3 copy-start.1
  73.7 29.1 %collective-permute-start.12 = (f32[4,160,256]{2,1,0:T(8,128)S(1)}, f32[4,160,256]{2,1,0:T(8,128)S(1)}, u32[]{:S(2)}, u32[]{:S(2)}) collective-permute-start(f32[4,160,256]{2,1,0:T(8,128)S(1)} %get-tuple-element.47), channel_id=1, source_target_pairs={{0,2},{1,3},{2,0},{3,1},{4,6},{5,7},{6,4},{7,5},{8,10},{9,11},{10,... | collective-permute-start | bytes 1966088 | tf_op jit(solution)/shard_map/ppermute | solution.py:490
  74.8 1.5 %copy-start.4 = (f32[4,4,2,768]{3,2,1,0:T(2,128)S(1)}, f32[4,4,2,768]{3,2,1,0:T(2,128)}, u32[]{:S(2)}) copy-start(f32[4,4,2,768]{3,2,1,0:T(2,128)} %pad_maximum_fusion.1.refs_9_) | copy-start | bytes 294916
  75.0 29.3 %collective-permute-start.16 = (f32[4,160,256]{2,1,0:T(8,128)S(1)}, f32[4,160,256]{2,1,0:T(8,128)S(1)}, u32[]{:S(2)}, u32[]{:S(2)}) collective-permute-start(f32[4,160,256]{2,1,0:T(8,128)S(1)} %get-tuple-element.43), channel_id=1, source_target_pairs={{0,4},{1,5},{2,6},{3,7},{4,0},{5,1},{6,2},{7,3},{8,12},{9,13},{10,... | collective-permute-start | bytes 1966088 | tf_op jit(solution)/shard_map/ppermute | solution.py:490
  76.3 56.1 %collective-permute-start.10 = (f32[4,2,768]{2,1,0:T(2,128)S(1)}, f32[4,2,768]{2,1,0:T(2,128)S(1)}, u32[]{:S(2)}, u32[]{:S(2)}) collective-permute-start(f32[4,2,768]{2,1,0:T(2,128)S(1)} %get-tuple-element.57), channel_id=1, source_target_pairs={{0,12},{1,13},{2,14},{3,15},{4,8},{5,9},{6,10},{7,11},{8,4},{9,5},... | collective-permute-start | bytes 73736 | tf_op jit(solution)/shard_map/ppermute | solution.py:490
  89.7 17.6 %collective-permute-start.20 = (f32[2,160,256]{2,1,0:T(8,128)S(1)}, f32[2,160,256]{2,1,0:T(8,128)S(1)}, u32[]{:S(2)}, u32[]{:S(2)}) collective-permute-start(f32[2,160,256]{2,1,0:T(8,128)S(1)} %get-tuple-element.37), channel_id=1, source_target_pairs={{0,4},{1,5},{2,6},{3,7},{4,0},{5,1},{6,2},{7,3},{8,12},{9,13},{10,... | collective-permute-start | bytes 983048 | tf_op jit(solution)/shard_map/ppermute | solution.py:490
  102.9 15.6 %collective-permute-start.13 = (f32[2,160,256]{2,1,0:T(8,128)S(1)}, f32[2,160,256]{2,1,0:T(8,128)S(1)}, u32[]{:S(2)}, u32[]{:S(2)}) collective-permute-start(f32[2,160,256]{2,1,0:T(8,128)S(1)} %get-tuple-element.45), channel_id=1, source_target_pairs={{0,4},{1,5},{2,6},{3,7},{4,0},{5,1},{6,2},{7,3},{8,12},{9,13},{10,... | collective-permute-start | bytes 983048 | tf_op jit(solution)/shard_map/ppermute | solution.py:490
  104.3 25.9 %collective-permute-start.17 = (f32[2,160,256]{2,1,0:T(8,128)S(1)}, f32[2,160,256]{2,1,0:T(8,128)S(1)}, u32[]{:S(2)}, u32[]{:S(2)}) collective-permute-start(f32[2,160,256]{2,1,0:T(8,128)S(1)} %get-tuple-element.41), channel_id=1, source_target_pairs={{0,8},{1,9},{2,10},{3,11},{4,12},{5,13},{6,14},{7,15},{8,0},{9,1},... | collective-permute-start | bytes 983048 | tf_op jit(solution)/shard_map/ppermute | solution.py:490
  108.0 30.1 %collective-permute-start.21 = (f32[1,160,256]{2,1,0:T(8,128)S(1)}, f32[1,160,256]{2,1,0:T(8,128)S(1)}, u32[]{:S(2)}, u32[]{:S(2)}) collective-permute-start(f32[1,160,256]{2,1,0:T(8,128)S(1)} %get-tuple-element.48), channel_id=1, source_target_pairs={{0,8},{1,9},{2,10},{3,11},{4,12},{5,13},{6,14},{7,15},{8,0},{9,1},... | collective-permute-start | bytes 491528 | tf_op jit(solution)/shard_map/ppermute | solution.py:490
  119.3 18.8 %collective-permute-start.14 = (f32[1,160,256]{2,1,0:T(8,128)S(1)}, f32[1,160,256]{2,1,0:T(8,128)S(1)}, u32[]{:S(2)}, u32[]{:S(2)}) collective-permute-start(f32[1,160,256]{2,1,0:T(8,128)S(1)} %get-tuple-element.52), channel_id=1, source_target_pairs={{0,8},{1,9},{2,10},{3,11},{4,12},{5,13},{6,14},{7,15},{8,0},{9,1},... | collective-permute-start | bytes 491528 | tf_op jit(solution)/shard_map/ppermute | solution.py:490
  131.0 7.2 %collective-permute-start.18 = (f32[1,160,256]{2,1,0:T(8,128)S(1)}, f32[1,160,256]{2,1,0:T(8,128)S(1)}, u32[]{:S(2)}, u32[]{:S(2)}) collective-permute-start(f32[1,160,256]{2,1,0:T(8,128)S(1)} %get-tuple-element.50), channel_id=1, source_target_pairs={{0,2},{1,3},{2,0},{3,1},{4,6},{5,7},{6,4},{7,5},{8,10},{9,11},{10,... | collective-permute-start | bytes 491528 | tf_op jit(solution)/shard_map/ppermute | solution.py:490
  132.4 4.7 %collective-permute-start.9 = (f32[4,2,768]{2,1,0:T(2,128)S(1)}, f32[4,2,768]{2,1,0:T(2,128)S(1)}, u32[]{:S(2)}, u32[]{:S(2)}) collective-permute-start(f32[4,2,768]{2,1,0:T(2,128)S(1)} %get-tuple-element.58), channel_id=1, source_target_pairs={{0,8},{1,9},{2,10},{3,11},{4,12},{5,13},{6,14},{7,15},{8,0},{9,1},... | collective-permute-start | bytes 73736 | tf_op jit(solution)/shard_map/ppermute | solution.py:490
  132.4 5.0 %collective-permute-start.8 = (f32[4,2,768]{2,1,0:T(2,128)S(1)}, f32[4,2,768]{2,1,0:T(2,128)S(1)}, u32[]{:S(2)}, u32[]{:S(2)}) collective-permute-start(f32[4,2,768]{2,1,0:T(2,128)S(1)} %get-tuple-element.59), channel_id=1, source_target_pairs={{0,4},{1,5},{2,6},{3,7},{4,0},{5,1},{6,2},{7,3},{8,12},{9,13},{10,... | collective-permute-start | bytes 73736 | tf_op jit(solution)/shard_map/ppermute | solution.py:490
  (3 other events, 2.2 us)

commit v3 on v2

--- a/solution.py
+++ b/solution.py
@@ -467,8 +467,7 @@
     last_count = code_info[:, 2 * listed + 8 : 2 * listed + 9]
     count = jnp.where(last_count > 0, last_count, first_count)
     start = 0
-    for cut, kept, got in zip(cuts, last_refs[::2], last_refs[1::2]):
-        last_sums = kept[0] + got[0]
+    for cut, last_sums in zip(cuts, last_refs):
         columns = slice(start, start + cut)
         start += cut
         coarse = coarse_in[:, columns]
@@ -587,7 +586,8 @@
             6e9,
             "own_codes",
         )(me, vectors, fine_codes, gathered)
-        first_to = swap(after(first_to, gathered), 2 - step)
+        if step == 2:
+            first_to = swap(after(first_to, gathered), 0)
         gathered = jnp.concatenate([gathered, exchange(gathered, step)])
 
     top = groups.bit_length() - 1
@@ -629,6 +629,7 @@
         "sums",
     )(me, gathered, vectors, fine_codes, *sums, first, second, fine_in, first_to)
 
+    first_to = swap(after(first_to, terms[0]), 1)
     finished = []
     for at, steps in enumerate(bits):
         away, other, kept = terms[3 * at : 3 * at + 3]
@@ -642,12 +643,12 @@
             got = exchange(other, 1 << bit)
             half = got.shape[0] // 2
             other, kept = halved(got, kept[:half], kept[half:])
-        finished += [kept, exchange(other, 1 << steps[-1])]
+        finished.append((kept + exchange(other, 1 << steps[-1]))[0])
     return local(
         lambda *refs: final_kernel(groups, slot_count, share_rows, cuts, *refs),
         [(coarse_in.shape, F32), ((share_rows, feature), F32)],
         [VMEM, block((share_rows, feature), None, 0)]
-        + [VMEM] * (1 + 2 * len(cuts))
+        + [VMEM] * (1 + len(cuts))
         + [block((share_rows, LANES), None, 0), block((listed, LANES), None, 0)],
         [VMEM] * 2,
         [pltpu.VMEM((listed, feature), F32)],

time: 143 us -> 134 us (0.937)
  starting transfers between devices: 26 us -> 20.8 us
  waiting for transfers between devices: 49 us -> 44.7 us
    ppermute x22, starting transfers between devices: 26 us -> 20.8 us  [exchange(): lax.ppermute(values, 'cell', [(at, at ^ step) for at in range(groups)])]
    ppermute x22, waiting for transfers between devices: 49 us -> 44.7 us  [exchange(): lax.ppermute(values, 'cell', [(at, at ^ step) for at in range(groups)])]
    squeeze x0 -> x3, other arithmetic: none -> 2.1 us  [dense_plan(): finished.append((kept + exchange(other, 1 << steps[-1]))[0])]
    add x9, other arithmetic: 4.28 us -> 2.22 us  [halved(): return (other + got[:half], kept + got[half:])]
  transfers between devices with their start and end apart: 22 -> 22, of which waited for: 8 -> 8; matrix products, arithmetic and copies ran while one was open for 4% -> 4% of each run, Pallas kernels for 13% -> 14%
where the time goes in v3:
time: 134 us
  Pallas kernels  59.1 us (44%)
  waiting for transfers between devices  44.7 us (33%)
  starting transfers between devices  20.8 us (16%)
  other arithmetic  5.73 us (4%)
  local copies, waits for them, and re-layouts  2.35 us (2%)
    ppermute x22, waiting for transfers between devices, exchange(): lax.ppermute(values, 'cell', [(at, at ^ step) for at in range(groups)])  44.7 us
    pallas_call x1, Pallas kernels, dense_plan(): local(lambda *refs: sums_kernel(groups, slot_count, owner_cells, cuts, or...  35.4 us
    ppermute x22, starting transfers between devices, exchange(): lax.ppermute(values, 'cell', [(at, at ^ step) for at in range(groups)])  20.8 us
    pallas_call x2, Pallas kernels, dense_plan(): local(lambda me_ref, *refs, base=base: own_codes_kernel(base, *refs), [((...  11.9 us
    pallas_call x1, Pallas kernels, dense_plan(): local(lambda *refs: own_cells_kernel(groups, listed, *refs), [((listed, f...  6.58 us
    pallas_call x1, Pallas kernels, dense_plan(): local(lambda *refs: final_kernel(groups, slot_count, share_rows, cuts, *r...  3.97 us
  transfers between devices with their start and end apart: 22, of which 8 were waited for; matrix products, arithmetic and copies ran while one was open for 4% of the time, Pallas kernels for 14%

profile of v3, /device:TPU:0, one launch (start us, length us, event | category | flops | bytes accessed | tf_op | source)
XLA Modules:
  0.0 133.6 jit_solution(10275054412191264329)
XLA Ops:
  0.6 1.3 %pack.1 = s32[8,896]{1,0:T(8,128)} custom-call(s32[1]{0:T(128)} %bitcast.refs_0_.me_ref, s32[2,1536]{1,0:T(2,128)} %refs_3_.3, s32[2,1536]{1,0:T(2,128)} %refs_1_.6, s32[2,32]{1,0:T(2,128)} %refs_2_.5), custom_call_target="tpu_custom_call" | custom-call | flops 1000000000 | bytes 1000000 | tf_op jit(solution)/shard_map/pack/pallas_call | solution.py:558
  2.0 5.0 %collective-permute-start.2 = (s32[8,896]{1,0:T(8,128)}, s32[8,896]{1,0:T(8,128)S(1)}, u32[]{:S(2)}, u32[]{:S(2)}) collective-permute-start(s32[8,896]{1,0:T(8,128)} %pack.1), channel_id=1, source_target_pairs={{0,12},{1,13},{2,14},{3,15},{4,8},{5,9},{6,10},{7,11},{8,4},{9,5},... | collective-permute-start | bytes 86024 | tf_op jit(solution)/shard_map/ppermute | solution.py:489
  7.6 6.6 %own_cells.1 = (f32[32,768]{1,0:T(8,128)}, f32[32,768]{1,0:T(8,128)}, f32[16,1,2,768]{3,2,1,0:T(2,128)}) custom-call(s32[1]{0:T(128)} %bitcast.refs_0_.me_ref, bf16[1536,768]{1,0:T(8,128)(2,1)} %refs_2_.6, s32[2,1536]{1,0:T(2,128)} %refs_3_.3, s32[2,1536]{1,0:T(2,128)} %refs_1_.6, f32[2048,768]{1,0:T(8,128)} %refs_2_.7), custom_call_target="tpu_custom_call" | custom-call | flops 5000000000 | bytes 1000000 | tf_op jit(solution)/shard_map/own_cells/pallas_call | solution.py:567
  14.3 1.8 %collective-permute-start.4 = (s32[4,8,896]{2,1,0:T(8,128)S(1)}, s32[4,8,896]{2,1,0:T(8,128)S(1)}, u32[]{:S(2)}, u32[]{:S(2)}) collective-permute-start(s32[4,8,896]{2,1,0:T(8,128)S(1)} %pad_add_fusion.refs_2_), channel_id=1, source_target_pairs={{0,2},{1,3},{2,0},{3,1},{4,6},{5,7},{6,4},{7,5},{8,10},{9,11},{10,... | collective-permute-start | bytes 344072 | tf_op jit(solution)/shard_map/ppermute | solution.py:489
  16.1 5.9 %own_codes.2.refs_4_ = f32[1024,768]{1,0:T(8,128)} custom-call(s32[1]{0:T(128)} %bitcast.refs_0_.me_ref, bf16[1536,768]{1,0:T(8,128)(2,1)} %refs_2_.6, s32[2,1536]{1,0:T(2,128)} %refs_3_.3, s32[4,8,896]{2,1,0:T(8,128)} %copy-done.5), custom_call_target="tpu_custom_call" | custom-call | flops 6000000000 | bytes 1000000 | tf_op jit(solution)/shard_map/own_codes/pallas_call | solution.py:580
  22.1 1.2 collective-permute-done.3
  23.3 0.7 pad_maximum_fusion.refs_9_
  24.7 5.9 %own_codes.3.refs_5_ = f32[1024,768]{1,0:T(8,128)} custom-call(s32[1]{0:T(128)} %bitcast.refs_0_.me_ref, bf16[1536,768]{1,0:T(8,128)(2,1)} %refs_2_.6, s32[2,1536]{1,0:T(2,128)} %refs_3_.3, s32[8,8,896]{2,1,0:T(8,128)} %copy-done.8), custom_call_target="tpu_custom_call" | custom-call | flops 6000000000 | bytes 1000000 | tf_op jit(solution)/shard_map/own_codes/pallas_call | solution.py:580
  30.7 0.8 copy-done.9
  31.4 35.4 %sums.1 = (f32[8,160,256]{2,1,0:T(8,128)}, f32[4,160,256]{2,1,0:T(8,128)}, f32[4,160,256]{2,1,0:T(8,128)}, f32[8,160,256]{2,1,0:T(8,128)}, f32[4,160,256]{2,1,0:...) custom-call(s32[1]{0:T(128)} %bitcast.refs_0_.me_ref, ...), custom_call_target="tpu_custom_call" | custom-call | flops 40000000000 | bytes 1000000 | tf_op jit(solution)/shard_map/sums/pallas_call | solution.py:604
  67.6 0.6 collective-permute-start.6
  68.2 3.5 %collective-permute-done.6 = f32[4,2,2,768]{3,2,1,0:T(2,128)S(1)} collective-permute-done((f32[4,2,2,768]{3,2,1,0:T(2,128)S(1)}, f32[4,2,2,768]{3,2,1,0:T(2,128)S(1)}, u32[]{:S(2)}, u32[]{:S(2)}) %collective-permute-start.6) | collective-permute-done | bytes 49184 | tf_op jit(solution)/shard_map/ppermute | solution.py:489
  71.8 1.6 %slice_add_fusion = (f32[4,160,256]{2,1,0:T(8,128)S(1)}, f32[4,160,256]{2,1,0:T(8,128)S(1)}) fusion(f32[4,160,256]{2,1,0:T(8,128)} %get-tuple-element.33, f32[8,160,256]{2,1,0:T(8,128)S(1)} %collective-permute-done.7, f32[4,160,256]{2,1,0:T(8,128)} %get-tuple-element.25), kind=kLoop, calls=%fused_computation | loop fusion | flops 327680 | bytes 3932160 | tf_op jit(solution)/shard_map/add | solution.py:511
  73.4 0.6 collective-permute-start.19
  74.0 3.7 %collective-permute-start.10 = (f32[4,2,768]{2,1,0:T(2,128)S(1)}, f32[4,2,768]{2,1,0:T(2,128)S(1)}, u32[]{:S(2)}, u32[]{:S(2)}) collective-permute-start(f32[4,2,768]{2,1,0:T(2,128)S(1)} %get-tuple-element.51), channel_id=1, source_target_pairs={{0,12},{1,13},{2,14},{3,15},{4,8},{5,9},{6,10},{7,11},{8,4},{9,5},... | collective-permute-start | bytes 73736 | tf_op jit(solution)/shard_map/ppermute | solution.py:489
  78.0 0.8 copy-done
  79.1 1.5 %collective-permute-start.12 = (f32[4,160,256]{2,1,0:T(8,128)S(1)}, f32[4,160,256]{2,1,0:T(8,128)S(1)}, u32[]{:S(2)}, u32[]{:S(2)}) collective-permute-start(f32[4,160,256]{2,1,0:T(8,128)S(1)} %get-tuple-element.47), channel_id=1, source_target_pairs={{0,2},{1,3},{2,0},{3,1},{4,6},{5,7},{6,4},{7,5},{8,10},{9,11},{10,... | collective-permute-start | bytes 1966088 | tf_op jit(solution)/shard_map/ppermute | solution.py:489
  80.7 1.0 collective-permute-start.8
  81.7 10.4 %collective-permute-done.9 = f32[4,2,768]{2,1,0:T(2,128)S(1)} collective-permute-done((f32[4,2,768]{2,1,0:T(2,128)S(1)}, f32[4,2,768]{2,1,0:T(2,128)S(1)}, u32[]{:S(2)}, u32[]{:S(2)}) %collective-permute-start.9) | collective-permute-done | bytes 24608 | tf_op jit(solution)/shard_map/ppermute | solution.py:489
  92.1 2.5 %collective-permute-done.8 = f32[4,2,768]{2,1,0:T(2,128)S(1)} collective-permute-done((f32[4,2,768]{2,1,0:T(2,128)S(1)}, f32[4,2,768]{2,1,0:T(2,128)S(1)}, u32[]{:S(2)}, u32[]{:S(2)}) %collective-permute-start.8) | collective-permute-done | bytes 24608 | tf_op jit(solution)/shard_map/ppermute | solution.py:489
  94.5 0.7 pad_maximum_fusion.2.refs_3_
  95.7 0.9 collective-permute-start.17
  96.7 6.7 %collective-permute-done.12 = f32[4,160,256]{2,1,0:T(8,128)S(1)} collective-permute-done((f32[4,160,256]{2,1,0:T(8,128)S(1)}, f32[4,160,256]{2,1,0:T(8,128)S(1)}, u32[]{:S(2)}, u32[]{:S(2)}) %collective-permute-start.12) | collective-permute-done | bytes 655392 | tf_op jit(solution)/shard_map/ppermute | solution.py:489
  103.4 1.3 collective-permute-start.13
  104.7 6.5 %collective-permute-done.20 = f32[2,160,256]{2,1,0:T(8,128)S(1)} collective-permute-done((f32[2,160,256]{2,1,0:T(8,128)S(1)}, f32[2,160,256]{2,1,0:T(8,128)S(1)}, u32[]{:S(2)}, u32[]{:S(2)}) %collective-permute-start.20) | collective-permute-done | bytes 327712 | tf_op jit(solution)/shard_map/ppermute | solution.py:489
  111.5 2.0 %collective-permute-start.18 = (f32[1,160,256]{2,1,0:T(8,128)S(1)}, f32[1,160,256]{2,1,0:T(8,128)S(1)}, u32[]{:S(2)}, u32[]{:S(2)}) collective-permute-start(f32[1,160,256]{2,1,0:T(8,128)S(1)} %slice_add_fusion.14), channel_id=1, source_target_pairs={{0,2},{1,3},{2,0},{3,1},{4,6},{5,7},{6,4},{7,5},{8,10},{9,11},{10,... | collective-permute-start | bytes 491528 | tf_op jit(solution)/shard_map/ppermute | solution.py:489
  113.5 7.0 %collective-permute-done.13 = f32[2,160,256]{2,1,0:T(8,128)S(1)} collective-permute-done((f32[2,160,256]{2,1,0:T(8,128)S(1)}, f32[2,160,256]{2,1,0:T(8,128)S(1)}, u32[]{:S(2)}, u32[]{:S(2)}) %collective-permute-start.13) | collective-permute-done | bytes 327712 | tf_op jit(solution)/shard_map/ppermute | solution.py:489
  120.6 0.7 fusion.1.refs_6_
  121.3 0.7 fusion.3.refs_5_
  122.0 6.9 %collective-permute-done.14 = f32[1,160,256]{2,1,0:T(8,128)S(1)} collective-permute-done((f32[1,160,256]{2,1,0:T(8,128)S(1)}, f32[1,160,256]{2,1,0:T(8,128)S(1)}, u32[]{:S(2)}, u32[]{:S(2)}) %collective-permute-start.14) | collective-permute-done | bytes 163872 | tf_op jit(solution)/shard_map/ppermute | solution.py:489
  128.9 0.7 fusion.5.refs_4_
  129.6 4.0 %outputs.1 = (f32[512,768]{1,0:T(8,128)}, f32[128,768]{1,0:T(8,128)}) custom-call(s32[1]{0:T(128)} %bitcast.refs_0_.me_ref, f32[512,768]{1,0:T(8,128)} %refs_1_.9, f32[2048,768]{1,0:T(8,128)} %refs_2_.7, f32[16,2,768]{2,1,0:T(2,128)} %pad_maximum_fusion.2.refs_3_, f32[160,256]{1,0:T(8,128)} %fusion.5.refs_4_, f32[160,256]{1,0:T(8,128)} %fusion.3.refs_5_, ...), custom_call_target="tpu_custom_call" | custom-call | flops 1000000000 | bytes 1000000 | tf_op jit(solution)/shard_map/outputs/pallas_call | solution.py:647
  (63 shorter events, 3.8 us)
Async XLA Ops:
  2.0 12.2 %copy-start.6 = (s32[8,896]{1,0:T(8,128)S(1)}, s32[8,896]{1,0:T(8,128)}, u32[]{:S(2)}) copy-start(s32[8,896]{1,0:T(8,128)} %pack.1) | copy-start | bytes 86020
  2.0 12.2 %collective-permute-start.2 = (s32[8,896]{1,0:T(8,128)}, s32[8,896]{1,0:T(8,128)S(1)}, u32[]{:S(2)}, u32[]{:S(2)}) collective-permute-start(s32[8,896]{1,0:T(8,128)} %pack.1), channel_id=1, source_target_pairs={{0,12},{1,13},{2,14},{3,15},{4,8},{5,9},{6,10},{7,11},{8,4},{9,5},... | collective-permute-start | bytes 86024 | tf_op jit(solution)/shard_map/ppermute | solution.py:489
  7.0 7.2 %collective-permute-start.1 = (s32[8,896]{1,0:T(8,128)}, s32[8,896]{1,0:T(8,128)S(1)}, u32[]{:S(2)}, u32[]{:S(2)}) collective-permute-start(s32[8,896]{1,0:T(8,128)} %pack.1), channel_id=1, source_target_pairs={{0,8},{1,9},{2,10},{3,11},{4,12},{5,13},{6,14},{7,15},{8,0},{9,1},... | collective-permute-start | bytes 86024 | tf_op jit(solution)/shard_map/ppermute | solution.py:489
  7.0 7.2 %collective-permute-start = (s32[8,896]{1,0:T(8,128)}, s32[8,896]{1,0:T(8,128)S(1)}, u32[]{:S(2)}, u32[]{:S(2)}) collective-permute-start(s32[8,896]{1,0:T(8,128)} %pack.1), channel_id=1, source_target_pairs={{0,4},{1,5},{2,6},{3,7},{4,0},{5,1},{6,2},{7,3},{8,12},{9,13},{10,... | collective-permute-start | bytes 86024 | tf_op jit(solution)/shard_map/ppermute | solution.py:489
  14.2 1.8 %copy-start.5 = (s32[4,8,896]{2,1,0:T(8,128)}, s32[4,8,896]{2,1,0:T(8,128)S(1)}, u32[]{:S(2)}) copy-start(s32[4,8,896]{2,1,0:T(8,128)S(1)} %pad_add_fusion.refs_2_) | copy-start | bytes 344068
  14.2 7.7 %copy-start.7 = (f32[16,1,2,768]{3,2,1,0:T(2,128)S(1)}, f32[16,1,2,768]{3,2,1,0:T(2,128)}, u32[]{:S(2)}) copy-start(f32[16,1,2,768]{3,2,1,0:T(2,128)} %get-tuple-element.20) | copy-start | bytes 294916
  14.3 9.7 %collective-permute-start.4 = (s32[4,8,896]{2,1,0:T(8,128)S(1)}, s32[4,8,896]{2,1,0:T(8,128)S(1)}, u32[]{:S(2)}, u32[]{:S(2)}) collective-permute-start(s32[4,8,896]{2,1,0:T(8,128)S(1)} %pad_add_fusion.refs_2_), channel_id=1, source_target_pairs={{0,2},{1,3},{2,0},{3,1},{4,6},{5,7},{6,4},{7,5},{8,10},{9,11},{10,... | collective-permute-start | bytes 344072 | tf_op jit(solution)/shard_map/ppermute | solution.py:489
  22.0 1.3 collective-permute-start.3
  24.0 0.7 copy-start.8
  24.0 6.6 %collective-permute-start.5 = (s32[8,8,896]{2,1,0:T(8,128)S(1)}, s32[8,8,896]{2,1,0:T(8,128)S(1)}, u32[]{:S(2)}, u32[]{:S(2)}) collective-permute-start(s32[8,8,896]{2,1,0:T(8,128)S(1)} %get-tuple-element.48.refs_2_), channel_id=1, source_target_pairs={{0,1},{1,0},{2,3},{3,2},{4,5},{5,4},{6,7},{7,6},{8,9},{9,8},{10,11... | collective-permute-start | bytes 688136 | tf_op jit(solution)/shard_map/ppermute | solution.py:489
  30.7 0.8 copy-start.9
  31.4 36.1 %copy-start.4 = (f32[8,2,2,768]{3,2,1,0:T(2,128)S(1)}, f32[8,2,2,768]{3,2,1,0:T(2,128)}, u32[]{:S(2)}) copy-start(f32[8,2,2,768]{3,2,1,0:T(2,128)} %pad_maximum_fusion.refs_9_) | copy-start | bytes 294916
  66.8 5.0 %collective-permute-start.7 = (f32[8,160,256]{2,1,0:T(8,128)}, f32[8,160,256]{2,1,0:T(8,128)S(1)}, u32[]{:S(2)}, u32[]{:S(2)}) collective-permute-start(f32[8,160,256]{2,1,0:T(8,128)} %get-tuple-element.26), channel_id=1, source_target_pairs={{0,1},{1,0},{2,3},{3,2},{4,5},{5,4},{6,7},{7,6},{8,9},{9,8},{10,11... | collective-permute-start | bytes 3932168 | tf_op jit(solution)/shard_map/ppermute | solution.py:489
  67.0 10.6 %collective-permute-start.15 = (f32[8,160,256]{2,1,0:T(8,128)}, f32[8,160,256]{2,1,0:T(8,128)S(1)}, u32[]{:S(2)}, u32[]{:S(2)}) collective-permute-start(f32[8,160,256]{2,1,0:T(8,128)} %get-tuple-element.31), channel_id=1, source_target_pairs={{0,1},{1,0},{2,3},{3,2},{4,5},{5,4},{6,7},{7,6},{8,9},{9,8},{10,11... | collective-permute-start | bytes 3932168 | tf_op jit(solution)/shard_map/ppermute | solution.py:489
  67.4 10.6 %collective-permute-start.11 = (f32[8,160,256]{2,1,0:T(8,128)}, f32[8,160,256]{2,1,0:T(8,128)S(1)}, u32[]{:S(2)}, u32[]{:S(2)}) collective-permute-start(f32[8,160,256]{2,1,0:T(8,128)} %get-tuple-element.23), channel_id=1, source_target_pairs={{0,1},{1,0},{2,3},{3,2},{4,5},{5,4},{6,7},{7,6},{8,9},{9,8},{10,11... | collective-permute-start | bytes 3932168 | tf_op jit(solution)/shard_map/ppermute | solution.py:489
  67.6 4.2 %collective-permute-start.6 = (f32[4,2,2,768]{3,2,1,0:T(2,128)S(1)}, f32[4,2,2,768]{3,2,1,0:T(2,128)S(1)}, u32[]{:S(2)}, u32[]{:S(2)}) collective-permute-start(f32[4,2,2,768]{3,2,1,0:T(2,128)S(1)} %get-tuple-element.55), channel_id=1, source_target_pairs={{0,2},{1,3},{2,0},{3,1},{4,6},{5,7},{6,4},{7,5},{8,10},{9,11},{10,... | collective-permute-start | bytes 147464 | tf_op jit(solution)/shard_map/ppermute | solution.py:489
  71.8 5.9 %copy-start.2 = (f32[4,160,256]{2,1,0:T(8,128)S(1)}, f32[4,160,256]{2,1,0:T(8,128)}, u32[]{:S(2)}) copy-start(f32[4,160,256]{2,1,0:T(8,128)} %get-tuple-element.32) | copy-start | bytes 1966084
  71.8 5.9 %copy-start.3 = (f32[4,160,256]{2,1,0:T(8,128)S(1)}, f32[4,160,256]{2,1,0:T(8,128)}, u32[]{:S(2)}) copy-start(f32[4,160,256]{2,1,0:T(8,128)} %get-tuple-element.30) | copy-start | bytes 1966084
  73.4 21.8 %collective-permute-start.19 = (f32[4,160,256]{2,1,0:T(8,128)S(1)}, f32[4,160,256]{2,1,0:T(8,128)S(1)}, u32[]{:S(2)}, u32[]{:S(2)}) collective-permute-start(f32[4,160,256]{2,1,0:T(8,128)S(1)} %get-tuple-element.39), channel_id=1, source_target_pairs={{0,2},{1,3},{2,0},{3,1},{4,6},{5,7},{6,4},{7,5},{8,10},{9,11},{10,... | collective-permute-start | bytes 1966088 | tf_op jit(solution)/shard_map/ppermute | solution.py:489
  74.0 6.7 %collective-permute-start.10 = (f32[4,2,768]{2,1,0:T(2,128)S(1)}, f32[4,2,768]{2,1,0:T(2,128)S(1)}, u32[]{:S(2)}, u32[]{:S(2)}) collective-permute-start(f32[4,2,768]{2,1,0:T(2,128)S(1)} %get-tuple-element.51), channel_id=1, source_target_pairs={{0,12},{1,13},{2,14},{3,15},{4,8},{5,9},{6,10},{7,11},{8,4},{9,5},... | collective-permute-start | bytes 73736 | tf_op jit(solution)/shard_map/ppermute | solution.py:489
  77.7 1.1 copy-start
  77.7 1.3 copy-start.1
  77.9 17.8 %collective-permute-start.16 = (f32[4,160,256]{2,1,0:T(8,128)S(1)}, f32[4,160,256]{2,1,0:T(8,128)S(1)}, u32[]{:S(2)}, u32[]{:S(2)}) collective-permute-start(f32[4,160,256]{2,1,0:T(8,128)S(1)} %get-tuple-element.43), channel_id=1, source_target_pairs={{0,4},{1,5},{2,6},{3,7},{4,0},{5,1},{6,2},{7,3},{8,12},{9,13},{10,... | collective-permute-start | bytes 1966088 | tf_op jit(solution)/shard_map/ppermute | solution.py:489
  79.1 24.2 %collective-permute-start.12 = (f32[4,160,256]{2,1,0:T(8,128)S(1)}, f32[4,160,256]{2,1,0:T(8,128)S(1)}, u32[]{:S(2)}, u32[]{:S(2)}) collective-permute-start(f32[4,160,256]{2,1,0:T(8,128)S(1)} %get-tuple-element.47), channel_id=1, source_target_pairs={{0,2},{1,3},{2,0},{3,1},{4,6},{5,7},{6,4},{7,5},{8,10},{9,11},{10,... | collective-permute-start | bytes 1966088 | tf_op jit(solution)/shard_map/ppermute | solution.py:489
  80.7 11.4 %collective-permute-start.9 = (f32[4,2,768]{2,1,0:T(2,128)S(1)}, f32[4,2,768]{2,1,0:T(2,128)S(1)}, u32[]{:S(2)}, u32[]{:S(2)}) collective-permute-start(f32[4,2,768]{2,1,0:T(2,128)S(1)} %get-tuple-element.52), channel_id=1, source_target_pairs={{0,8},{1,9},{2,10},{3,11},{4,12},{5,13},{6,14},{7,15},{8,0},{9,1},... | collective-permute-start | bytes 73736 | tf_op jit(solution)/shard_map/ppermute | solution.py:489
  80.7 13.8 %collective-permute-start.8 = (f32[4,2,768]{2,1,0:T(2,128)S(1)}, f32[4,2,768]{2,1,0:T(2,128)S(1)}, u32[]{:S(2)}, u32[]{:S(2)}) collective-permute-start(f32[4,2,768]{2,1,0:T(2,128)S(1)} %get-tuple-element.53), channel_id=1, source_target_pairs={{0,4},{1,5},{2,6},{3,7},{4,0},{5,1},{6,2},{7,3},{8,12},{9,13},{10,... | collective-permute-start | bytes 73736 | tf_op jit(solution)/shard_map/ppermute | solution.py:489
  95.3 15.9 %collective-permute-start.20 = (f32[2,160,256]{2,1,0:T(8,128)S(1)}, f32[2,160,256]{2,1,0:T(8,128)S(1)}, u32[]{:S(2)}, u32[]{:S(2)}) collective-permute-start(f32[2,160,256]{2,1,0:T(8,128)S(1)} %get-tuple-element.37), channel_id=1, source_target_pairs={{0,4},{1,5},{2,6},{3,7},{4,0},{5,1},{6,2},{7,3},{8,12},{9,13},{10,... | collective-permute-start | bytes 983048 | tf_op jit(solution)/shard_map/ppermute | solution.py:489
  95.7 15.7 %collective-permute-start.17 = (f32[2,160,256]{2,1,0:T(8,128)S(1)}, f32[2,160,256]{2,1,0:T(8,128)S(1)}, u32[]{:S(2)}, u32[]{:S(2)}) collective-permute-start(f32[2,160,256]{2,1,0:T(8,128)S(1)} %get-tuple-element.41), channel_id=1, source_target_pairs={{0,8},{1,9},{2,10},{3,11},{4,12},{5,13},{6,14},{7,15},{8,0},{9,1},... | collective-permute-start | bytes 983048 | tf_op jit(solution)/shard_map/ppermute | solution.py:489
  103.4 17.1 %collective-permute-start.13 = (f32[2,160,256]{2,1,0:T(8,128)S(1)}, f32[2,160,256]{2,1,0:T(8,128)S(1)}, u32[]{:S(2)}, u32[]{:S(2)}) collective-permute-start(f32[2,160,256]{2,1,0:T(8,128)S(1)} %get-tuple-element.45), channel_id=1, source_target_pairs={{0,4},{1,5},{2,6},{3,7},{4,0},{5,1},{6,2},{7,3},{8,12},{9,13},{10,... | collective-permute-start | bytes 983048 | tf_op jit(solution)/shard_map/ppermute | solution.py:489
  111.3 9.4 %collective-permute-start.21 = (f32[1,160,256]{2,1,0:T(8,128)S(1)}, f32[1,160,256]{2,1,0:T(8,128)S(1)}, u32[]{:S(2)}, u32[]{:S(2)}) collective-permute-start(f32[1,160,256]{2,1,0:T(8,128)S(1)} %slice_add_fusion.12), channel_id=1, source_target_pairs={{0,8},{1,9},{2,10},{3,11},{4,12},{5,13},{6,14},{7,15},{8,0},{9,1},... | collective-permute-start | bytes 491528 | tf_op jit(solution)/shard_map/ppermute | solution.py:489
  111.5 9.8 %collective-permute-start.18 = (f32[1,160,256]{2,1,0:T(8,128)S(1)}, f32[1,160,256]{2,1,0:T(8,128)S(1)}, u32[]{:S(2)}, u32[]{:S(2)}) collective-permute-start(f32[1,160,256]{2,1,0:T(8,128)S(1)} %slice_add_fusion.14), channel_id=1, source_target_pairs={{0,2},{1,3},{2,0},{3,1},{4,6},{5,7},{6,4},{7,5},{8,10},{9,11},{10,... | collective-permute-start | bytes 491528 | tf_op jit(solution)/shard_map/ppermute | solution.py:489
  120.5 8.4 %collective-permute-start.14 = (f32[1,160,256]{2,1,0:T(8,128)S(1)}, f32[1,160,256]{2,1,0:T(8,128)S(1)}, u32[]{:S(2)}, u32[]{:S(2)}) collective-permute-start(f32[1,160,256]{2,1,0:T(8,128)S(1)} %slice_add_fusion.16), channel_id=1, source_target_pairs={{0,8},{1,9},{2,10},{3,11},{4,12},{5,13},{6,14},{7,15},{8,0},{9,1},... | collective-permute-start | bytes 491528 | tf_op jit(solution)/shard_map/ppermute | solution.py:489

commit v4 on v3

--- a/solution.py
+++ b/solution.py
@@ -200,10 +200,11 @@
     slot_count,
     owner_cells,
     cuts,
+    starts,
     orders,
     me_ref,
     codes_ref,
-    vectors,
+    vectors_ref,
     fine_codes,
     low_sums_ref,
     high_sums_ref,
@@ -217,7 +218,7 @@
     code_info_ref, entry_info_ref, refs = refs[0], refs[1], refs[2:]
     table0, table1, cell0, cell1, wide, terms, permuted, rows_hot = refs[:8]
     fine, bracket, centers_ref, pairs_ref, left = refs[8:13]
-    in_sem, out_sem, stages = refs[13], refs[14], refs[15:]
+    in_sem, out_sem, vectors, stages = refs[13], refs[14], refs[15], refs[16:]
     me = me_ref[0]
     codewords, feature = fine.shape
     listed = groups * slot_count
@@ -232,6 +233,7 @@
         )
         for at, ref in enumerate((low_sums_ref, high_sums_ref))
     ]
+    loads.append(pltpu.make_async_copy(vectors_ref, vectors, in_sem.at[2]))
     for load in loads:
         load.start()
 
@@ -403,10 +405,8 @@
             own = jnp.where((own >= 0) & (own < share_rows), own, -1)
             left[to, :rows_here] = hot(own)[:share_rows]
             left[to, rows_here:] = pairs_ref[rows, :]
-        start = 0
-        for chunk, cut in enumerate(cuts):
+        for chunk, (start, cut) in enumerate(zip(starts, cuts)):
             columns = slice(start, start + cut)
-            start += cut
             sums = (
                 matmul(left[:, :rows_here], vectors[:, columns])
                 + matmul(left[:, rows_here:], centers_ref[0, :, columns])
@@ -446,9 +446,19 @@
 
 
 def final_kernel(
-    groups, slot_count, share_rows, cuts, me_ref, coarse_in, fine_share, first_sums, *refs
+    groups,
+    slot_count,
+    share_rows,
+    starts,
+    me_ref,
+    coarse_in,
+    fine_share,
+    first_sums,
+    code_info,
+    entry_info,
+    *refs,
 ):
-    last_refs, (code_info, entry_info, coarse_out, fine_out, own_first) = refs[:-5], refs[-5:]
+    last_refs, (coarse_out, fine_out, own_first) = refs[: len(starts)], refs[-3:]
     listed = entry_info.shape[0]
     owner_cells = coarse_in.shape[0]
     by_lane = entry_info[...].T
@@ -466,10 +476,8 @@
     first_count = code_info[:, 2 * listed : 2 * listed + 1]
     last_count = code_info[:, 2 * listed + 8 : 2 * listed + 9]
     count = jnp.where(last_count > 0, last_count, first_count)
-    start = 0
-    for cut, last_sums in zip(cuts, last_refs):
-        columns = slice(start, start + cut)
-        start += cut
+    for start, last_sums in zip(starts, last_refs):
+        columns = slice(start, start + last_sums.shape[1])
         coarse = coarse_in[:, columns]
         for sweep, sums in enumerate((own_first[:, columns], last_sums[share_rows:, :])):
             sums_high, sums_low = split(sums)
@@ -595,6 +603,7 @@
     far_first = near_first[1:] + near_first[:1]
     cuts = [feature // 3] * 3
     bits = [near_first, far_first, near_first]
+    starts = [feature - cuts[0], cuts[0], 0]
     orders = [block_orders(each) for each in bits]
     shapes = [
         (len(order), share_rows + listed, cut)
@@ -602,10 +611,12 @@
         for order in three
     ]
     *terms, code_info, entry_info = local(
-        lambda *refs: sums_kernel(groups, slot_count, owner_cells, cuts, orders, *refs),
+        lambda *refs: sums_kernel(
+            groups, slot_count, owner_cells, cuts, starts, orders, *refs
+        ),
         [(shape, F32) for shape in shapes]
         + [((codewords, LANES), F32), ((entries, LANES), F32)],
-        [VMEM] * 3 + [ANY] * 2 + [VMEM] * 2 + [block((share_rows, feature), None, 0), ANY],
+        [VMEM, ANY, VMEM] + [ANY] * 2 + [VMEM] * 2 + [block((share_rows, feature), None, 0), ANY],
         [ANY] * len(shapes) + [VMEM] * 2,
         [
             pltpu.VMEM((entries, codewords), F32),
@@ -621,8 +632,9 @@
             pltpu.VMEM((2, entries, feature), BF16),
             pltpu.VMEM((codewords, entries), BF16),
             pltpu.VMEM((codewords // 2, rows_here + entries), BF16),
-            pltpu.SemaphoreType.DMA((2,)),
+            pltpu.SemaphoreType.DMA((3,)),
             pltpu.SemaphoreType.DMA((len(shapes),)),
+            pltpu.VMEM(vectors.shape, BF16),
         ]
         + [pltpu.VMEM(shape, F32) for shape in shapes],
         40e9,
@@ -644,17 +656,43 @@
             half = got.shape[0] // 2
             other, kept = halved(got, kept[:half], kept[half:])
         finished.append((kept + exchange(other, 1 << steps[-1]))[0])
-    return local(
-        lambda *refs: final_kernel(groups, slot_count, share_rows, cuts, *refs),
-        [(coarse_in.shape, F32), ((share_rows, feature), F32)],
-        [VMEM, block((share_rows, feature), None, 0)]
-        + [VMEM] * (1 + len(cuts))
-        + [block((share_rows, LANES), None, 0), block((listed, LANES), None, 0)],
-        [VMEM] * 2,
-        [pltpu.VMEM((listed, feature), F32)],
-        1e9,
-        "outputs",
-    )(me, coarse_in, fine_in, first_to, *finished, code_info, entry_info)
+    outs = ()
+    for chunks, width in ((range(1, len(cuts)), feature), ((0,), cuts[0])):
+        place = feature // width - 1
+        outs = local(
+            lambda *refs, chunks=chunks, width=width, place=place: final_kernel(
+                groups,
+                slot_count,
+                share_rows,
+                [starts[at] - place * width for at in chunks],
+                *refs,
+            ),
+            [(coarse_in.shape, F32), ((share_rows, feature), F32)],
+            [
+                block((owner_cells, width), 0, place),
+                block((share_rows, width), None, place),
+                block((groups, slot_count, width), 0, 0, place),
+                block((share_rows, LANES), None, 0),
+                block((listed, LANES), None, 0),
+            ]
+            + [VMEM] * len(chunks)
+            + [ANY] * len(outs),
+            [block((owner_cells, width), 0, place), block((share_rows, width), 0, place)],
+            [pltpu.VMEM((listed, width), F32)],
+            1e9,
+            "outputs",
+            {6 + len(chunks) + number: number for number in range(len(outs))},
+        )(
+            me,
+            coarse_in,
+            fine_in,
+            first_to,
+            code_info,
+            entry_info,
+            *(finished[at] for at in chunks),
+            *outs,
+        )
+    return tuple(outs)
 
 
 def fits_dense(mesh_groups, listed, codewords, rows_here, feature):

time: 134 us -> 132 us (0.985)
  waiting for transfers between devices: 44.7 us -> 41 us
  Pallas kernels: 59.1 us -> 60.6 us
    ppermute x22, waiting for transfers between devices: 44.7 us -> 41 us  [exchange(): lax.ppermute(values, 'cell', [(at, at ^ step) for at in range(groups)])]
    pallas_call x2 -> x3, Pallas kernels: 39.3 us -> 40.9 us  [the longest x1 34.7 us: dense_plan(): local(lambda *refs: sums_kernel(groups, slot_count, owner_cells, cuts, st...]
  transfers between devices with their start and end apart: 22 -> 22, of which waited for: 8 -> 8; matrix products, arithmetic and copies ran while one was open for 4% -> 4% of each run, Pallas kernels for 14% -> 17%
where the time goes in v4:
time: 132 us
  Pallas kernels  60.6 us (46%)
  waiting for transfers between devices  41 us (31%)
  starting transfers between devices  20.9 us (16%)
  other arithmetic  5.74 us (4%)
  local copies, waits for them, and re-layouts  2.36 us (2%)
    ppermute x22, waiting for transfers between devices, exchange(): lax.ppermute(values, 'cell', [(at, at ^ step) for at in range(groups)])  41 us
    pallas_call x1, Pallas kernels, dense_plan(): local(lambda *refs: sums_kernel(groups, slot_count, owner_cells, cuts, st...  34.7 us
    ppermute x22, starting transfers between devices, exchange(): lax.ppermute(values, 'cell', [(at, at ^ step) for at in range(groups)])  20.9 us
    pallas_call x2, Pallas kernels, dense_plan(): local(lambda me_ref, *refs, base=base: own_codes_kernel(base, *refs), [((...  11.8 us
    pallas_call x1, Pallas kernels, dense_plan(): local(lambda *refs: own_cells_kernel(groups, listed, *refs), [((listed, f...  6.58 us
    pallas_call x2, Pallas kernels, dense_plan(): local(lambda *refs, chunks=chunks, width=width, place=place: final_kernel...  6.16 us
  transfers between devices with their start and end apart: 22, of which 8 were waited for; matrix products, arithmetic and copies ran while one was open for 4% of the time, Pallas kernels for 17%

profile of v4, /device:TPU:0, one launch (start us, length us, event | category | flops | bytes accessed | tf_op | source)
XLA Modules:
  0.0 131.5 jit_solution(13586803192718492084)
XLA Ops:
  0.6 1.3 %pack.1 = s32[8,896]{1,0:T(8,128)} custom-call(s32[1]{0:T(128)} %bitcast.refs_0_.me_ref, s32[2,1536]{1,0:T(2,128)} %refs_3_.3, s32[2,1536]{1,0:T(2,128)} %refs_1_.7, s32[2,32]{1,0:T(2,128)} %refs_2_.6), custom_call_target="tpu_custom_call" | custom-call | flops 1000000000 | bytes 1000000 | tf_op jit(solution)/shard_map/pack/pallas_call | solution.py:566
  2.0 5.0 %collective-permute-start.2 = (s32[8,896]{1,0:T(8,128)}, s32[8,896]{1,0:T(8,128)S(1)}, u32[]{:S(2)}, u32[]{:S(2)}) collective-permute-start(s32[8,896]{1,0:T(8,128)} %pack.1), channel_id=1, source_target_pairs={{0,12},{1,13},{2,14},{3,15},{4,8},{5,9},{6,10},{7,11},{8,4},{9,5},... | collective-permute-start | bytes 86024 | tf_op jit(solution)/shard_map/ppermute | solution.py:497
  7.6 6.6 %own_cells.1 = (f32[32,768]{1,0:T(8,128)}, f32[32,768]{1,0:T(8,128)}, f32[16,1,2,768]{3,2,1,0:T(2,128)}) custom-call(s32[1]{0:T(128)} %bitcast.refs_0_.me_ref, bf16[1536,768]{1,0:T(8,128)(2,1)} %refs_2_.7, s32[2,1536]{1,0:T(2,128)} %refs_3_.3, s32[2,1536]{1,0:T(2,128)} %refs_1_.7, f32[2048,768]{1,0:T(8,128)} %refs_2_.9), custom_call_target="tpu_custom_call" | custom-call | flops 5000000000 | bytes 1000000 | tf_op jit(solution)/shard_map/own_cells/pallas_call | solution.py:575
  14.3 1.8 %collective-permute-start.4 = (s32[4,8,896]{2,1,0:T(8,128)S(1)}, s32[4,8,896]{2,1,0:T(8,128)S(1)}, u32[]{:S(2)}, u32[]{:S(2)}) collective-permute-start(s32[4,8,896]{2,1,0:T(8,128)S(1)} %pad_add_fusion.refs_2_), channel_id=1, source_target_pairs={{0,2},{1,3},{2,0},{3,1},{4,6},{5,7},{6,4},{7,5},{8,10},{9,11},{10,... | collective-permute-start | bytes 344072 | tf_op jit(solution)/shard_map/ppermute | solution.py:497
  16.1 5.9 %own_codes.2.refs_4_ = f32[1024,768]{1,0:T(8,128)} custom-call(s32[1]{0:T(128)} %bitcast.refs_0_.me_ref, bf16[1536,768]{1,0:T(8,128)(2,1)} %refs_2_.7, s32[2,1536]{1,0:T(2,128)} %refs_3_.3, s32[4,8,896]{2,1,0:T(8,128)} %copy-done.5), custom_call_target="tpu_custom_call" | custom-call | flops 6000000000 | bytes 1000000 | tf_op jit(solution)/shard_map/own_codes/pallas_call | solution.py:588
  22.1 1.2 collective-permute-done.3
  23.3 0.7 pad_maximum_fusion.refs_9_
  24.7 5.9 %own_codes.3.refs_5_ = f32[1024,768]{1,0:T(8,128)} custom-call(s32[1]{0:T(128)} %bitcast.refs_0_.me_ref, bf16[1536,768]{1,0:T(8,128)(2,1)} %refs_2_.7, s32[2,1536]{1,0:T(2,128)} %refs_3_.3, s32[8,8,896]{2,1,0:T(8,128)} %copy-done.8), custom_call_target="tpu_custom_call" | custom-call | flops 6000000000 | bytes 1000000 | tf_op jit(solution)/shard_map/own_codes/pallas_call | solution.py:588
  30.7 0.8 copy-done.9
  31.4 34.7 %sums.1 = (f32[8,160,256]{2,1,0:T(8,128)}, f32[4,160,256]{2,1,0:T(8,128)}, f32[4,160,256]{2,1,0:T(8,128)}, f32[8,160,256]{2,1,0:T(8,128)}, f32[4,160,256]{2,1,0:...) custom-call(s32[1]{0:T(128)} %bitcast.refs_0_.me_ref, ...), custom_call_target="tpu_custom_call" | custom-call | flops 40000000000 | bytes 1000000 | tf_op jit(solution)/shard_map/sums/pallas_call | solution.py:613
  67.5 3.5 %collective-permute-done.6 = f32[4,2,2,768]{3,2,1,0:T(2,128)S(1)} collective-permute-done((f32[4,2,2,768]{3,2,1,0:T(2,128)S(1)}, f32[4,2,2,768]{3,2,1,0:T(2,128)S(1)}, u32[]{:S(2)}, u32[]{:S(2)}) %collective-permute-start.6) | collective-permute-done | bytes 49184 | tf_op jit(solution)/shard_map/ppermute | solution.py:497
  71.1 1.6 %slice_add_fusion = (f32[4,160,256]{2,1,0:T(8,128)S(1)}, f32[4,160,256]{2,1,0:T(8,128)S(1)}) fusion(f32[4,160,256]{2,1,0:T(8,128)} %get-tuple-element.37, f32[8,160,256]{2,1,0:T(8,128)S(1)} %collective-permute-done.7, f32[4,160,256]{2,1,0:T(8,128)} %get-tuple-element.27), kind=kLoop, calls=%fused_computation | loop fusion | flops 327680 | bytes 3932160 | tf_op jit(solution)/shard_map/add | solution.py:519
  72.7 0.6 collective-permute-start.19
  73.3 3.7 %collective-permute-start.10 = (f32[4,2,768]{2,1,0:T(2,128)S(1)}, f32[4,2,768]{2,1,0:T(2,128)S(1)}, u32[]{:S(2)}, u32[]{:S(2)}) collective-permute-start(f32[4,2,768]{2,1,0:T(2,128)S(1)} %get-tuple-element.55), channel_id=1, source_target_pairs={{0,12},{1,13},{2,14},{3,15},{4,8},{5,9},{6,10},{7,11},{8,4},{9,5},... | collective-permute-start | bytes 73736 | tf_op jit(solution)/shard_map/ppermute | solution.py:497
  77.3 0.8 copy-done
  78.5 1.5 %collective-permute-start.12 = (f32[4,160,256]{2,1,0:T(8,128)S(1)}, f32[4,160,256]{2,1,0:T(8,128)S(1)}, u32[]{:S(2)}, u32[]{:S(2)}) collective-permute-start(f32[4,160,256]{2,1,0:T(8,128)S(1)} %get-tuple-element.51), channel_id=1, source_target_pairs={{0,2},{1,3},{2,0},{3,1},{4,6},{5,7},{6,4},{7,5},{8,10},{9,11},{10,... | collective-permute-start | bytes 1966088 | tf_op jit(solution)/shard_map/ppermute | solution.py:497
  80.0 1.0 collective-permute-start.8
  81.0 10.4 %collective-permute-done.9 = f32[4,2,768]{2,1,0:T(2,128)S(1)} collective-permute-done((f32[4,2,768]{2,1,0:T(2,128)S(1)}, f32[4,2,768]{2,1,0:T(2,128)S(1)}, u32[]{:S(2)}, u32[]{:S(2)}) %collective-permute-start.9) | collective-permute-done | bytes 24608 | tf_op jit(solution)/shard_map/ppermute | solution.py:497
  91.4 2.5 %collective-permute-done.8 = f32[4,2,768]{2,1,0:T(2,128)S(1)} collective-permute-done((f32[4,2,768]{2,1,0:T(2,128)S(1)}, f32[4,2,768]{2,1,0:T(2,128)S(1)}, u32[]{:S(2)}, u32[]{:S(2)}) %collective-permute-start.8) | collective-permute-done | bytes 24608 | tf_op jit(solution)/shard_map/ppermute | solution.py:497
  93.9 0.7 pad_maximum_fusion.2.refs_3_
  95.1 0.9 collective-permute-start.17
  96.0 6.6 %collective-permute-done.12 = f32[4,160,256]{2,1,0:T(8,128)S(1)} collective-permute-done((f32[4,160,256]{2,1,0:T(8,128)S(1)}, f32[4,160,256]{2,1,0:T(8,128)S(1)}, u32[]{:S(2)}, u32[]{:S(2)}) %collective-permute-start.12) | collective-permute-done | bytes 655392 | tf_op jit(solution)/shard_map/ppermute | solution.py:497
  102.7 1.3 collective-permute-start.13
  104.0 6.5 %collective-permute-done.20 = f32[2,160,256]{2,1,0:T(8,128)S(1)} collective-permute-done((f32[2,160,256]{2,1,0:T(8,128)S(1)}, f32[2,160,256]{2,1,0:T(8,128)S(1)}, u32[]{:S(2)}, u32[]{:S(2)}) %collective-permute-start.20) | collective-permute-done | bytes 327712 | tf_op jit(solution)/shard_map/ppermute | solution.py:497
  110.9 2.0 %collective-permute-start.18 = (f32[1,160,256]{2,1,0:T(8,128)S(1)}, f32[1,160,256]{2,1,0:T(8,128)S(1)}, u32[]{:S(2)}, u32[]{:S(2)}) collective-permute-start(f32[1,160,256]{2,1,0:T(8,128)S(1)} %slice_add_fusion.14), channel_id=1, source_target_pairs={{0,2},{1,3},{2,0},{3,1},{4,6},{5,7},{6,4},{7,5},{8,10},{9,11},{10,... | collective-permute-start | bytes 491528 | tf_op jit(solution)/shard_map/ppermute | solution.py:497
  112.9 7.0 %collective-permute-done.13 = f32[2,160,256]{2,1,0:T(8,128)S(1)} collective-permute-done((f32[2,160,256]{2,1,0:T(8,128)S(1)}, f32[2,160,256]{2,1,0:T(8,128)S(1)}, u32[]{:S(2)}, u32[]{:S(2)}) %collective-permute-start.13) | collective-permute-done | bytes 327712 | tf_op jit(solution)/shard_map/ppermute | solution.py:497
  120.0 0.7 fusion.1.refs_7_
  120.7 0.7 fusion.3.refs_6_
  121.4 3.6 %outputs.2 = (f32[512,768]{1,0:T(8,128)}, f32[128,768]{1,0:T(8,128)}) custom-call(s32[1]{0:T(128)} %bitcast.refs_0_.me_ref, f32[512,768]{1,0:T(8,128)} %refs_1_.11, f32[2048,768]{1,0:T(8,128)} %refs_2_.9, f32[16,2,768]{2,1,0:T(2,128)} %pad_maximum_fusion.2.refs_3_, f32[2048,128]{1,0:T(8,128)} %get-tuple-element.30.refs_4_, ...), custom_call_target="tpu_custom_call" | custom-call | flops 1000000000 | bytes 1000000 | tf_op jit(solution)/shard_map/outputs/pallas_call | solution.py:662
  125.0 3.3 %collective-permute-done.14 = f32[1,160,256]{2,1,0:T(8,128)S(1)} collective-permute-done((f32[1,160,256]{2,1,0:T(8,128)S(1)}, f32[1,160,256]{2,1,0:T(8,128)S(1)}, u32[]{:S(2)}, u32[]{:S(2)}) %collective-permute-start.14) | collective-permute-done | bytes 163872 | tf_op jit(solution)/shard_map/ppermute | solution.py:497
  128.3 0.7 fusion.5.refs_6_
  129.0 2.5 %outputs.3 = (f32[512,768]{1,0:T(8,128)}, f32[128,768]{1,0:T(8,128)}) custom-call(s32[1]{0:T(128)} %bitcast.refs_0_.me_ref, f32[512,768]{1,0:T(8,128)} %refs_1_.11, f32[2048,768]{1,0:T(8,128)} %refs_2_.9, f32[16,2,768]{2,1,0:T(2,128)} %pad_maximum_fusion.2.refs_3_, ...), custom_call_target="tpu_custom_call", output_to_operand_aliasing={{0}: (7, {}), {1}: (8, {})} | custom-call | flops 1000000000 | bytes 1000000 | tf_op jit(solution)/shard_map/outputs/pallas_call | solution.py:662
  (64 shorter events, 4.5 us)
Async XLA Ops:
  2.0 12.2 %copy-start.6 = (s32[8,896]{1,0:T(8,128)S(1)}, s32[8,896]{1,0:T(8,128)}, u32[]{:S(2)}) copy-start(s32[8,896]{1,0:T(8,128)} %pack.1) | copy-start | bytes 86020
  2.0 12.2 %collective-permute-start.2 = (s32[8,896]{1,0:T(8,128)}, s32[8,896]{1,0:T(8,128)S(1)}, u32[]{:S(2)}, u32[]{:S(2)}) collective-permute-start(s32[8,896]{1,0:T(8,128)} %pack.1), channel_id=1, source_target_pairs={{0,12},{1,13},{2,14},{3,15},{4,8},{5,9},{6,10},{7,11},{8,4},{9,5},... | collective-permute-start | bytes 86024 | tf_op jit(solution)/shard_map/ppermute | solution.py:497
  7.0 7.2 %collective-permute-start.1 = (s32[8,896]{1,0:T(8,128)}, s32[8,896]{1,0:T(8,128)S(1)}, u32[]{:S(2)}, u32[]{:S(2)}) collective-permute-start(s32[8,896]{1,0:T(8,128)} %pack.1), channel_id=1, source_target_pairs={{0,8},{1,9},{2,10},{3,11},{4,12},{5,13},{6,14},{7,15},{8,0},{9,1},... | collective-permute-start | bytes 86024 | tf_op jit(solution)/shard_map/ppermute | solution.py:497
  7.0 7.2 %collective-permute-start = (s32[8,896]{1,0:T(8,128)}, s32[8,896]{1,0:T(8,128)S(1)}, u32[]{:S(2)}, u32[]{:S(2)}) collective-permute-start(s32[8,896]{1,0:T(8,128)} %pack.1), channel_id=1, source_target_pairs={{0,4},{1,5},{2,6},{3,7},{4,0},{5,1},{6,2},{7,3},{8,12},{9,13},{10,... | collective-permute-start | bytes 86024 | tf_op jit(solution)/shard_map/ppermute | solution.py:497
  14.2 1.8 %copy-start.5 = (s32[4,8,896]{2,1,0:T(8,128)}, s32[4,8,896]{2,1,0:T(8,128)S(1)}, u32[]{:S(2)}) copy-start(s32[4,8,896]{2,1,0:T(8,128)S(1)} %pad_add_fusion.refs_2_) | copy-start | bytes 344068
  14.2 7.7 %copy-start.7 = (f32[16,1,2,768]{3,2,1,0:T(2,128)S(1)}, f32[16,1,2,768]{3,2,1,0:T(2,128)}, u32[]{:S(2)}) copy-start(f32[16,1,2,768]{3,2,1,0:T(2,128)} %get-tuple-element.22) | copy-start | bytes 294916
  14.3 9.7 %collective-permute-start.4 = (s32[4,8,896]{2,1,0:T(8,128)S(1)}, s32[4,8,896]{2,1,0:T(8,128)S(1)}, u32[]{:S(2)}, u32[]{:S(2)}) collective-permute-start(s32[4,8,896]{2,1,0:T(8,128)S(1)} %pad_add_fusion.refs_2_), channel_id=1, source_target_pairs={{0,2},{1,3},{2,0},{3,1},{4,6},{5,7},{6,4},{7,5},{8,10},{9,11},{10,... | collective-permute-start | bytes 344072 | tf_op jit(solution)/shard_map/ppermute | solution.py:497
  22.0 1.3 collective-permute-start.3
  24.0 0.7 copy-start.8
  24.0 6.6 %collective-permute-start.5 = (s32[8,8,896]{2,1,0:T(8,128)S(1)}, s32[8,8,896]{2,1,0:T(8,128)S(1)}, u32[]{:S(2)}, u32[]{:S(2)}) collective-permute-start(s32[8,8,896]{2,1,0:T(8,128)S(1)} %get-tuple-element.52.refs_2_), channel_id=1, source_target_pairs={{0,1},{1,0},{2,3},{3,2},{4,5},{5,4},{6,7},{7,6},{8,9},{9,8},{10,11... | collective-permute-start | bytes 688136 | tf_op jit(solution)/shard_map/ppermute | solution.py:497
  30.6 0.8 copy-start.9
  31.4 35.4 %copy-start.4 = (f32[8,2,2,768]{3,2,1,0:T(2,128)S(1)}, f32[8,2,2,768]{3,2,1,0:T(2,128)}, u32[]{:S(2)}) copy-start(f32[8,2,2,768]{3,2,1,0:T(2,128)} %pad_maximum_fusion.refs_9_) | copy-start | bytes 294916
  66.1 5.0 %collective-permute-start.7 = (f32[8,160,256]{2,1,0:T(8,128)}, f32[8,160,256]{2,1,0:T(8,128)S(1)}, u32[]{:S(2)}, u32[]{:S(2)}) collective-permute-start(f32[8,160,256]{2,1,0:T(8,128)} %get-tuple-element.28), channel_id=1, source_target_pairs={{0,1},{1,0},{2,3},{3,2},{4,5},{5,4},{6,7},{7,6},{8,9},{9,8},{10,11... | collective-permute-start | bytes 3932168 | tf_op jit(solution)/shard_map/ppermute | solution.py:497
  66.4 10.6 %collective-permute-start.15 = (f32[8,160,256]{2,1,0:T(8,128)}, f32[8,160,256]{2,1,0:T(8,128)S(1)}, u32[]{:S(2)}, u32[]{:S(2)}) collective-permute-start(f32[8,160,256]{2,1,0:T(8,128)} %get-tuple-element.35), channel_id=1, source_target_pairs={{0,1},{1,0},{2,3},{3,2},{4,5},{5,4},{6,7},{7,6},{8,9},{9,8},{10,11... | collective-permute-start | bytes 3932168 | tf_op jit(solution)/shard_map/ppermute | solution.py:497
  66.7 10.6 %collective-permute-start.11 = (f32[8,160,256]{2,1,0:T(8,128)}, f32[8,160,256]{2,1,0:T(8,128)S(1)}, u32[]{:S(2)}, u32[]{:S(2)}) collective-permute-start(f32[8,160,256]{2,1,0:T(8,128)} %get-tuple-element.25), channel_id=1, source_target_pairs={{0,1},{1,0},{2,3},{3,2},{4,5},{5,4},{6,7},{7,6},{8,9},{9,8},{10,11... | collective-permute-start | bytes 3932168 | tf_op jit(solution)/shard_map/ppermute | solution.py:497
  66.9 4.2 %collective-permute-start.6 = (f32[4,2,2,768]{3,2,1,0:T(2,128)S(1)}, f32[4,2,2,768]{3,2,1,0:T(2,128)S(1)}, u32[]{:S(2)}, u32[]{:S(2)}) collective-permute-start(f32[4,2,2,768]{3,2,1,0:T(2,128)S(1)} %get-tuple-element.59), channel_id=1, source_target_pairs={{0,2},{1,3},{2,0},{3,1},{4,6},{5,7},{6,4},{7,5},{8,10},{9,11},{10,... | collective-permute-start | bytes 147464 | tf_op jit(solution)/shard_map/ppermute | solution.py:497
  71.1 5.9 %copy-start.2 = (f32[4,160,256]{2,1,0:T(8,128)S(1)}, f32[4,160,256]{2,1,0:T(8,128)}, u32[]{:S(2)}) copy-start(f32[4,160,256]{2,1,0:T(8,128)} %get-tuple-element.36) | copy-start | bytes 1966084
  71.1 5.9 %copy-start.3 = (f32[4,160,256]{2,1,0:T(8,128)S(1)}, f32[4,160,256]{2,1,0:T(8,128)}, u32[]{:S(2)}) copy-start(f32[4,160,256]{2,1,0:T(8,128)} %get-tuple-element.34) | copy-start | bytes 1966084
  72.7 21.9 %collective-permute-start.19 = (f32[4,160,256]{2,1,0:T(8,128)S(1)}, f32[4,160,256]{2,1,0:T(8,128)S(1)}, u32[]{:S(2)}, u32[]{:S(2)}) collective-permute-start(f32[4,160,256]{2,1,0:T(8,128)S(1)} %get-tuple-element.43), channel_id=1, source_target_pairs={{0,2},{1,3},{2,0},{3,1},{4,6},{5,7},{6,4},{7,5},{8,10},{9,11},{10,... | collective-permute-start | bytes 1966088 | tf_op jit(solution)/shard_map/ppermute | solution.py:497
  73.3 6.7 %collective-permute-start.10 = (f32[4,2,768]{2,1,0:T(2,128)S(1)}, f32[4,2,768]{2,1,0:T(2,128)S(1)}, u32[]{:S(2)}, u32[]{:S(2)}) collective-permute-start(f32[4,2,768]{2,1,0:T(2,128)S(1)} %get-tuple-element.55), channel_id=1, source_target_pairs={{0,12},{1,13},{2,14},{3,15},{4,8},{5,9},{6,10},{7,11},{8,4},{9,5},... | collective-permute-start | bytes 73736 | tf_op jit(solution)/shard_map/ppermute | solution.py:497
  77.0 1.1 copy-start
  77.0 1.3 copy-start.1
  77.2 17.8 %collective-permute-start.16 = (f32[4,160,256]{2,1,0:T(8,128)S(1)}, f32[4,160,256]{2,1,0:T(8,128)S(1)}, u32[]{:S(2)}, u32[]{:S(2)}) collective-permute-start(f32[4,160,256]{2,1,0:T(8,128)S(1)} %get-tuple-element.47), channel_id=1, source_target_pairs={{0,4},{1,5},{2,6},{3,7},{4,0},{5,1},{6,2},{7,3},{8,12},{9,13},{10,... | collective-permute-start | bytes 1966088 | tf_op jit(solution)/shard_map/ppermute | solution.py:497
  78.5 24.2 %collective-permute-start.12 = (f32[4,160,256]{2,1,0:T(8,128)S(1)}, f32[4,160,256]{2,1,0:T(8,128)S(1)}, u32[]{:S(2)}, u32[]{:S(2)}) collective-permute-start(f32[4,160,256]{2,1,0:T(8,128)S(1)} %get-tuple-element.51), channel_id=1, source_target_pairs={{0,2},{1,3},{2,0},{3,1},{4,6},{5,7},{6,4},{7,5},{8,10},{9,11},{10,... | collective-permute-start | bytes 1966088 | tf_op jit(solution)/shard_map/ppermute | solution.py:497
  80.0 11.4 %collective-permute-start.9 = (f32[4,2,768]{2,1,0:T(2,128)S(1)}, f32[4,2,768]{2,1,0:T(2,128)S(1)}, u32[]{:S(2)}, u32[]{:S(2)}) collective-permute-start(f32[4,2,768]{2,1,0:T(2,128)S(1)} %get-tuple-element.56), channel_id=1, source_target_pairs={{0,8},{1,9},{2,10},{3,11},{4,12},{5,13},{6,14},{7,15},{8,0},{9,1},... | collective-permute-start | bytes 73736 | tf_op jit(solution)/shard_map/ppermute | solution.py:497
  80.0 13.8 %collective-permute-start.8 = (f32[4,2,768]{2,1,0:T(2,128)S(1)}, f32[4,2,768]{2,1,0:T(2,128)S(1)}, u32[]{:S(2)}, u32[]{:S(2)}) collective-permute-start(f32[4,2,768]{2,1,0:T(2,128)S(1)} %get-tuple-element.57), channel_id=1, source_target_pairs={{0,4},{1,5},{2,6},{3,7},{4,0},{5,1},{6,2},{7,3},{8,12},{9,13},{10,... | collective-permute-start | bytes 73736 | tf_op jit(solution)/shard_map/ppermute | solution.py:497
  94.6 15.9 %collective-permute-start.20 = (f32[2,160,256]{2,1,0:T(8,128)S(1)}, f32[2,160,256]{2,1,0:T(8,128)S(1)}, u32[]{:S(2)}, u32[]{:S(2)}) collective-permute-start(f32[2,160,256]{2,1,0:T(8,128)S(1)} %get-tuple-element.41), channel_id=1, source_target_pairs={{0,4},{1,5},{2,6},{3,7},{4,0},{5,1},{6,2},{7,3},{8,12},{9,13},{10,... | collective-permute-start | bytes 983048 | tf_op jit(solution)/shard_map/ppermute | solution.py:497
  95.1 15.7 %collective-permute-start.17 = (f32[2,160,256]{2,1,0:T(8,128)S(1)}, f32[2,160,256]{2,1,0:T(8,128)S(1)}, u32[]{:S(2)}, u32[]{:S(2)}) collective-permute-start(f32[2,160,256]{2,1,0:T(8,128)S(1)} %get-tuple-element.45), channel_id=1, source_target_pairs={{0,8},{1,9},{2,10},{3,11},{4,12},{5,13},{6,14},{7,15},{8,0},{9,1},... | collective-permute-start | bytes 983048 | tf_op jit(solution)/shard_map/ppermute | solution.py:497
  102.7 17.1 %collective-permute-start.13 = (f32[2,160,256]{2,1,0:T(8,128)S(1)}, f32[2,160,256]{2,1,0:T(8,128)S(1)}, u32[]{:S(2)}, u32[]{:S(2)}) collective-permute-start(f32[2,160,256]{2,1,0:T(8,128)S(1)} %get-tuple-element.49), channel_id=1, source_target_pairs={{0,4},{1,5},{2,6},{3,7},{4,0},{5,1},{6,2},{7,3},{8,12},{9,13},{10,... | collective-permute-start | bytes 983048 | tf_op jit(solution)/shard_map/ppermute | solution.py:497
  110.6 9.4 %collective-permute-start.21 = (f32[1,160,256]{2,1,0:T(8,128)S(1)}, f32[1,160,256]{2,1,0:T(8,128)S(1)}, u32[]{:S(2)}, u32[]{:S(2)}) collective-permute-start(f32[1,160,256]{2,1,0:T(8,128)S(1)} %slice_add_fusion.12), channel_id=1, source_target_pairs={{0,8},{1,9},{2,10},{3,11},{4,12},{5,13},{6,14},{7,15},{8,0},{9,1},... | collective-permute-start | bytes 491528 | tf_op jit(solution)/shard_map/ppermute | solution.py:497
  110.9 9.8 %collective-permute-start.18 = (f32[1,160,256]{2,1,0:T(8,128)S(1)}, f32[1,160,256]{2,1,0:T(8,128)S(1)}, u32[]{:S(2)}, u32[]{:S(2)}) collective-permute-start(f32[1,160,256]{2,1,0:T(8,128)S(1)} %slice_add_fusion.14), channel_id=1, source_target_pairs={{0,2},{1,3},{2,0},{3,1},{4,6},{5,7},{6,4},{7,5},{8,10},{9,11},{10,... | collective-permute-start | bytes 491528 | tf_op jit(solution)/shard_map/ppermute | solution.py:497
  119.9 8.4 %collective-permute-start.14 = (f32[1,160,256]{2,1,0:T(8,128)S(1)}, f32[1,160,256]{2,1,0:T(8,128)S(1)}, u32[]{:S(2)}, u32[]{:S(2)}) collective-permute-start(f32[1,160,256]{2,1,0:T(8,128)S(1)} %slice_add_fusion.16), channel_id=1, source_target_pairs={{0,8},{1,9},{2,10},{3,11},{4,12},{5,13},{6,14},{7,15},{8,0},{9,1},... | collective-permute-start | bytes 491528 | tf_op jit(solution)/shard_map/ppermute | solution.py:497

commit v5 on v4

--- a/solution.py
+++ b/solution.py
@@ -594,8 +594,7 @@
             6e9,
             "own_codes",
         )(me, vectors, fine_codes, gathered)
-        if step == 2:
-            first_to = swap(after(first_to, gathered), 0)
+        first_to = swap(after(first_to, gathered), 2 - step)
         gathered = jnp.concatenate([gathered, exchange(gathered, step)])
 
     top = groups.bit_length() - 1
@@ -641,12 +640,11 @@
         "sums",
     )(me, gathered, vectors, fine_codes, *sums, first, second, fine_in, first_to)
 
-    first_to = swap(after(first_to, terms[0]), 1)
     finished = []
     for at, steps in enumerate(bits):
         away, other, kept = terms[3 * at : 3 * at + 3]
         other, kept = halved(exchange(away, 1), other, kept)
-        if at == len(bits) - 1:
+        if at == 0:
             first_to = after(first_to, other)[::-1]
             first_to = jnp.concatenate(
                 [first_to[0]] + [exchange(first_to[z], 4 * z) for z in range(1, far)]
@@ -655,6 +653,8 @@
             got = exchange(other, 1 << bit)
             half = got.shape[0] // 2
             other, kept = halved(got, kept[:half], kept[half:])
+            if at == 0 and bit == steps[0]:
+                other, first_to = lax.optimization_barrier((other, first_to))
         finished.append((kept + exchange(other, 1 << steps[-1]))[0])
     outs = ()
     for chunks, width in ((range(1, len(cuts)), feature), ((0,), cuts[0])):

time: 132 us -> 137 us (1.038)
  waiting for transfers between devices: 41 us -> 47.8 us
  starting transfers between devices: 20.9 us -> 19.4 us
    ppermute x22, waiting for transfers between devices: 41 us -> 47.8 us  [exchange(): lax.ppermute(values, 'cell', [(at, at ^ step) for at in range(groups)])]
    ppermute x22, starting transfers between devices: 20.9 us -> 19.4 us  [exchange(): lax.ppermute(values, 'cell', [(at, at ^ step) for at in range(groups)])]
  transfers between devices with their start and end apart: 22 -> 22, of which waited for: 8 -> 9; matrix products, arithmetic and copies ran while one was open for 4% -> 4% of each run, Pallas kernels for 17% -> 16%
where the time goes in v5:
time: 137 us; the launch traced here: 136 us
  Pallas kernels  60.6 us (44%)
  waiting for transfers between devices  47.8 us (35%)
  starting transfers between devices  19.4 us (14%)
  other arithmetic  5.74 us (4%)
  local copies, waits for them, and re-layouts  1.91 us (1%)
    ppermute x22, waiting for transfers between devices, exchange(): lax.ppermute(values, 'cell', [(at, at ^ step) for at in range(groups)])  47.8 us
    pallas_call x1, Pallas kernels, dense_plan(): local(lambda *refs: sums_kernel(groups, slot_count, owner_cells, cuts, st...  34.7 us
    ppermute x22, starting transfers between devices, exchange(): lax.ppermute(values, 'cell', [(at, at ^ step) for at in range(groups)])  19.4 us
    pallas_call x2, Pallas kernels, dense_plan(): local(lambda me_ref, *refs, base=base: own_codes_kernel(base, *refs), [((...  11.8 us
    pallas_call x1, Pallas kernels, dense_plan(): local(lambda *refs: own_cells_kernel(groups, listed, *refs), [((listed, f...  6.58 us
    pallas_call x2, Pallas kernels, dense_plan(): local(lambda *refs, chunks=chunks, width=width, place=place: final_kernel...  6.16 us
  transfers between devices with their start and end apart: 22, of which 9 were waited for; matrix products, arithmetic and copies ran while one was open for 4% of the time, Pallas kernels for 16%

profile of v5, /device:TPU:0, one launch (start us, length us, event | category | flops | bytes accessed | tf_op | source)
XLA Modules:
  0.0 136.3 jit_solution(4591979746024763532)
XLA Ops:
  0.6 1.3 pack.1
  2.0 5.0 %collective-permute-start.2 = (s32[8,896]{1,0:T(8,128)}, s32[8,896]{1,0:T(8,128)S(1)}, u32[]{:S(2)}, u32[]{:S(2)}) collective-permute-start(s32[8,896]{1,0:T(8,128)} %pack.1), channel_id=1, source_target_pairs={{0,12},{1,13},{2,14},{3,15},{4,8},{5,9},{6,10},{7,11},{8,4},{9,5},... | collective-permute-start | bytes 86024 | tf_op jit(solution)/shard_map/ppermute | solution.py:497
  7.6 6.6 %own_cells.1 = (f32[32,768]{1,0:T(8,128)}, f32[32,768]{1,0:T(8,128)}, f32[16,1,2,768]{3,2,1,0:T(2,128)}) custom-call(s32[1]{0:T(128)} %bitcast.me_ref.refs_0_, bf16[1536,768]{1,0:T(8,128)(2,1)} %refs_2_.7, s32[2,1536]{1,0:T(2,128)} %refs_3_.3, s32[2,1536]{1,0:T(2,128)} %refs_3_.2, f32[2048,768]{1,0:T(8,128)} %refs_2_.9), custom_call_target="tpu_custom_call" | custom-call | flops 5000000000 | bytes 1000000 | tf_op jit(solution)/shard_map/own_cells/pallas_call | solution.py:575
  14.3 1.8 %collective-permute-start.3 = (s32[4,8,896]{2,1,0:T(8,128)S(1)}, s32[4,8,896]{2,1,0:T(8,128)S(1)}, u32[]{:S(2)}, u32[]{:S(2)}) collective-permute-start(s32[4,8,896]{2,1,0:T(8,128)S(1)} %pad_add_fusion.refs_2_), channel_id=1, source_target_pairs={{0,2},{1,3},{2,0},{3,1},{4,6},{5,7},{6,4},{7,5},{8,10},{9,11},{10,... | collective-permute-start | bytes 344072 | tf_op jit(solution)/shard_map/ppermute | solution.py:497
  16.1 5.9 %own_codes.2.refs_4_ = f32[1024,768]{1,0:T(8,128)} custom-call(s32[1]{0:T(128)} %bitcast.me_ref.refs_0_, bf16[1536,768]{1,0:T(8,128)(2,1)} %refs_2_.7, s32[2,1536]{1,0:T(2,128)} %refs_3_.3, s32[4,8,896]{2,1,0:T(8,128)} %copy-done.5), custom_call_target="tpu_custom_call" | custom-call | flops 6000000000 | bytes 1000000 | tf_op jit(solution)/shard_map/own_codes/pallas_call | solution.py:588
  22.1 1.2 collective-permute-done.5
  24.2 5.9 %own_codes.3.refs_5_ = f32[1024,768]{1,0:T(8,128)} custom-call(s32[1]{0:T(128)} %bitcast.me_ref.refs_0_, bf16[1536,768]{1,0:T(8,128)(2,1)} %refs_2_.7, s32[2,1536]{1,0:T(2,128)} %refs_3_.3, s32[8,8,896]{2,1,0:T(8,128)} %copy-done.8), custom_call_target="tpu_custom_call" | custom-call | flops 6000000000 | bytes 1000000 | tf_op jit(solution)/shard_map/own_codes/pallas_call | solution.py:588
  30.2 0.7 pad_maximum_fusion.1.refs_9_
  30.9 0.8 copy-done.9
  31.7 34.7 %sums.1 = (f32[8,160,256]{2,1,0:T(8,128)}, f32[4,160,256]{2,1,0:T(8,128)}, f32[4,160,256]{2,1,0:T(8,128)}, f32[8,160,256]{2,1,0:T(8,128)}, f32[4,160,256]{2,1,0:...) custom-call(s32[1]{0:T(128)} %bitcast.me_ref.refs_0_, ...), custom_call_target="tpu_custom_call" | custom-call | flops 40000000000 | bytes 1000000 | tf_op jit(solution)/shard_map/sums/pallas_call | solution.py:612
  67.0 2.7 %collective-permute-done.7 = f32[8,160,256]{2,1,0:T(8,128)S(1)} collective-permute-done((f32[8,160,256]{2,1,0:T(8,128)}, f32[8,160,256]{2,1,0:T(8,128)S(1)}, u32[]{:S(2)}, u32[]{:S(2)}) %collective-permute-start.7) | collective-permute-done | bytes 1310752 | tf_op jit(solution)/shard_map/ppermute | solution.py:497
  69.7 1.6 %slice_add_fusion.5 = (f32[4,160,256]{2,1,0:T(8,128)S(1)}, f32[4,160,256]{2,1,0:T(8,128)S(1)}) fusion(f32[4,160,256]{2,1,0:T(8,128)} %get-tuple-element.28, f32[8,160,256]{2,1,0:T(8,128)S(1)} %collective-permute-done.7, f32[4,160,256]{2,1,0:T(8,128)} %get-tuple-element.30), kind=kLoop, calls=%fused_computation.5 | loop fusion | flops 327680 | bytes 3932160 | tf_op jit(solution)/shard_map/add | solution.py:519
  71.3 1.5 %collective-permute-start.8 = (f32[4,160,256]{2,1,0:T(8,128)S(1)}, f32[4,160,256]{2,1,0:T(8,128)S(1)}, u32[]{:S(2)}, u32[]{:S(2)}) collective-permute-start(f32[4,160,256]{2,1,0:T(8,128)S(1)} %get-tuple-element.55), channel_id=1, source_target_pairs={{0,2},{1,3},{2,0},{3,1},{4,6},{5,7},{6,4},{7,5},{8,10},{9,11},{10,... | collective-permute-start | bytes 1966088 | tf_op jit(solution)/shard_map/ppermute | solution.py:497
  72.8 3.7 %collective-permute-start.11 = (f32[4,2,768]{2,1,0:T(2,128)S(1)}, f32[4,2,768]{2,1,0:T(2,128)S(1)}, u32[]{:S(2)}, u32[]{:S(2)}) collective-permute-start(f32[4,2,768]{2,1,0:T(2,128)S(1)} %get-tuple-element.59), channel_id=1, source_target_pairs={{0,12},{1,13},{2,14},{3,15},{4,8},{5,9},{6,10},{7,11},{8,4},{9,5},... | collective-permute-start | bytes 73736 | tf_op jit(solution)/shard_map/ppermute | solution.py:497
  76.8 0.8 copy-done
  78.0 0.6 collective-permute-start.19
  78.7 0.9 collective-permute-start.9
  79.6 12.2 %collective-permute-done.10 = f32[4,2,768]{2,1,0:T(2,128)S(1)} collective-permute-done((f32[4,2,768]{2,1,0:T(2,128)S(1)}, f32[4,2,768]{2,1,0:T(2,128)S(1)}, u32[]{:S(2)}, u32[]{:S(2)}) %collective-permute-start.10) | collective-permute-done | bytes 24608 | tf_op jit(solution)/shard_map/ppermute | solution.py:497
  91.8 2.2 %collective-permute-done.9 = f32[4,2,768]{2,1,0:T(2,128)S(1)} collective-permute-done((f32[4,2,768]{2,1,0:T(2,128)S(1)}, f32[4,2,768]{2,1,0:T(2,128)S(1)}, u32[]{:S(2)}, u32[]{:S(2)}) %collective-permute-start.9) | collective-permute-done | bytes 24608 | tf_op jit(solution)/shard_map/ppermute | solution.py:497
  94.0 0.7 pad_maximum_fusion.2.refs_3_
  95.5 0.9 collective-permute-start.16
  96.4 5.7 %collective-permute-done.19 = f32[4,160,256]{2,1,0:T(8,128)S(1)} collective-permute-done((f32[4,160,256]{2,1,0:T(8,128)S(1)}, f32[4,160,256]{2,1,0:T(8,128)S(1)}, u32[]{:S(2)}, u32[]{:S(2)}) %collective-permute-start.19) | collective-permute-done | bytes 655392 | tf_op jit(solution)/shard_map/ppermute | solution.py:497
  102.2 1.3 collective-permute-start.20
  103.5 9.7 %collective-permute-done.12 = f32[2,160,256]{2,1,0:T(8,128)S(1)} collective-permute-done((f32[2,160,256]{2,1,0:T(8,128)S(1)}, f32[2,160,256]{2,1,0:T(8,128)S(1)}, u32[]{:S(2)}, u32[]{:S(2)}) %collective-permute-start.12) | collective-permute-done | bytes 327712 | tf_op jit(solution)/shard_map/ppermute | solution.py:497
  113.4 0.6 collective-permute-start.17
  114.0 6.2 %collective-permute-done.20 = f32[2,160,256]{2,1,0:T(8,128)S(1)} collective-permute-done((f32[2,160,256]{2,1,0:T(8,128)S(1)}, f32[2,160,256]{2,1,0:T(8,128)S(1)}, u32[]{:S(2)}, u32[]{:S(2)}) %collective-permute-start.20) | collective-permute-done | bytes 327712 | tf_op jit(solution)/shard_map/ppermute | solution.py:497
  120.4 0.7 fusion.3.refs_6_
  121.1 7.7 %collective-permute-done.21 = f32[1,160,256]{2,1,0:T(8,128)S(1)} collective-permute-done((f32[1,160,256]{2,1,0:T(8,128)S(1)}, f32[1,160,256]{2,1,0:T(8,128)S(1)}, u32[]{:S(2)}, u32[]{:S(2)}) %collective-permute-start.21) | collective-permute-done | bytes 163872 | tf_op jit(solution)/shard_map/ppermute | solution.py:497
  128.8 0.7 fusion.1.refs_7_
  129.5 3.6 %outputs.2 = (f32[512,768]{1,0:T(8,128)}, f32[128,768]{1,0:T(8,128)}) custom-call(s32[1]{0:T(128)} %bitcast.me_ref.refs_0_, f32[512,768]{1,0:T(8,128)} %refs_1_.11, f32[2048,768]{1,0:T(8,128)} %refs_2_.9, f32[16,2,768]{2,1,0:T(2,128)} %pad_maximum_fusion.2.refs_3_, f32[2048,128]{1,0:T(8,128)} %get-tuple-element.33.refs_4_, ...), custom_call_target="tpu_custom_call" | custom-call | flops 1000000000 | bytes 1000000 | tf_op jit(solution)/shard_map/outputs/pallas_call | solution.py:662
  133.1 0.7 fusion.5.refs_6_
  133.8 2.5 %outputs.3 = (f32[512,768]{1,0:T(8,128)}, f32[128,768]{1,0:T(8,128)}) custom-call(s32[1]{0:T(128)} %bitcast.me_ref.refs_0_, f32[512,768]{1,0:T(8,128)} %refs_1_.11, f32[2048,768]{1,0:T(8,128)} %refs_2_.9, f32[16,2,768]{2,1,0:T(2,128)} %pad_maximum_fusion.2.refs_3_, ...), custom_call_target="tpu_custom_call", output_to_operand_aliasing={{0}: (7, {}), {1}: (8, {})} | custom-call | flops 1000000000 | bytes 1000000 | tf_op jit(solution)/shard_map/outputs/pallas_call | solution.py:662
  (64 shorter events, 4.2 us)
Async XLA Ops:
  2.0 12.2 %copy-start.6 = (s32[8,896]{1,0:T(8,128)S(1)}, s32[8,896]{1,0:T(8,128)}, u32[]{:S(2)}) copy-start(s32[8,896]{1,0:T(8,128)} %pack.1) | copy-start | bytes 86020
  2.0 12.2 %collective-permute-start.2 = (s32[8,896]{1,0:T(8,128)}, s32[8,896]{1,0:T(8,128)S(1)}, u32[]{:S(2)}, u32[]{:S(2)}) collective-permute-start(s32[8,896]{1,0:T(8,128)} %pack.1), channel_id=1, source_target_pairs={{0,12},{1,13},{2,14},{3,15},{4,8},{5,9},{6,10},{7,11},{8,4},{9,5},... | collective-permute-start | bytes 86024 | tf_op jit(solution)/shard_map/ppermute | solution.py:497
  7.0 7.2 %collective-permute-start.1 = (s32[8,896]{1,0:T(8,128)}, s32[8,896]{1,0:T(8,128)S(1)}, u32[]{:S(2)}, u32[]{:S(2)}) collective-permute-start(s32[8,896]{1,0:T(8,128)} %pack.1), channel_id=1, source_target_pairs={{0,8},{1,9},{2,10},{3,11},{4,12},{5,13},{6,14},{7,15},{8,0},{9,1},... | collective-permute-start | bytes 86024 | tf_op jit(solution)/shard_map/ppermute | solution.py:497
  7.0 7.2 %collective-permute-start = (s32[8,896]{1,0:T(8,128)}, s32[8,896]{1,0:T(8,128)S(1)}, u32[]{:S(2)}, u32[]{:S(2)}) collective-permute-start(s32[8,896]{1,0:T(8,128)} %pack.1), channel_id=1, source_target_pairs={{0,4},{1,5},{2,6},{3,7},{4,0},{5,1},{6,2},{7,3},{8,12},{9,13},{10,... | collective-permute-start | bytes 86024 | tf_op jit(solution)/shard_map/ppermute | solution.py:497
  14.2 1.8 %copy-start.5 = (s32[4,8,896]{2,1,0:T(8,128)}, s32[4,8,896]{2,1,0:T(8,128)S(1)}, u32[]{:S(2)}) copy-start(s32[4,8,896]{2,1,0:T(8,128)S(1)} %pad_add_fusion.refs_2_) | copy-start | bytes 344068
  14.2 7.7 %copy-start.7 = (f32[16,1,2,768]{3,2,1,0:T(2,128)S(1)}, f32[16,1,2,768]{3,2,1,0:T(2,128)}, u32[]{:S(2)}) copy-start(f32[16,1,2,768]{3,2,1,0:T(2,128)} %get-tuple-element.26) | copy-start | bytes 294916
  14.3 9.1 %collective-permute-start.3 = (s32[4,8,896]{2,1,0:T(8,128)S(1)}, s32[4,8,896]{2,1,0:T(8,128)S(1)}, u32[]{:S(2)}, u32[]{:S(2)}) collective-permute-start(s32[4,8,896]{2,1,0:T(8,128)S(1)} %pad_add_fusion.refs_2_), channel_id=1, source_target_pairs={{0,2},{1,3},{2,0},{3,1},{4,6},{5,7},{6,4},{7,5},{8,10},{9,11},{10,... | collective-permute-start | bytes 344072 | tf_op jit(solution)/shard_map/ppermute | solution.py:497
  22.0 1.3 collective-permute-start.5
  23.4 0.9 copy-start.8
  23.4 7.5 %collective-permute-start.4 = (s32[8,8,896]{2,1,0:T(8,128)S(1)}, s32[8,8,896]{2,1,0:T(8,128)S(1)}, u32[]{:S(2)}, u32[]{:S(2)}) collective-permute-start(s32[8,8,896]{2,1,0:T(8,128)S(1)} %get-tuple-element.56.refs_2_), channel_id=1, source_target_pairs={{0,1},{1,0},{2,3},{3,2},{4,5},{5,4},{6,7},{7,6},{8,9},{9,8},{10,11... | collective-permute-start | bytes 688136 | tf_op jit(solution)/shard_map/ppermute | solution.py:497
  23.6 6.6 %collective-permute-start.6 = (f32[4,2,2,768]{3,2,1,0:T(2,128)S(1)}, f32[4,2,2,768]{3,2,1,0:T(2,128)S(1)}, u32[]{:S(2)}, u32[]{:S(2)}) collective-permute-start(f32[4,2,2,768]{3,2,1,0:T(2,128)S(1)} %get-tuple-element.63), channel_id=1, source_target_pairs={{0,2},{1,3},{2,0},{3,1},{4,6},{5,7},{6,4},{7,5},{8,10},{9,11},{10,... | collective-permute-start | bytes 147464 | tf_op jit(solution)/shard_map/ppermute | solution.py:497
  30.9 0.8 copy-start.9
  66.4 3.3 %collective-permute-start.7 = (f32[8,160,256]{2,1,0:T(8,128)}, f32[8,160,256]{2,1,0:T(8,128)S(1)}, u32[]{:S(2)}, u32[]{:S(2)}) collective-permute-start(f32[8,160,256]{2,1,0:T(8,128)} %get-tuple-element.29), channel_id=1, source_target_pairs={{0,1},{1,0},{2,3},{3,2},{4,5},{5,4},{6,7},{7,6},{8,9},{9,8},{10,11... | collective-permute-start | bytes 3932168 | tf_op jit(solution)/shard_map/ppermute | solution.py:497
  66.5 10.0 %collective-permute-start.14 = (f32[8,160,256]{2,1,0:T(8,128)}, f32[8,160,256]{2,1,0:T(8,128)S(1)}, u32[]{:S(2)}, u32[]{:S(2)}) collective-permute-start(f32[8,160,256]{2,1,0:T(8,128)} %get-tuple-element.37), channel_id=1, source_target_pairs={{0,1},{1,0},{2,3},{3,2},{4,5},{5,4},{6,7},{7,6},{8,9},{9,8},{10,11... | collective-permute-start | bytes 3932168 | tf_op jit(solution)/shard_map/ppermute | solution.py:497
  66.9 9.8 %collective-permute-start.18 = (f32[8,160,256]{2,1,0:T(8,128)}, f32[8,160,256]{2,1,0:T(8,128)S(1)}, u32[]{:S(2)}, u32[]{:S(2)}) collective-permute-start(f32[8,160,256]{2,1,0:T(8,128)} %get-tuple-element.40), channel_id=1, source_target_pairs={{0,1},{1,0},{2,3},{3,2},{4,5},{5,4},{6,7},{7,6},{8,9},{9,8},{10,11... | collective-permute-start | bytes 3932168 | tf_op jit(solution)/shard_map/ppermute | solution.py:497
  69.7 3.1 %copy-start.4 = (f32[4,4,2,768]{3,2,1,0:T(2,128)S(1)}, f32[4,4,2,768]{3,2,1,0:T(2,128)}, u32[]{:S(2)}) copy-start(f32[4,4,2,768]{3,2,1,0:T(2,128)} %pad_maximum_fusion.1.refs_9_) | copy-start | bytes 294916
  69.7 6.8 %copy-start.2 = (f32[4,160,256]{2,1,0:T(8,128)S(1)}, f32[4,160,256]{2,1,0:T(8,128)}, u32[]{:S(2)}) copy-start(f32[4,160,256]{2,1,0:T(8,128)} %get-tuple-element.38) | copy-start | bytes 1966084
  69.7 6.8 %copy-start.3 = (f32[4,160,256]{2,1,0:T(8,128)S(1)}, f32[4,160,256]{2,1,0:T(8,128)}, u32[]{:S(2)}) copy-start(f32[4,160,256]{2,1,0:T(8,128)} %get-tuple-element.36) | copy-start | bytes 1966084
  71.3 23.5 %collective-permute-start.8 = (f32[4,160,256]{2,1,0:T(8,128)S(1)}, f32[4,160,256]{2,1,0:T(8,128)S(1)}, u32[]{:S(2)}, u32[]{:S(2)}) collective-permute-start(f32[4,160,256]{2,1,0:T(8,128)S(1)} %get-tuple-element.55), channel_id=1, source_target_pairs={{0,2},{1,3},{2,0},{3,1},{4,6},{5,7},{6,4},{7,5},{8,10},{9,11},{10,... | collective-permute-start | bytes 1966088 | tf_op jit(solution)/shard_map/ppermute | solution.py:497
  72.8 5.9 %collective-permute-start.11 = (f32[4,2,768]{2,1,0:T(2,128)S(1)}, f32[4,2,768]{2,1,0:T(2,128)S(1)}, u32[]{:S(2)}, u32[]{:S(2)}) collective-permute-start(f32[4,2,768]{2,1,0:T(2,128)S(1)} %get-tuple-element.59), channel_id=1, source_target_pairs={{0,12},{1,13},{2,14},{3,15},{4,8},{5,9},{6,10},{7,11},{8,4},{9,5},... | collective-permute-start | bytes 73736 | tf_op jit(solution)/shard_map/ppermute | solution.py:497
  76.5 1.1 copy-start
  76.5 1.3 copy-start.1
  76.7 18.7 %collective-permute-start.15 = (f32[4,160,256]{2,1,0:T(8,128)S(1)}, f32[4,160,256]{2,1,0:T(8,128)S(1)}, u32[]{:S(2)}, u32[]{:S(2)}) collective-permute-start(f32[4,160,256]{2,1,0:T(8,128)S(1)} %get-tuple-element.51), channel_id=1, source_target_pairs={{0,4},{1,5},{2,6},{3,7},{4,0},{5,1},{6,2},{7,3},{8,12},{9,13},{10,... | collective-permute-start | bytes 1966088 | tf_op jit(solution)/shard_map/ppermute | solution.py:497
  78.0 24.2 %collective-permute-start.19 = (f32[4,160,256]{2,1,0:T(8,128)S(1)}, f32[4,160,256]{2,1,0:T(8,128)S(1)}, u32[]{:S(2)}, u32[]{:S(2)}) collective-permute-start(f32[4,160,256]{2,1,0:T(8,128)S(1)} %get-tuple-element.47), channel_id=1, source_target_pairs={{0,2},{1,3},{2,0},{3,1},{4,6},{5,7},{6,4},{7,5},{8,10},{9,11},{10,... | collective-permute-start | bytes 1966088 | tf_op jit(solution)/shard_map/ppermute | solution.py:497
  78.6 13.2 %collective-permute-start.10 = (f32[4,2,768]{2,1,0:T(2,128)S(1)}, f32[4,2,768]{2,1,0:T(2,128)S(1)}, u32[]{:S(2)}, u32[]{:S(2)}) collective-permute-start(f32[4,2,768]{2,1,0:T(2,128)S(1)} %get-tuple-element.60), channel_id=1, source_target_pairs={{0,8},{1,9},{2,10},{3,11},{4,12},{5,13},{6,14},{7,15},{8,0},{9,1},... | collective-permute-start | bytes 73736 | tf_op jit(solution)/shard_map/ppermute | solution.py:497
  78.7 15.3 %collective-permute-start.9 = (f32[4,2,768]{2,1,0:T(2,128)S(1)}, f32[4,2,768]{2,1,0:T(2,128)S(1)}, u32[]{:S(2)}, u32[]{:S(2)}) collective-permute-start(f32[4,2,768]{2,1,0:T(2,128)S(1)} %get-tuple-element.61), channel_id=1, source_target_pairs={{0,4},{1,5},{2,6},{3,7},{4,0},{5,1},{6,2},{7,3},{8,12},{9,13},{10,... | collective-permute-start | bytes 73736 | tf_op jit(solution)/shard_map/ppermute | solution.py:497
  94.8 18.5 %collective-permute-start.12 = (f32[2,160,256]{2,1,0:T(8,128)S(1)}, f32[2,160,256]{2,1,0:T(8,128)S(1)}, u32[]{:S(2)}, u32[]{:S(2)}) collective-permute-start(f32[2,160,256]{2,1,0:T(8,128)S(1)} %get-tuple-element.35), channel_id=1, source_target_pairs={{0,4},{1,5},{2,6},{3,7},{4,0},{5,1},{6,2},{7,3},{8,12},{9,13},{10,... | collective-permute-start | bytes 983048 | tf_op jit(solution)/shard_map/ppermute | solution.py:497
  95.5 17.9 %collective-permute-start.16 = (f32[2,160,256]{2,1,0:T(8,128)S(1)}, f32[2,160,256]{2,1,0:T(8,128)S(1)}, u32[]{:S(2)}, u32[]{:S(2)}) collective-permute-start(f32[2,160,256]{2,1,0:T(8,128)S(1)} %get-tuple-element.49), channel_id=1, source_target_pairs={{0,8},{1,9},{2,10},{3,11},{4,12},{5,13},{6,14},{7,15},{8,0},{9,1},... | collective-permute-start | bytes 983048 | tf_op jit(solution)/shard_map/ppermute | solution.py:497
  102.2 18.0 %collective-permute-start.20 = (f32[2,160,256]{2,1,0:T(8,128)S(1)}, f32[2,160,256]{2,1,0:T(8,128)S(1)}, u32[]{:S(2)}, u32[]{:S(2)}) collective-permute-start(f32[2,160,256]{2,1,0:T(8,128)S(1)} %get-tuple-element.45), channel_id=1, source_target_pairs={{0,4},{1,5},{2,6},{3,7},{4,0},{5,1},{6,2},{7,3},{8,12},{9,13},{10,... | collective-permute-start | bytes 983048 | tf_op jit(solution)/shard_map/ppermute | solution.py:497
  113.3 19.8 %collective-permute-start.13 = (f32[1,160,256]{2,1,0:T(8,128)S(1)}, f32[1,160,256]{2,1,0:T(8,128)S(1)}, u32[]{:S(2)}, u32[]{:S(2)}) collective-permute-start(f32[1,160,256]{2,1,0:T(8,128)S(1)} %slice_add_fusion.16), channel_id=1, source_target_pairs={{0,8},{1,9},{2,10},{3,11},{4,12},{5,13},{6,14},{7,15},{8,0},{9,1},... | collective-permute-start | bytes 491528 | tf_op jit(solution)/shard_map/ppermute | solution.py:497
  113.4 7.0 %collective-permute-start.17 = (f32[1,160,256]{2,1,0:T(8,128)S(1)}, f32[1,160,256]{2,1,0:T(8,128)S(1)}, u32[]{:S(2)}, u32[]{:S(2)}) collective-permute-start(f32[1,160,256]{2,1,0:T(8,128)S(1)} %slice_add_fusion.14), channel_id=1, source_target_pairs={{0,2},{1,3},{2,0},{3,1},{4,6},{5,7},{6,4},{7,5},{8,10},{9,11},{10,... | collective-permute-start | bytes 491528 | tf_op jit(solution)/shard_map/ppermute | solution.py:497
  120.3 8.5 %collective-permute-start.21 = (f32[1,160,256]{2,1,0:T(8,128)S(1)}, f32[1,160,256]{2,1,0:T(8,128)S(1)}, u32[]{:S(2)}, u32[]{:S(2)}) collective-permute-start(f32[1,160,256]{2,1,0:T(8,128)S(1)} %slice_add_fusion.12), channel_id=1, source_target_pairs={{0,8},{1,9},{2,10},{3,11},{4,12},{5,13},{6,14},{7,15},{8,0},{9,1},... | collective-permute-start | bytes 491528 | tf_op jit(solution)/shard_map/ppermute | solution.py:497
